TPU v7x, 256 devices: a whole 4x4x8 slice. The times are simulated.
256 devices in a mesh: group: 8 (over y, core), member: 32 (over x, z).
Axes of the slice: x: 4, y: 4, z: 8, core: 2. Of those that a mesh axis runs over, the one named last changes fastest.
Arguments:
- histories: bfloat16 [131072, 1024], P(('group', 'member')), may hold values from -24 to 24
- lengths: int32 [512], P(('group', 'member')), may hold values from 0 to 384, as said below
- cotangent: bfloat16 [131072, 512], P(('group', 'member')), may hold values from -6 to 6
- w_in: bfloat16 [1024, 2048], replicated, may hold values from -0.1875 to 0.1875
Outputs:
- grad_histories: bfloat16 [131072, 1024], P(('group', 'member'))
- grad_w_in: float32 [1024, 2048], P('member')
Inputs may be any that keep to these rules, and one draw needn't show every extreme that they name: `lengths`: with each history rounded up to whole blocks of 128 rows, a device's 2 histories take at most 4 blocks; in every group some device takes all 4.
All inputs are finite; a program needn't handle non-finite values.
Results may differ from a plain program's by a relative error of at most 0.0071.
Values may be sent and summed in bfloat16 or wider, within the bound.
No kernel may reach another device: no remote copies, remote signals or barrier semaphores. Data moves between devices by JAX's collectives and lax.ppermute only.
A program may use at most 128 MiB of HBM per device.

v0:
```python
import jax
import jax.numpy as jnp
from jax import lax
from jax.sharding import PartitionSpec as P

HEADS = 4
BLOCK = 128


def layout(lens, rows, block):
    blocks = (lens + block - 1) // block
    start = jnp.concatenate([jnp.zeros((1,), jnp.int32), (jnp.cumsum(blocks) * block)[:-1]])
    row_index = jnp.arange(rows, dtype=jnp.int32)
    offset = row_index[:, None] - start[None, :]
    inside = (offset >= 0) & (offset < lens[None, :])
    live = jnp.any(inside, axis=1)
    slots = jnp.arange(lens.shape[0], dtype=jnp.int32)
    history = jnp.sum(jnp.where(inside, slots[None, :], 0), axis=1)
    position = jnp.sum(jnp.where(inside, offset, 0), axis=1)
    count = jnp.sum(jnp.where(inside, lens[None, :], 0), axis=1)
    used = jnp.sum(blocks)
    return (history, position, live, count, used)


def attend(uvqk, history, position, live, count, heads, block):
    rows = uvqk.shape[0]
    width = uvqk.shape[1] // 4
    size = width // heads
    nblocks = rows // block
    parts = uvqk.astype(jnp.float32)
    gate_u = parts[:, :width]
    values = parts[:, width : 2 * width].reshape(rows, heads, size)
    queries = parts[:, 2 * width : 3 * width].reshape(rows, heads, size)
    keys = parts[:, 3 * width :].reshape(rows, heads, size)
    inverse = 1.0 / jnp.maximum(count, 1).astype(jnp.float32)
    outputs = []
    for query_block in range(nblocks):
        low = query_block * block
        high = low + block
        scores = jnp.einsum(
            "qhd,khd->hqk", queries[low:high], keys[:high], precision=lax.Precision.HIGHEST
        ) * size ** (-0.5)
        valid = (history[low:high, None] == history[None, :high]) & (
            position[None, :high] <= position[low:high, None]
        )
        valid = valid & live[low:high, None] & live[None, :high]
        weights = jnp.where(valid[None], jax.nn.silu(scores), 0.0) * inverse[None, low:high, None]
        outputs.append(
            jnp.einsum(
                "hqk,khd->qhd", weights, values[:high], precision=lax.Precision.HIGHEST
            ).reshape(block, width)
        )
    attended = jnp.concatenate(outputs, axis=0)
    centred = attended - jnp.mean(attended, axis=1, keepdims=True)
    spread = jnp.mean(centred * centred, axis=1, keepdims=True)
    return centred * lax.rsqrt(spread + 1e-05) * gate_u


def pull_back(uvqk, cotangent, history, position, live, count, heads, block):

    def local(table):
        return attend(table, history, position, live, count, heads, block)

    _, pull = jax.vjp(local, uvqk)
    upstream = cotangent.astype(jnp.float32) * live[:, None].astype(jnp.float32)
    return pull(upstream)[0]


def silu_slope(h):
    sig = jax.nn.sigmoid(h)
    return sig * (1.0 + h * (1.0 - sig))


def forward_rows(x_rows, w_in, blocks, block):
    rows = x_rows.shape[0]
    wide = w_in.shape[1]
    stacked = x_rows.reshape(rows // block, block, x_rows.shape[1])
    indices = jnp.arange(rows // block, dtype=jnp.int32)

    def forward_one_block(item):
        index, piece = item

        def forward_compute(piece):
            h = jnp.dot(piece, w_in, preferred_element_type=jnp.float32)
            return (h, jax.nn.silu(h).astype(jnp.bfloat16))

        def forward_empty(piece):
            return (jnp.zeros((block, wide), jnp.float32), jnp.zeros((block, wide), jnp.bfloat16))

        return lax.cond(index < blocks, forward_compute, forward_empty, piece)

    h_all, mapped = lax.map(forward_one_block, (indices, stacked))
    return (h_all.reshape(rows, wide), mapped.reshape(rows, wide))


def backward_rows(x_rows, grad_rows, h_all, w_in, blocks, block):
    rows = x_rows.shape[0]
    wide = w_in.shape[1]
    width = w_in.shape[0]
    nblocks = rows // block
    indices = jnp.arange(nblocks, dtype=jnp.int32)

    def backward_one_block(item):
        index, slope, h = item

        def backward_compute(args):
            slope, h = args
            grad_h = (slope.astype(jnp.float32) * silu_slope(h)).astype(jnp.bfloat16)
            back = lax.dot_general(
                grad_h, w_in, (((1,), (1,)), ((), ())), preferred_element_type=jnp.float32
            )
            return (back.astype(jnp.bfloat16), grad_h)

        def backward_empty(args):
            return (jnp.zeros((block, width), jnp.bfloat16), jnp.zeros((block, wide), jnp.bfloat16))

        return lax.cond(index < blocks, backward_compute, backward_empty, (slope, h))

    grad_x, grad_h = lax.map(
        backward_one_block,
        (indices, grad_rows.reshape(nblocks, block, wide), h_all.reshape(nblocks, block, wide)),
    )
    grad_h = grad_h.reshape(rows, wide)
    grad_w = lax.dot_general(
        x_rows, grad_h, (((0,), (0,)), ((), ())), preferred_element_type=jnp.float32
    )
    return (grad_x.reshape(rows, width), grad_w)


def shards(histories, lengths, cotangent, w_in):
    rows = histories.shape[0]
    width = histories.shape[1]
    wide = w_in.shape[1]
    block = BLOCK
    history, position, live, count, used = layout(lengths, rows, block)
    members = lax.axis_size("member")
    per = rows // members
    flags = live.astype(jnp.int32)
    moved, moved_flags = (
        lax.all_to_all(
            histories.reshape(per, members, width),
            "member",
            split_axis=1,
            concat_axis=1,
            tiled=True,
        ),
        lax.all_to_all(
            flags.reshape(per, members), "member", split_axis=1, concat_axis=1, tiled=True
        ),
    )
    moved = moved.reshape(rows, width)
    moved_flags = moved_flags.reshape(rows)
    order = jnp.argsort(1 - moved_flags, stable=True)
    restore = jnp.argsort(order)
    present = jnp.sum(moved_flags).astype(jnp.int32)
    blocks = (present + block - 1) // block
    packed = moved[order]
    h_all, mapped = forward_rows(packed, w_in, blocks, block)
    mapped = lax.all_to_all(
        mapped[restore].reshape(per, members, wide),
        "member",
        split_axis=1,
        concat_axis=1,
        tiled=True,
    ).reshape(rows, wide)
    slopes = pull_back(mapped, cotangent, history, position, live, count, HEADS, block)
    arrived = lax.all_to_all(
        slopes.reshape(per, members, wide), "member", split_axis=1, concat_axis=1, tiled=True
    ).reshape(rows, wide)
    grad_packed, partial_value = backward_rows(packed, arrived[order], h_all, w_in, blocks, block)
    grad_rows = lax.all_to_all(
        grad_packed[restore].reshape(per, members, width),
        "member",
        split_axis=1,
        concat_axis=1,
        tiled=True,
    ).reshape(rows, width)
    grad_w = lax.psum_scatter(partial_value, "member", scatter_dimension=0, tiled=True)
    grad_w = lax.psum(grad_w, "group")
    return (grad_rows, grad_w)


def solution(mesh):
    return jax.shard_map(
        shards,
        mesh=mesh,
        in_specs=(
            P(("group", "member"), None),
            P(("group", "member")),
            P(("group", "member"), None),
            P(),
        ),
        out_specs=(P(("group", "member"), None), P("member", None)),
        check_vma=False,
    )
```

profile of v0, /device:TPU:1, one launch (start us, length us, event | category | flops | bytes accessed | tf_op | source)
XLA Modules:
  0.0 627.1 jit_solution(17876297318785806232)
XLA Ops:
  9.6 11.9 %all-to-all-start = ((s32[16,32,1]{0,2,1:T(1,128)}), s32[16,32,1]{0,2,1:T(1,128)S(1)}, u32[]{:S(2)}, u32[]{:S(2)}) async-start(s32[16,32,1]{0,2,1:T(1,128)} %copy.256), calls=%async_computation | async-start | bytes 32768 | tf_op jit(solution)/shard_map/all_to_all | solution.py:147
  21.5 2.8 copy.257
  24.3 5.8 all-to-all-done
  30.1 3.9 all-to-all-start.1
  35.5 3.8 sort.34
  39.3 3.8 sort.35
  43.1 15.3 %all-to-all-done.1 = bf16[16,32,1024]{2,0,1:T(8,128)(2,1)S(1)} async-done(((bf16[16,32,1024]{2,0,1:T(8,128)(2,1)}), bf16[16,32,1024]{2,0,1:T(8,128)(2,1)S(1)}, u32[]{:S(2)}, u32[]{:S(2)}) %all-to-all-start.1) | async-done | bytes 1048608 | tf_op jit(solution)/shard_map/all_to_all | solution.py:140
  59.0 2.8 gather_fusion
  62.0 28.0 %while.24 = (s32[]{:T(128)}, f32[4,128,2048]{2,1,0:T(8,128)}, bf16[4,128,2048]{2,1,0:T(8,128)(2,1)S(1)}, s32[4]{0:T(128)S(1)}, s32[]{:T(128)}, /*index=5*/bf16[4...) while((s32[]{:T(128)}, f32[4,128,2048]{2,1,0:T(8,128)}, bf16[4,128,2048]{2,1,0:T(8,128)(2,1)S(1)}, ...), condition=%wide.region_9.10_spmd, body=%wide.region_6.9_spmd.sunk | while | flops 538181632 | bytes 10224795 | solution.py:92
  63.3 5.5 conditional.4
  63.3 4.0 fusion.1
  72.4 5.5 conditional.4
  72.5 4.0 fusion.1
  90.0 3.4 gather_fusion.1
  93.4 4.1 copy.260
  97.5 7.4 %all-to-all-start.2 = ((bf16[16,32,2048]{2,0,1:T(8,128)(2,1)}), bf16[16,32,2048]{2,0,1:T(8,128)(2,1)}, u32[]{:S(2)}, u32[]{:S(2)}) async-start(bf16[16,32,2048]{2,0,1:T(8,128)(2,1)} %copy.260), calls=%async_computation.2 | async-start | bytes 4194304 | tf_op jit(solution)/shard_map/all_to_all | solution.py:159
  108.6 43.9 %all-to-all-done.2 = bf16[16,32,2048]{2,0,1:T(8,128)(2,1)} async-done(((bf16[16,32,2048]{2,0,1:T(8,128)(2,1)}), bf16[16,32,2048]{2,0,1:T(8,128)(2,1)}, u32[]{:S(2)}, u32[]{:S(2)}) %all-to-all-start.2) | async-done | bytes 2097184 | tf_op jit(solution)/shard_map/all_to_all | solution.py:159
  152.4 2.7 copy.261
  172.9 2.9 fusion.52
  181.6 3.1 fusion.53
  224.0 6.1 all-to-all-start.3
  230.1 48.0 %all-to-all-done.3 = bf16[16,32,2048]{2,0,1:T(8,128)(2,1)} async-done(((bf16[16,32,2048]{2,0,1:T(8,128)(2,1)}), bf16[16,32,2048]{2,0,1:T(8,128)(2,1)}, u32[]{:S(2)}, u32[]{:S(2)}) %all-to-all-start.3) | async-done | bytes 2097184 | tf_op jit(solution)/shard_map/all_to_all | solution.py:167
  280.8 3.5 gather_fusion.2
  286.0 20.8 %while.25 = (s32[]{:T(128)}, bf16[4,128,1024]{2,1,0:T(8,128)(2,1)S(1)}, bf16[4,128,2048]{2,1,0:T(8,128)(2,1)}, s32[4]{0:T(128)S(1)}, s32[]{:T(128)}, /*index=5*/...) while((s32[]{:T(128)}, ...), condition=%wide.region_19.20_spmd, body=%wide.region_16.19_spmd.sunk | while | flops 542244864 | bytes 9700527 | solution.py:119
  287.2 6.0 conditional.5
  289.0 4.2 fusion.5
  295.4 6.0 conditional.5
  297.2 4.2 fusion.5
  306.8 7.2 %fusion.66 = f32[1024,2048]{1,0:T(8,128)} fusion(bf16[512,1024]{1,0:T(8,128)(2,1)S(1)} %bitcast.205, bf16[512,2048]{1,0:T(8,128)(2,1)} %bitcast.215), kind=kOutput, calls=%fused_computation.144 | convolution fusion | flops 2147483648 | bytes 11534336 | tf_op jit(solution)/shard_map/dot_general | solution.py:124
  317.6 4.4 all-to-all-start.4
  322.1 228.6 %reduce-scatter.2.cloned.1.call-done = f32[32,2048]{1,0:T(8,128)} async-done(((f32[1024,2048]{1,0:T(8,128)}), f32[32,2048]{1,0:T(8,128)}) %reduce-scatter.2.cloned.1.call-update) | async-done | bytes 262160 | tf_op jit(solution)/shard_map/reduce_scatter | solution.py:178
  552.3 66.1 %all-reduce.16.cloned.1.call-done = f32[32,2048]{1,0:T(8,128)} async-done(((f32[32,2048]{1,0:T(8,128)}), f32[32,2048]{1,0:T(8,128)}) %all-reduce.16.cloned.1.call-update) | async-done | bytes 262160 | tf_op jit(solution)/shard_map/psum | solution.py:179
  (248 shorter events, 110.3 us)
Async XLA Ops:
  9.6 20.4 %all-to-all-start = ((s32[16,32,1]{0,2,1:T(1,128)}), s32[16,32,1]{0,2,1:T(1,128)S(1)}, u32[]{:S(2)}, u32[]{:S(2)}) async-start(s32[16,32,1]{0,2,1:T(1,128)} %copy.256), calls=%async_computation | async-start | bytes 32768 | tf_op jit(solution)/shard_map/all_to_all | solution.py:147
  30.1 28.3 %all-to-all-start.1 = ((bf16[16,32,1024]{2,0,1:T(8,128)(2,1)}), bf16[16,32,1024]{2,0,1:T(8,128)(2,1)S(1)}, u32[]{:S(2)}, u32[]{:S(2)}) async-start(bf16[16,32,1024]{2,0,1:T(8,128)(2,1)} %copy.257), calls=%async_computation.1 | async-start | bytes 2097152 | tf_op jit(solution)/shard_map/all_to_all | solution.py:140
  97.5 7.4 %copy-start.43 = (s32[2]{0:T(128)S(1)}, s32[2]{0:T(128)}, u32[]{:S(2)}) copy-start(s32[2]{0:T(128)} %param.13) | copy-start | bytes 28
  97.5 55.0 %all-to-all-start.2 = ((bf16[16,32,2048]{2,0,1:T(8,128)(2,1)}), bf16[16,32,2048]{2,0,1:T(8,128)(2,1)}, u32[]{:S(2)}, u32[]{:S(2)}) async-start(bf16[16,32,2048]{2,0,1:T(8,128)(2,1)} %copy.260), calls=%async_computation.2 | async-start | bytes 4194304 | tf_op jit(solution)/shard_map/all_to_all | solution.py:159
  158.8 4.6 copy-start.9
  158.9 4.4 copy-start.11
  163.4 4.7 copy-start.7
  164.5 3.6 copy-start.4
  170.4 5.4 copy-start.2
  171.6 4.2 copy-start.13
  172.9 2.9 copy-start.28
  181.6 3.1 copy-start.21
  186.6 2.9 copy-start.1
  186.6 2.9 copy-start.6
  194.2 3.6 copy-start.31
  194.2 3.6 copy-start.36
  194.2 3.6 copy-start.45
  196.2 3.1 copy-start.8
  199.3 2.8 copy-start.34
  199.3 2.8 copy-start.44
  200.0 3.5 copy-start.10
  200.0 4.5 copy-start.12
  201.3 4.5 copy-start.17
  205.9 3.8 copy-start.27
  211.9 2.6 copy-start.16
  211.9 2.6 copy-start.32
  211.9 2.6 copy-start.41
  224.0 54.1 %all-to-all-start.3 = ((bf16[16,32,2048]{2,0,1:T(8,128)(2,1)}), bf16[16,32,2048]{2,0,1:T(8,128)(2,1)}, u32[]{:S(2)}, u32[]{:S(2)}) async-start(bf16[16,32,2048]{2,0,1:T(8,128)(2,1)} %copy.305), calls=%async_computation.3 | async-start | bytes 4194304 | tf_op jit(solution)/shard_map/all_to_all | solution.py:167
  230.0 320.6 %reduce-scatter.2.cloned.1.call-start = ((), (), s32[]{:S(2)}) async-start(), calls=%async_computation.6 | async-start | bytes 8650752 | tf_op jit(solution)/shard_map/reduce_scatter | solution.py:178
  286.0 20.8 %copy-start = (bf16[4,128,1024]{2,1,0:T(8,128)(2,1)S(1)}, bf16[4,128,1024]{2,1,0:T(8,128)(2,1)}, u32[]{:S(2)}) copy-start(bf16[4,128,1024]{2,1,0:T(8,128)(2,1)} %get-tuple-element.400) | copy-start | bytes 3145732
  317.6 233.1 %all-to-all-start.4 = ((bf16[16,32,1024]{2,0,1:T(8,128)(2,1)}), bf16[16,32,1024]{2,0,1:T(8,128)(2,1)S(1)}, u32[]{:S(2)}, u32[]{:S(2)}) async-start(bf16[16,32,1024]{2,0,1:T(8,128)(2,1)} %copy.307), calls=%async_computation.4 | async-start | bytes 2097152 | tf_op jit(solution)/shard_map/all_to_all | solution.py:171
  322.0 296.4 %all-reduce.16.cloned.1.call-start = ((), (), s32[]{:S(2)}) async-start(), calls=%async_computation.7 | async-start | bytes 524288 | tf_op jit(solution)/shard_map/psum | solution.py:179
  (24 other events, 35.8 us)
Sparse Core Ops, SparseCore 0:
  314.1 236.4 reduce-scatter.1
  553.1 65.2 all-reduce.15
where the time goes:
time: 636 us; the launch traced here: 627 us
  waiting for transfers between devices  408 us (64%)
  local copies, waits for them, and re-layouts  82.3 us (13%)
  matrix products  56.1 us (9%)
  starting transfers between devices  33.7 us (5%)
  other arithmetic  25.7 us (4%)
  between operations  15.9 us (2%)
    reduce_scatter x1, waiting for transfers between devices, shards(): lax.psum_scatter(partial_value, 'member', scatter_dimension=0, tiled=True)  229 us
    psum x1, waiting for transfers between devices, shards(): grad_w = lax.psum(grad_w, 'group')  66.1 us
    all_to_all x1, waiting for transfers between devices, shards(): lax.all_to_all(slopes.reshape(per, members, wide), 'member', split_axis=1...  48 us
    all_to_all x1, waiting for transfers between devices, shards(): lax.all_to_all(mapped[restore].reshape(per, members, wide), 'member', spl...  43.9 us
    dot_general x12, matrix products, attend(): jnp.einsum('hqk,khd->qhd', weights, values[:high], precision=lax.Precisio...  23.4 us
    all_to_all x1, waiting for transfers between devices, shards(): lax.all_to_all(histories.reshape(per, members, width), 'member', split_ax...  15.3 us
    dynamic_update_slice x12, local copies, waits for them, and re-layouts, forward_rows(): h_all, mapped = lax.map(forward_one_block, (indices, stacked))  12.9 us
  transfers between devices with their start and end apart: 7, of which 6 were waited for; matrix products, arithmetic and copies ran while one was open for 3% of the time, Pallas kernels for 0%

commit v1 on v0

v1 whole, which is shorter than its diff:
```python
import jax
import jax.numpy as jnp
from jax import lax
from jax.sharding import PartitionSpec as P
from jax.experimental import pallas as pl
from jax.experimental.pallas import tpu as pltpu

HEADS = 4
BLOCK = 128
NT = (((1,), (1,)), ((), ()))
TN = (((0,), (0,)), ((), ()))


def mm(a, b, dims=(((1,), (0,)), ((), ()))):
    return lax.dot_general(a, b, dims, preferred_element_type=jnp.float32)


def grads_kernel(core_ref, len_ref, x_ref, w_hbm, cot_ref, keep_ref, send_ref,
                 w_ref, slope_ref, act_ref, p_ref, s_ref, att_ref, da_ref, g_ref, sems):
    rows, width = cot_ref.shape
    nblocks = rows // BLOCK
    size = width // HEADS
    half = width // 2
    scale = size ** -0.5
    order = (2, 3, 1, 0)
    copies = {}
    for s in order:
        cols = pl.ds(s * width, width)
        copies[s] = pltpu.make_async_copy(w_hbm.at[:, cols], w_ref.at[:, cols], sems.at[s])
        copies[s].start()
    for s in order:
        copies[s].wait()
        for i in range(2):
            r = pl.ds(i * (rows // 2), rows // 2)
            cols = pl.ds(s * width, width)
            h = mm(x_ref[r, :], w_ref[:, cols])
            sig = 0.5 * jnp.tanh(0.5 * h) + 0.5
            act = h * sig
            act_ref[r, cols] = act.astype(jnp.bfloat16)
            slope_ref[r, cols] = sig + act * (1.0 - sig)

    def col(s, h):
        return pl.ds(s * width + h * size, size)

    core = core_ref[0]

    def put(s, h, r, grad):
        value = grad.astype(jnp.bfloat16).astype(jnp.float32) * slope_ref[r, col(s, h)]
        to = s * half + (h % (HEADS // 2)) * size
        g_ref[(h // (HEADS // 2)) ^ core, r, pl.ds(to, size)] = value.astype(jnp.bfloat16)

    l0 = len_ref[0]
    l1 = len_ref[1]
    start1 = ((l0 + (BLOCK - 1)) // BLOCK) * BLOCK
    for i in range(nblocks):
        first = max(0, i - 2)
        span = i + 1 - first
        r = pl.ds(i * BLOCK, BLOCK)
        keys = pl.ds(first * BLOCK, span * BLOCK)
        row = i * BLOCK + lax.broadcasted_iota(jnp.int32, (BLOCK, 1), 0)
        in0 = row < l0
        in1 = (row >= start1) & (row < start1 + l1)
        low = jnp.where(in1, start1, 0)
        high = jnp.where(in0 | in1, row, -1)
        count = jnp.where(in0, l0, jnp.where(in1, l1, 1))
        inv = 1.0 / count.astype(jnp.float32)
        live = in0 | in1
        c = first * BLOCK + lax.broadcasted_iota(jnp.int32, (BLOCK, span * BLOCK), 1)
        valid = (c >= low) & (c <= high)
        for h in range(HEADS):
            t = mm(act_ref[r, col(2, h)], act_ref[keys, col(3, h)], NT)
            sig = 0.5 * jnp.tanh(t * (0.5 * scale)) + 0.5
            p = t * scale * sig
            p_b = jnp.where(valid, p, 0.0).astype(jnp.bfloat16)
            p_ref[h, r, keys] = p_b
            s_ref[h, r, keys] = jnp.where(valid, sig + p * (1.0 - sig), 0.0)
            att_ref[r, pl.ds(h * size, size)] = mm(p_b, act_ref[keys, col(1, h)]) * inv
        att = att_ref[r, :]
        cen = att - jnp.mean(att, axis=1, keepdims=True)
        rstd = lax.rsqrt(jnp.mean(cen * cen, axis=1, keepdims=True) + 1e-05)
        z = cen * rstd
        up = jnp.where(live, cot_ref[r, :].astype(jnp.float32), 0.0)
        du = up * z
        dz = up * act_ref[r, pl.ds(0, width)].astype(jnp.float32)
        m1 = jnp.mean(dz, axis=1, keepdims=True)
        m2 = jnp.mean(dz * z, axis=1, keepdims=True)
        da = (dz - m1 - z * m2) * (rstd * inv)
        da_ref[r, :] = da.astype(jnp.bfloat16)
        for h in range(HEADS):
            put(0, h, r, du[:, h * size:(h + 1) * size])
        for h in range(HEADS):
            dp = mm(da_ref[r, pl.ds(h * size, size)], act_ref[keys, col(1, h)], NT)
            ds = (dp * s_ref[h, r, keys]).astype(jnp.bfloat16)
            s_ref[h, r, keys] = ds.astype(jnp.float32)
            put(2, h, r, mm(ds, act_ref[keys, col(3, h)]) * scale)
    for j in range(nblocks):
        last = min(nblocks, j + 3)
        r = pl.ds(j * BLOCK, BLOCK)
        qs = pl.ds(j * BLOCK, (last - j) * BLOCK)
        for h in range(HEADS):
            put(1, h, r, mm(p_ref[h, qs, r], da_ref[qs, pl.ds(h * size, size)], TN))
            ds = s_ref[h, qs, r].astype(jnp.bfloat16)
            put(3, h, r, mm(ds, act_ref[qs, col(2, h)], TN) * scale)
    keep_ref[...] = g_ref[0]
    send_ref[...] = g_ref[1]


def grads(core, lengths, x, w, cot):
    rows, d = x.shape
    width = cot.shape[1]
    wide = w.shape[1]
    vmem = pl.BlockSpec(memory_space=pltpu.VMEM)
    smem = pl.BlockSpec(memory_space=pltpu.SMEM)
    return pl.pallas_call(
        grads_kernel,
        out_shape=[jax.ShapeDtypeStruct((rows, wide // 2), jnp.bfloat16)] * 2,
        in_specs=[smem, smem, vmem, pl.BlockSpec(memory_space=pl.ANY), vmem],
        out_specs=[vmem, vmem],
        scratch_shapes=[
            pltpu.VMEM((d, wide), jnp.bfloat16),
            pltpu.VMEM((rows, wide), jnp.float32),
            pltpu.VMEM((rows, wide), jnp.bfloat16),
            pltpu.VMEM((HEADS, rows, rows), jnp.bfloat16),
            pltpu.VMEM((HEADS, rows, rows), jnp.float32),
            pltpu.VMEM((rows, width), jnp.float32),
            pltpu.VMEM((rows, width), jnp.bfloat16),
            pltpu.VMEM((2, rows, wide // 2), jnp.bfloat16),
            pltpu.SemaphoreType.DMA((4,)),
        ],
        compiler_params=pltpu.CompilerParams(vmem_limit_bytes=40 * 2**20),
        cost_estimate=pl.CostEstimate(flops=4 * 10**9, bytes_accessed=8 * 10**6, transcendentals=2 * 10**6),
        name="uvqk_grads",
    )(core, lengths, x, w, cot)


def transpose_kernel(x_ref, y_ref, xt_ref):
    rows, d = x_ref.shape
    for i, ref in enumerate((x_ref, y_ref)):
        for b in range(0, d, 256):
            for r in range(0, rows, 256):
                xt_ref[pl.ds(b, 256), pl.ds(i * rows + r, 256)] = ref[pl.ds(r, 256), pl.ds(b, 256)].T


def transposed(x, y):
    rows, d = x.shape
    vmem = pl.BlockSpec(memory_space=pltpu.VMEM)
    return pl.pallas_call(
        transpose_kernel,
        out_shape=jax.ShapeDtypeStruct((d, 2 * rows), jnp.bfloat16),
        in_specs=[vmem, vmem],
        out_specs=vmem,
        compiler_params=pltpu.CompilerParams(vmem_limit_bytes=16 * 2**20),
        cost_estimate=pl.CostEstimate(flops=0, bytes_accessed=4 * 2**20, transcendentals=0),
        name="transpose_rows",
    )(x, y)


def weights_kernel(where_ref, xt_ref, keep_ref, recv_ref, o0, o1, o2, o3):
    core, first, second = where_ref[0], where_ref[1], where_ref[2]
    rows = keep_ref.shape[0]
    for k, out in enumerate((o0, o1, o2, o3)):
        for l in range(4):
            a = lax.rem(first + k, 4)
            b = lax.rem(second + l, 4)
            rb = jnp.where(core == 0, a, b)
            cb = jnp.where(core == 0, b, a)
            rs = pl.ds(pl.multiple_of(rb * 256, 256), 256)
            cs = pl.ds(pl.multiple_of(cb * 256, 256), 256)
            total = mm(xt_ref[rs, pl.ds(0, rows)], keep_ref[:, cs])
            total += mm(xt_ref[rs, pl.ds(rows, rows)], recv_ref[:, cs])
            out[l] = total.astype(jnp.bfloat16)


def weights(where, xt, keep, recv):
    vmem = pl.BlockSpec(memory_space=pltpu.VMEM)
    smem = pl.BlockSpec(memory_space=pltpu.SMEM)
    return pl.pallas_call(
        weights_kernel,
        out_shape=[jax.ShapeDtypeStruct((4, 256, 256), jnp.bfloat16)] * 4,
        in_specs=[smem, vmem, vmem, vmem],
        out_specs=[vmem] * 4,
        compiler_params=pltpu.CompilerParams(vmem_limit_bytes=24 * 2**20),
        cost_estimate=pl.CostEstimate(flops=2 * 2**30, bytes_accessed=6 * 2**20, transcendentals=0),
        name="weight_grads",
    )(where, xt, keep, recv)


def rows_kernel(core_ref, keep_ref, send_ref, w_ref, out_ref):
    core = core_ref[0]
    rows = keep_ref.shape[0]
    for r in range(0, rows, 256):
        total = jnp.zeros((256, w_ref.shape[0]), jnp.float32)
        for i, ref in enumerate((keep_ref, send_ref)):
            for s in range(4):
                cols = pl.ds(pl.multiple_of(s * 512 + (core ^ i) * 256, 256), 256)
                total += mm(ref[pl.ds(r, 256), pl.ds(s * 256, 256)], w_ref[:, cols], NT)
        out_ref[pl.ds(r, 256), :] = total.astype(jnp.bfloat16)


def row_grads(core, keep, send, w):
    vmem = pl.BlockSpec(memory_space=pltpu.VMEM)
    smem = pl.BlockSpec(memory_space=pltpu.SMEM)
    return pl.pallas_call(
        rows_kernel,
        out_shape=jax.ShapeDtypeStruct((keep.shape[0], w.shape[0]), jnp.bfloat16),
        in_specs=[smem, vmem, vmem, vmem],
        out_specs=vmem,
        compiler_params=pltpu.CompilerParams(vmem_limit_bytes=24 * 2**20),
        cost_estimate=pl.CostEstimate(flops=2 * 2**30, bytes_accessed=7 * 2**20, transcendentals=0),
        name="row_grads",
    )(core, keep, send, w)


def place_kernel(where_ref, mine_ref, other_ref, out_ref):
    core, y = where_ref[0], where_ref[3]
    for i, ref in enumerate((mine_ref, other_ref)):
        for k in range(4):
            s = lax.rem(y + 4 - k, 4)
            cols = pl.ds(pl.multiple_of(s * 512 + (core ^ i) * 256, 256), 256)
            out_ref[:, cols] = ref[k]


def place(where, mine, other):
    vmem = pl.BlockSpec(memory_space=pltpu.VMEM)
    smem = pl.BlockSpec(memory_space=pltpu.SMEM)
    return pl.pallas_call(
        place_kernel,
        out_shape=jax.ShapeDtypeStruct((mine.shape[1], 2048), jnp.float32),
        in_specs=[smem, vmem, vmem],
        out_specs=vmem,
        name="place_columns",
    )(where, mine, other)


AXES = ("group", "member")
NY, NX, NZ = 4, 4, 8


def pairs(move):
    out = []
    for i in range(2 * NY * NX * NZ):
        g, m = divmod(i, NX * NZ)
        y, c = divmod(g, 2)
        x, z = divmod(m, NZ)
        y, c, x, z = move(y, c, x, z)
        out.append((i, ((y % NY) * 2 + c % 2) * NX * NZ + (x % NX) * NZ + z % NZ))
    return out


def permute(value, move):
    return lax.ppermute(value, AXES, pairs(move))


def other_core(y, c, x, z):
    return (y, c + 1, x, z)


def first_axis(k):
    return lambda y, c, x, z: (y, c, x + k, z) if c == 0 else (y + k, c, x, z)


def second_axis(k):
    return lambda y, c, x, z: (y + k, c, x, z) if c == 0 else (y, c, x + k, z)


def along_y(k):
    return lambda y, c, x, z: (y + k, c, x, z)


def along_z(k):
    return lambda y, c, x, z: (y, c, x, z + k)


def f32(value):
    return value.astype(jnp.float32)


def shards(histories, lengths, cotangent, w_in):
    group, member = lax.axis_index("group"), lax.axis_index("member")
    y, core = group // 2, group % 2
    x, z = member // NZ, member % NZ
    first = jnp.where(core == 0, x, y)
    second = jnp.where(core == 0, y, x)
    where = jnp.stack([core, first, second, y]).astype(jnp.int32)
    theirs = permute(histories, other_core)
    keep, send = grads(where, lengths, histories, w_in, cotangent)
    recv = permute(send, other_core)
    xt = transposed(histories, theirs)
    parts = weights(where, xt, keep, recv)
    moved = [permute(parts[k], first_axis(k)) for k in (1, 2, 3)]
    grad_rows = row_grads(where, keep, send, w_in)
    summed = [f32(parts[0][l]) + f32(moved[0][l]) + f32(moved[1][l]) + f32(moved[2][l]) for l in range(4)]
    moved = [permute(summed[k].astype(jnp.bfloat16), second_axis(k)) for k in (1, 2, 3)]
    block = summed[0] + f32(moved[0]) + f32(moved[1]) + f32(moved[2])

    block = block.astype(jnp.bfloat16).reshape(NZ, 32, 256)
    nz = [[g * NZ + i for i in range(NZ)] for g in range(NX)]
    block = lax.all_to_all(block, "member", 0, 0, tiled=True, axis_index_groups=nz)
    block = jnp.sum(f32(block), axis=0)

    gathered = jnp.stack([block] + [permute(block, along_y(k)) for k in (1, 2, 3)])
    grad_w = place(where, gathered, permute(gathered, other_core))
    return (grad_rows, grad_w)


def solution(mesh):
    return jax.shard_map(
        shards,
        mesh=mesh,
        in_specs=(
            P(("group", "member"), None),
            P(("group", "member")),
            P(("group", "member"), None),
            P(),
        ),
        out_specs=(P(("group", "member"), None), P("member", None)),
        check_vma=False,
    )
```

time: 636 us -> 84.6 us (0.13); the launches traced: 627 us -> 84.3 us
  waiting for transfers between devices: 408 us -> 23.3 us
  local copies, waits for them, and re-layouts: 82.3 us -> 5.76 us
  matrix products: 56.1 us -> 0 us
  other arithmetic: 25.7 us -> 0.46 us
  Pallas kernels: 0 us -> 21.3 us
  starting transfers between devices: 33.7 us -> 18 us
  between operations: 15.9 us -> 0.71 us
  blocking collectives: 0 us -> 14.8 us
    reduce_scatter x1 -> x0, waiting for transfers between devices: 229 us -> none  [shards(): lax.psum_scatter(partial_value, 'member', scatter_dimension=0, tiled=True)]
    all_to_all x5 -> x0, waiting for transfers between devices: 113 us -> none  [the longest x1 48 us: shards(): lax.all_to_all(slopes.reshape(per, members, wide), 'member', split_axis=1...]
    psum x1 -> x0, waiting for transfers between devices: 66.1 us -> none  [shards(): grad_w = lax.psum(grad_w, 'group')]
    dot_general x29 -> x0, matrix products: 56.1 us -> none  [the longest x12 23.4 us: attend(): jnp.einsum('hqk,khd->qhd', weights, values[:high], precision=lax.Precisio...]
    all_to_all x5 -> x0, starting transfers between devices: 33.7 us -> none  [the longest x1 11.9 us: shards(): lax.all_to_all(flags.reshape(per, members), 'member', split_axis=1, conca...]
    ppermute x0 -> x12, waiting for transfers between devices: none -> 23.3 us  [permute(): return lax.ppermute(value, AXES, pairs(move))]
    pallas_call x0 -> x5, Pallas kernels: none -> 21.3 us  [the longest x1 12.1 us: grads(): pl.pallas_call(grads_kernel, out_shape=[jax.ShapeDtypeStruct((rows, wide...]
    reshape x15 -> x0, local copies, waits for them, and re-layouts: 20.1 us -> none  [the longest x8 6.96 us: attend(): outputs.append(jnp.einsum('hqk,khd->qhd', weights, values[:high], precisi...]
  transfers between devices with their start and end apart: 7 -> 12, of which waited for: 6 -> 8; matrix products, arithmetic and copies ran while one was open for 3% -> 0% of each run, Pallas kernels for 0% -> 20%
where the time goes in v1:
time: 84.6 us; the launch traced here: 84.3 us
  waiting for transfers between devices  23.3 us (28%)
  Pallas kernels  21.3 us (25%)
  starting transfers between devices  18 us (21%)
  blocking collectives  14.8 us (17%)
  local copies, waits for them, and re-layouts  5.76 us (7%)
    ppermute x12, waiting for transfers between devices, permute(): return lax.ppermute(value, AXES, pairs(move))  23.3 us
    ppermute x12, starting transfers between devices, permute(): return lax.ppermute(value, AXES, pairs(move))  18 us
    all_to_all x1, blocking collectives, shards(): lax.all_to_all(block, 'member', 0, 0, tiled=True, axis_index_groups=nz)  14.8 us
    pallas_call x1, Pallas kernels, grads(): pl.pallas_call(grads_kernel, out_shape=[jax.ShapeDtypeStruct((rows, wide...  12.1 us
    unnamed x14, local copies, waits for them, and re-layouts  5.76 us
    pallas_call x1, Pallas kernels, row_grads(): pl.pallas_call(rows_kernel, out_shape=jax.ShapeDtypeStruct((keep.shape[0]...  3.89 us
    pallas_call x1, Pallas kernels, weights(): pl.pallas_call(weights_kernel, out_shape=[jax.ShapeDtypeStruct((4, 256, 2...  2.97 us
    pallas_call x1, Pallas kernels, place(): pl.pallas_call(place_kernel, out_shape=jax.ShapeDtypeStruct((mine.shape[1...  1.71 us
  transfers between devices with their start and end apart: 12, of which 8 were waited for; matrix products, arithmetic and copies ran while one was open for 0% of the time, Pallas kernels for 20%

profile of v1, /device:TPU:1, one launch (start us, length us, event | category | flops | bytes accessed | tf_op | source)
XLA Modules:
  0.0 84.3 jit_solution(4123354075722558332)
XLA Ops:
  0.6 3.3 %collective-permute-start = (bf16[512,1024]{1,0:T(8,128)(2,1)}, bf16[512,1024]{1,0:T(8,128)(2,1)S(1)}, u32[]{:S(2)}, u32[]{:S(2)}) collective-permute-start(bf16[512,1024]{1,0:T(8,128)(2,1)} %x_ref.3), channel_id=1, source_target_pairs={{0,32},{1,33},{2,34},{3,35},{4,36},{5,37},{6,38},{7,39},{8,40},{9,... | collective-permute-start | bytes 3145736 | tf_op jit(solution)/shard_map/ppermute | solution.py:251
  4.0 1.2 %copy-done = bf16[512,1024]{1,0:T(8,128)(2,1)S(1)} copy-done((bf16[512,1024]{1,0:T(8,128)(2,1)S(1)}, bf16[512,1024]{1,0:T(8,128)(2,1)}, u32[]{:S(2)}) %copy-start) | copy-done | bytes 1048600
  5.3 2.2 %copy-done.2 = bf16[1024,2048]{1,0:T(8,128)(2,1)S(1)} copy-done((bf16[1024,2048]{1,0:T(8,128)(2,1)S(1)}, bf16[1024,2048]{1,0:T(8,128)(2,1)}, u32[]{:S(2)}) %copy-start.2) | copy-done | bytes 4194328
  7.5 1.0 %copy-done.3 = bf16[512,512]{1,0:T(8,128)(2,1)S(1)} copy-done((bf16[512,512]{1,0:T(8,128)(2,1)S(1)}, bf16[512,512]{1,0:T(8,128)(2,1)}, u32[]{:S(2)}) %copy-start.3) | copy-done | bytes 524312
  8.5 0.7 copy-done.4
  9.1 12.1 %uvqk_grads.1 = (bf16[512,1024]{1,0:T(8,128)(2,1)S(1)}, bf16[512,1024]{1,0:T(8,128)(2,1)S(1)}) custom-call(s32[4]{0:T(128)S(1)} %pad_add_fusion.core_ref.where_ref, s32[2]{0:T(128)S(1)} %copy-done.4, bf16[512,1024]{1,0:T(8,128)(2,1)S(1)} %copy-done, bf16[1024,2048]{1,0:T(8,128)(2,1)S(1)} %copy-done.2, bf16[512,512]{1,0:T(8,128)(2,1)S(1)} %copy-done.3), custom_call_target="tpu_custom_call" | custom-call | flops 4000000000 | bytes 8000000 | tf_op jit(solution)/shard_map/uvqk_grads/pallas_call | solution.py:114
  21.3 0.3 collective-permute-start.1
  21.6 0.6 transpose_rows.1.xt_ref
  22.2 2.0 %collective-permute-done.1.recv_ref = bf16[512,1024]{1,0:T(8,128)(2,1)S(1)} collective-permute-done((bf16[512,1024]{1,0:T(8,128)(2,1)S(1)}, bf16[512,1024]{1,0:T(8,128)(2,1)S(1)}, u32[]{:S(2)}, u32[]{:S(2)}) %collective-permute-start.1) | collective-permute-done | bytes 1048608 | tf_op jit(solution)/shard_map/ppermute | solution.py:251
  24.2 3.0 %weight_grads.1 = (bf16[4,256,256]{2,1,0:T(8,128)(2,1)S(1)}, bf16[4,256,256]{2,1,0:T(8,128)(2,1)S(1)}, bf16[4,256,256]{2,1,0:T(8,128)(2,1)S(1)}, bf16[4,256,256]{2,1,0:T(8,128)(2,1)S(1)}) custom-call(s32[4]{0:T(128)S(1)} %pad_add_fusion.core_ref.where_ref, bf16[1024,1024]{1,0:T(8,128)(2,1)S(1)} %transpose_rows.1.xt_ref, ...), custom_call_target="tpu_custom_call" | custom-call | flops 2147483648 | bytes 6291456 | tf_op jit(solution)/shard_map/weight_grads/pallas_call | solution.py:177
  27.2 0.1 collective-permute-start.2
  27.3 2.2 %collective-permute-start.3 = (bf16[4,256,256]{2,1,0:T(8,128)(2,1)S(1)}, bf16[4,256,256]{2,1,0:T(8,128)(2,1)S(1)}, u32[]{:S(2)}, u32[]{:S(2)}) collective-permute-start(bf16[4,256,256]{2,1,0:T(8,128)(2,1)S(1)} %get-tuple-element.12), channel_id=1, source_target_pairs={{0,16},{1,17},{2,18},{3,19},{4,20},{5,21},{6,22},{7,23},{8,24},{9,... | collective-permute-start | bytes 1572872 | tf_op jit(solution)/shard_map/ppermute | solution.py:251
  29.4 1.1 %collective-permute-start.4 = (bf16[4,256,256]{2,1,0:T(8,128)(2,1)S(1)}, bf16[4,256,256]{2,1,0:T(8,128)(2,1)S(1)}, u32[]{:S(2)}, u32[]{:S(2)}) collective-permute-start(bf16[4,256,256]{2,1,0:T(8,128)(2,1)S(1)} %get-tuple-element.13), channel_id=1, source_target_pairs={{0,24},{1,25},{2,26},{3,27},{4,28},{5,29},{6,30},{7,31},{8,0},{9,1... | collective-permute-start | bytes 1572872 | tf_op jit(solution)/shard_map/ppermute | solution.py:251
  30.5 11.9 %collective-permute-done.2 = bf16[4,256,256]{2,1,0:T(8,128)(2,1)S(1)} collective-permute-done((bf16[4,256,256]{2,1,0:T(8,128)(2,1)S(1)}, bf16[4,256,256]{2,1,0:T(8,128)(2,1)S(1)}, u32[]{:S(2)}, u32[]{:S(2)}) %collective-permute-start.2) | collective-permute-done | bytes 524320 | tf_op jit(solution)/shard_map/ppermute | solution.py:251
  42.4 0.6 collective-permute-done.4
  43.0 0.2 fusion.3
  43.3 2.7 %collective-permute-start.7 = (bf16[256,256]{1,0:T(8,128)(2,1)S(1)}, bf16[256,256]{1,0:T(8,128)(2,1)S(1)}, u32[]{:S(2)}, u32[]{:S(2)}) collective-permute-start(bf16[256,256]{1,0:T(8,128)(2,1)S(1)} %get-tuple-element.15), channel_id=1, source_target_pairs={{0,192},{1,193},{2,194},{3,195},{4,196},{5,197},{6,198},{7,199},{8... | collective-permute-start | bytes 393224 | tf_op jit(solution)/shard_map/ppermute | solution.py:251
  46.0 0.1 collective-permute-start.6
  46.1 2.2 %collective-permute-done.5 = bf16[256,256]{1,0:T(8,128)(2,1)S(1)} collective-permute-done((bf16[256,256]{1,0:T(8,128)(2,1)S(1)}, bf16[256,256]{1,0:T(8,128)(2,1)S(1)}, u32[]{:S(2)}, u32[]{:S(2)}) %collective-permute-start.5) | collective-permute-done | bytes 131104 | tf_op jit(solution)/shard_map/ppermute | solution.py:251
  48.3 1.0 %collective-permute-done.7 = bf16[256,256]{1,0:T(8,128)(2,1)S(1)} collective-permute-done((bf16[256,256]{1,0:T(8,128)(2,1)S(1)}, bf16[256,256]{1,0:T(8,128)(2,1)S(1)}, u32[]{:S(2)}, u32[]{:S(2)}) %collective-permute-start.7) | collective-permute-done | bytes 131104 | tf_op jit(solution)/shard_map/ppermute | solution.py:251
  49.3 2.0 %collective-permute-done.6 = bf16[256,256]{1,0:T(8,128)(2,1)S(1)} collective-permute-done((bf16[256,256]{1,0:T(8,128)(2,1)S(1)}, bf16[256,256]{1,0:T(8,128)(2,1)S(1)}, u32[]{:S(2)}, u32[]{:S(2)}) %collective-permute-start.6) | collective-permute-done | bytes 131104 | tf_op jit(solution)/shard_map/ppermute | solution.py:251
  51.3 0.1 fusion.2
  51.5 14.8 %all_to_all.5 = bf16[8,32,256]{2,1,0:T(8,128)(2,1)S(1)} all-to-all(bf16[8,32,256]{2,1,0:T(8,128)(2,1)S(1)} %bitcast.23), channel_id=1, replica_groups={{0,1,2,3,4,5,6,7},{8,9,10,11,12,13,14,15},{16,17,18,19,20,21,22,23},{24..., dimensions={0} | all-to-all | bytes 262144 | tf_op jit(solution)/shard_map/all_to_all | solution.py:298
  66.3 2.4 %collective-permute-start.10 = (f32[32,256]{1,0:T(8,128)S(1)}, f32[32,256]{1,0:T(8,128)S(1)}, u32[]{:S(2)}, u32[]{:S(2)}) collective-permute-start(f32[32,256]{1,0:T(8,128)S(1)} %convert_reduce_fusion), channel_id=1, source_target_pairs={{0,192},{1,193},{2,194},{3,195},{4,196},{5,197},{6,198},{7,199},{8... | collective-permute-start | bytes 98312 | tf_op jit(solution)/shard_map/ppermute | solution.py:251
  68.6 0.6 collective-permute-start.9
  69.2 0.4 collective-permute-start.8
  69.7 3.2 %collective-permute-done.9 = f32[32,256]{1,0:T(8,128)S(1)} collective-permute-done((f32[32,256]{1,0:T(8,128)S(1)}, f32[32,256]{1,0:T(8,128)S(1)}, u32[]{:S(2)}, u32[]{:S(2)}) %collective-permute-start.9) | collective-permute-done | bytes 32800 | tf_op jit(solution)/shard_map/ppermute | solution.py:251
  72.9 0.3 collective-permute-done.8
  73.3 4.8 %collective-permute-start.11 = (f32[4,32,256]{2,1,0:T(8,128)S(1)}, f32[4,32,256]{2,1,0:T(8,128)S(1)}, u32[]{:S(2)}, u32[]{:S(2)}) collective-permute-start(f32[4,32,256]{2,1,0:T(8,128)S(1)} %pad_maximum_fusion.mine_ref), channel_id=1, source_target_pairs={{0,32},{1,33},{2,34},{3,35},{4,36},{5,37},{6,38},{7,39},{8,40},{9,... | collective-permute-start | bytes 393224 | tf_op jit(solution)/shard_map/ppermute | solution.py:251
  78.1 3.9 %row_grads.1 = bf16[512,1024]{1,0:T(8,128)(2,1)} custom-call(s32[4]{0:T(128)S(1)} %pad_add_fusion.core_ref.where_ref, bf16[512,1024]{1,0:T(8,128)(2,1)S(1)} %get-tuple-element.8.keep_ref, bf16[512,1024]{1,0:T(8,128)(2,1)S(1)} %get-tuple-element.9.send_ref, bf16[1024,2048]{1,0:T(8,128)(2,1)S(1)} %copy-done.2), custom_call_target="tpu_custom_call" | custom-call | flops 2147483648 | bytes 7340032 | tf_op jit(solution)/shard_map/row_grads/pallas_call | solution.py:203
  82.0 0.6 copy-done.6
  82.6 1.7 %place_columns.1 = f32[32,2048]{1,0:T(8,128)} custom-call(s32[4]{0:T(128)} %copy-done.1, f32[4,32,256]{2,1,0:T(8,128)} %copy-done.5, f32[4,32,256]{2,1,0:T(8,128)} %copy-done.6), custom_call_target="tpu_custom_call" | custom-call | tf_op jit(solution)/shard_map/place_columns/pallas_call | solution.py:226
  (17 shorter events, 0.3 us)
Async XLA Ops:
  0.6 20.9 %collective-permute-start = (bf16[512,1024]{1,0:T(8,128)(2,1)}, bf16[512,1024]{1,0:T(8,128)(2,1)S(1)}, u32[]{:S(2)}, u32[]{:S(2)}) collective-permute-start(bf16[512,1024]{1,0:T(8,128)(2,1)} %x_ref.3), channel_id=1, source_target_pairs={{0,32},{1,33},{2,34},{3,35},{4,36},{5,37},{6,38},{7,39},{8,40},{9,... | collective-permute-start | bytes 3145736 | tf_op jit(solution)/shard_map/ppermute | solution.py:251
  4.0 1.2 %copy-start = (bf16[512,1024]{1,0:T(8,128)(2,1)S(1)}, bf16[512,1024]{1,0:T(8,128)(2,1)}, u32[]{:S(2)}) copy-start(bf16[512,1024]{1,0:T(8,128)(2,1)} %x_ref.3) | copy-start | bytes 3145732
  5.3 2.2 %copy-start.2 = (bf16[1024,2048]{1,0:T(8,128)(2,1)S(1)}, bf16[1024,2048]{1,0:T(8,128)(2,1)}, u32[]{:S(2)}) copy-start(bf16[1024,2048]{1,0:T(8,128)(2,1)} %w_ref.1) | copy-start | bytes 12582916
  7.4 1.0 %copy-start.3 = (bf16[512,512]{1,0:T(8,128)(2,1)S(1)}, bf16[512,512]{1,0:T(8,128)(2,1)}, u32[]{:S(2)}) copy-start(bf16[512,512]{1,0:T(8,128)(2,1)} %cot_ref.1) | copy-start | bytes 1572868
  8.5 0.7 copy-start.4
  9.1 68.9 %copy-start.1 = (s32[4]{0:T(128)}, s32[4]{0:T(128)S(1)}, u32[]{:S(2)}) copy-start(s32[4]{0:T(128)S(1)} %pad_add_fusion.core_ref.where_ref) | copy-start | bytes 52
  21.3 2.9 %collective-permute-start.1 = (bf16[512,1024]{1,0:T(8,128)(2,1)S(1)}, bf16[512,1024]{1,0:T(8,128)(2,1)S(1)}, u32[]{:S(2)}, u32[]{:S(2)}) collective-permute-start(bf16[512,1024]{1,0:T(8,128)(2,1)S(1)} %get-tuple-element.9.send_ref), channel_id=1, source_target_pairs={{0,32},{1,33},{2,34},{3,35},{4,36},{5,37},{6,38},{7,39},{8,40},{9,... | collective-permute-start | bytes 3145736 | tf_op jit(solution)/shard_map/ppermute | solution.py:251
  27.2 15.2 %collective-permute-start.2 = (bf16[4,256,256]{2,1,0:T(8,128)(2,1)S(1)}, bf16[4,256,256]{2,1,0:T(8,128)(2,1)S(1)}, u32[]{:S(2)}, u32[]{:S(2)}) collective-permute-start(bf16[4,256,256]{2,1,0:T(8,128)(2,1)S(1)} %get-tuple-element.11), channel_id=1, source_target_pairs={{0,8},{1,9},{2,10},{3,11},{4,12},{5,13},{6,14},{7,15},{8,16},{9,17... | collective-permute-start | bytes 1572872 | tf_op jit(solution)/shard_map/ppermute | solution.py:251
  27.3 15.1 %collective-permute-start.3 = (bf16[4,256,256]{2,1,0:T(8,128)(2,1)S(1)}, bf16[4,256,256]{2,1,0:T(8,128)(2,1)S(1)}, u32[]{:S(2)}, u32[]{:S(2)}) collective-permute-start(bf16[4,256,256]{2,1,0:T(8,128)(2,1)S(1)} %get-tuple-element.12), channel_id=1, source_target_pairs={{0,16},{1,17},{2,18},{3,19},{4,20},{5,21},{6,22},{7,23},{8,24},{9,... | collective-permute-start | bytes 1572872 | tf_op jit(solution)/shard_map/ppermute | solution.py:251
  29.4 13.6 %collective-permute-start.4 = (bf16[4,256,256]{2,1,0:T(8,128)(2,1)S(1)}, bf16[4,256,256]{2,1,0:T(8,128)(2,1)S(1)}, u32[]{:S(2)}, u32[]{:S(2)}) collective-permute-start(bf16[4,256,256]{2,1,0:T(8,128)(2,1)S(1)} %get-tuple-element.13), channel_id=1, source_target_pairs={{0,24},{1,25},{2,26},{3,27},{4,28},{5,29},{6,30},{7,31},{8,0},{9,1... | collective-permute-start | bytes 1572872 | tf_op jit(solution)/shard_map/ppermute | solution.py:251
  43.2 5.1 %collective-permute-start.5 = (bf16[256,256]{1,0:T(8,128)(2,1)S(1)}, bf16[256,256]{1,0:T(8,128)(2,1)S(1)}, u32[]{:S(2)}, u32[]{:S(2)}) collective-permute-start(bf16[256,256]{1,0:T(8,128)(2,1)S(1)} %get-tuple-element.14), channel_id=1, source_target_pairs={{0,64},{1,65},{2,66},{3,67},{4,68},{5,69},{6,70},{7,71},{8,72},{9,... | collective-permute-start | bytes 393224 | tf_op jit(solution)/shard_map/ppermute | solution.py:251
  43.3 6.0 %collective-permute-start.7 = (bf16[256,256]{1,0:T(8,128)(2,1)S(1)}, bf16[256,256]{1,0:T(8,128)(2,1)S(1)}, u32[]{:S(2)}, u32[]{:S(2)}) collective-permute-start(bf16[256,256]{1,0:T(8,128)(2,1)S(1)} %get-tuple-element.15), channel_id=1, source_target_pairs={{0,192},{1,193},{2,194},{3,195},{4,196},{5,197},{6,198},{7,199},{8... | collective-permute-start | bytes 393224 | tf_op jit(solution)/shard_map/ppermute | solution.py:251
  46.0 5.3 %collective-permute-start.6 = (bf16[256,256]{1,0:T(8,128)(2,1)S(1)}, bf16[256,256]{1,0:T(8,128)(2,1)S(1)}, u32[]{:S(2)}, u32[]{:S(2)}) collective-permute-start(bf16[256,256]{1,0:T(8,128)(2,1)S(1)} %get-tuple-element.16), channel_id=1, source_target_pairs={{0,128},{1,129},{2,130},{3,131},{4,132},{5,133},{6,134},{7,135},{8... | collective-permute-start | bytes 393224 | tf_op jit(solution)/shard_map/ppermute | solution.py:251
  66.3 3.4 %collective-permute-start.10 = (f32[32,256]{1,0:T(8,128)S(1)}, f32[32,256]{1,0:T(8,128)S(1)}, u32[]{:S(2)}, u32[]{:S(2)}) collective-permute-start(f32[32,256]{1,0:T(8,128)S(1)} %convert_reduce_fusion), channel_id=1, source_target_pairs={{0,192},{1,193},{2,194},{3,195},{4,196},{5,197},{6,198},{7,199},{8... | collective-permute-start | bytes 98312 | tf_op jit(solution)/shard_map/ppermute | solution.py:251
  68.6 4.3 %collective-permute-start.9 = (f32[32,256]{1,0:T(8,128)S(1)}, f32[32,256]{1,0:T(8,128)S(1)}, u32[]{:S(2)}, u32[]{:S(2)}) collective-permute-start(f32[32,256]{1,0:T(8,128)S(1)} %convert_reduce_fusion), channel_id=1, source_target_pairs={{0,128},{1,129},{2,130},{3,131},{4,132},{5,133},{6,134},{7,135},{8... | collective-permute-start | bytes 98312 | tf_op jit(solution)/shard_map/ppermute | solution.py:251
  69.2 4.1 %collective-permute-start.8 = (f32[32,256]{1,0:T(8,128)S(1)}, f32[32,256]{1,0:T(8,128)S(1)}, u32[]{:S(2)}, u32[]{:S(2)}) collective-permute-start(f32[32,256]{1,0:T(8,128)S(1)} %convert_reduce_fusion), channel_id=1, source_target_pairs={{0,64},{1,65},{2,66},{3,67},{4,68},{5,69},{6,70},{7,71},{8,72},{9,... | collective-permute-start | bytes 98312 | tf_op jit(solution)/shard_map/ppermute | solution.py:251
  73.3 8.7 %copy-start.5 = (f32[4,32,256]{2,1,0:T(8,128)}, f32[4,32,256]{2,1,0:T(8,128)S(1)}, u32[]{:S(2)}) copy-start(f32[4,32,256]{2,1,0:T(8,128)S(1)} %pad_maximum_fusion.mine_ref) | copy-start | bytes 393220
  73.3 8.7 %collective-permute-start.11 = (f32[4,32,256]{2,1,0:T(8,128)S(1)}, f32[4,32,256]{2,1,0:T(8,128)S(1)}, u32[]{:S(2)}, u32[]{:S(2)}) collective-permute-start(f32[4,32,256]{2,1,0:T(8,128)S(1)} %pad_maximum_fusion.mine_ref), channel_id=1, source_target_pairs={{0,32},{1,33},{2,34},{3,35},{4,36},{5,37},{6,38},{7,39},{8,40},{9,... | collective-permute-start | bytes 393224 | tf_op jit(solution)/shard_map/ppermute | solution.py:251
  82.0 0.6 copy-start.6

commit v2 on v1

--- a/solution.py
+++ b/solution.py
@@ -15,92 +15,124 @@
     return lax.dot_general(a, b, dims, preferred_element_type=jnp.float32)
 
 
-def grads_kernel(core_ref, len_ref, x_ref, w_hbm, cot_ref, keep_ref, send_ref,
-                 w_ref, slope_ref, act_ref, p_ref, s_ref, att_ref, da_ref, g_ref, sems):
+def grads_kernel(core_ref, len_ref, x_hbm, w_hbm, cot_hbm, keep_ref, send_ref,
+                 x_ref, w_ref, cot_ref, slope_ref, act_ref, mask_ref, p_ref, s_ref, ds_ref,
+                 att_ref, da_ref, g_ref, sems):
     rows, width = cot_ref.shape
     nblocks = rows // BLOCK
     size = width // HEADS
     half = width // 2
     scale = size ** -0.5
-    order = (2, 3, 1, 0)
-    copies = {}
-    for s in order:
-        cols = pl.ds(s * width, width)
-        copies[s] = pltpu.make_async_copy(w_hbm.at[:, cols], w_ref.at[:, cols], sems.at[s])
-        copies[s].start()
-    for s in order:
-        copies[s].wait()
-        for i in range(2):
-            r = pl.ds(i * (rows // 2), rows // 2)
-            cols = pl.ds(s * width, width)
-            h = mm(x_ref[r, :], w_ref[:, cols])
-            sig = 0.5 * jnp.tanh(0.5 * h) + 0.5
-            act = h * sig
-            act_ref[r, cols] = act.astype(jnp.bfloat16)
-            slope_ref[r, cols] = sig + act * (1.0 - sig)
-
-    def col(s, h):
-        return pl.ds(s * width + h * size, size)
-
-    core = core_ref[0]
-
-    def put(s, h, r, grad):
-        value = grad.astype(jnp.bfloat16).astype(jnp.float32) * slope_ref[r, col(s, h)]
-        to = s * half + (h % (HEADS // 2)) * size
-        g_ref[(h // (HEADS // 2)) ^ core, r, pl.ds(to, size)] = value.astype(jnp.bfloat16)
+    bf16 = jnp.bfloat16
+
+    def section(s):
+        return pl.ds(s * width, width)
+
+    loads = {s: pltpu.make_async_copy(w_hbm.at[:, section(s)], w_ref.at[:, section(s)], sems.at[s])
+             for s in range(4)}
+    load_x = pltpu.make_async_copy(x_hbm, x_ref, sems.at[4])
+    load_cot = pltpu.make_async_copy(cot_hbm, cot_ref, sems.at[5])
+    load_x.start()
+    loads[2].start()
+    loads[3].start()
 
     l0 = len_ref[0]
     l1 = len_ref[1]
     start1 = ((l0 + (BLOCK - 1)) // BLOCK) * BLOCK
-    for i in range(nblocks):
+
+    def spans(i):
         first = max(0, i - 2)
-        span = i + 1 - first
-        r = pl.ds(i * BLOCK, BLOCK)
-        keys = pl.ds(first * BLOCK, span * BLOCK)
+        return pl.ds(i * BLOCK, BLOCK), pl.ds(first * BLOCK, (i + 1 - first) * BLOCK), first
+
+    def row_facts(i):
         row = i * BLOCK + lax.broadcasted_iota(jnp.int32, (BLOCK, 1), 0)
         in0 = row < l0
         in1 = (row >= start1) & (row < start1 + l1)
+        return row, in0, in1
+
+    for i in range(nblocks):
+        r, keys, first = spans(i)
+        row, in0, in1 = row_facts(i)
         low = jnp.where(in1, start1, 0)
         high = jnp.where(in0 | in1, row, -1)
         count = jnp.where(in0, l0, jnp.where(in1, l1, 1))
         inv = 1.0 / count.astype(jnp.float32)
-        live = in0 | in1
-        c = first * BLOCK + lax.broadcasted_iota(jnp.int32, (BLOCK, span * BLOCK), 1)
-        valid = (c >= low) & (c <= high)
-        for h in range(HEADS):
-            t = mm(act_ref[r, col(2, h)], act_ref[keys, col(3, h)], NT)
-            sig = 0.5 * jnp.tanh(t * (0.5 * scale)) + 0.5
-            p = t * scale * sig
-            p_b = jnp.where(valid, p, 0.0).astype(jnp.bfloat16)
-            p_ref[h, r, keys] = p_b
-            s_ref[h, r, keys] = jnp.where(valid, sig + p * (1.0 - sig), 0.0)
-            att_ref[r, pl.ds(h * size, size)] = mm(p_b, act_ref[keys, col(1, h)]) * inv
+        c = first * BLOCK + lax.broadcasted_iota(jnp.int32, (BLOCK, keys.size), 1)
+        mask_ref[r, keys] = jnp.where((c >= low) & (c <= high), inv, 0.0)
+
+    def project(s):
+        loads[s].wait()
+        h = mm(x_ref[...], w_ref[:, section(s)])
+        sig = 0.5 * jnp.tanh(0.5 * h) + 0.5
+        act = h * sig
+        act_ref[:, section(s)] = act.astype(bf16)
+        slope_ref[:, section(s)] = sig + act * (1.0 - sig)
+
+    def col(s, h):
+        return pl.ds(s * width + h * size, size)
+
+    def head(h):
+        return pl.ds(h * size, size)
+
+    core = core_ref[0]
+
+    def put(s, h, r, grad):
+        value = grad.astype(bf16).astype(jnp.float32) * slope_ref[r, col(s, h)]
+        to = s * half + (h % (HEADS // 2)) * size
+        g_ref[(h // (HEADS // 2)) ^ core, r, pl.ds(to, size)] = value.astype(bf16)
+
+    load_x.wait()
+    loads[1].start()
+    project(2)
+    loads[0].start()
+    load_cot.start()
+    project(3)
+    for i in range(nblocks):
+        r, keys, _ = spans(i)
+        for h in range(HEADS):
+            t = mm(act_ref[r, col(2, h)], act_ref[keys, col(3, h)], NT) * scale
+            sig = 0.5 * jnp.tanh(0.5 * t) + 0.5
+            p = t * sig
+            p_ref[h, r, keys] = (p * mask_ref[r, keys]).astype(bf16)
+            s_ref[h, r, keys] = (sig + p * (1.0 - sig)) * mask_ref[r, keys]
+    project(1)
+    for i in range(nblocks):
+        r, keys, _ = spans(i)
+        for h in range(HEADS):
+            att_ref[r, head(h)] = mm(p_ref[h, r, keys], act_ref[keys, col(1, h)])
+    project(0)
+    load_cot.wait()
+    for i in range(nblocks):
+        r, _, _ = spans(i)
+        _, in0, in1 = row_facts(i)
         att = att_ref[r, :]
         cen = att - jnp.mean(att, axis=1, keepdims=True)
         rstd = lax.rsqrt(jnp.mean(cen * cen, axis=1, keepdims=True) + 1e-05)
         z = cen * rstd
-        up = jnp.where(live, cot_ref[r, :].astype(jnp.float32), 0.0)
-        du = up * z
-        dz = up * act_ref[r, pl.ds(0, width)].astype(jnp.float32)
+        up = jnp.where(in0 | in1, cot_ref[r, :].astype(jnp.float32), 0.0)
+        dz = up * act_ref[r, section(0)].astype(jnp.float32)
         m1 = jnp.mean(dz, axis=1, keepdims=True)
         m2 = jnp.mean(dz * z, axis=1, keepdims=True)
-        da = (dz - m1 - z * m2) * (rstd * inv)
-        da_ref[r, :] = da.astype(jnp.bfloat16)
+        da_ref[r, :] = ((dz - m1 - z * m2) * rstd).astype(bf16)
+        du = up * z
         for h in range(HEADS):
             put(0, h, r, du[:, h * size:(h + 1) * size])
-        for h in range(HEADS):
-            dp = mm(da_ref[r, pl.ds(h * size, size)], act_ref[keys, col(1, h)], NT)
-            ds = (dp * s_ref[h, r, keys]).astype(jnp.bfloat16)
-            s_ref[h, r, keys] = ds.astype(jnp.float32)
-            put(2, h, r, mm(ds, act_ref[keys, col(3, h)]) * scale)
+    for i in range(nblocks):
+        r, keys, _ = spans(i)
+        for h in range(HEADS):
+            dp = mm(da_ref[r, head(h)], act_ref[keys, col(1, h)], NT)
+            ds_ref[h, r, keys] = (dp * s_ref[h, r, keys]).astype(bf16)
+    for i in range(nblocks):
+        r, keys, _ = spans(i)
+        for h in range(HEADS):
+            put(2, h, r, mm(ds_ref[h, r, keys], act_ref[keys, col(3, h)]) * scale)
     for j in range(nblocks):
         last = min(nblocks, j + 3)
         r = pl.ds(j * BLOCK, BLOCK)
         qs = pl.ds(j * BLOCK, (last - j) * BLOCK)
         for h in range(HEADS):
-            put(1, h, r, mm(p_ref[h, qs, r], da_ref[qs, pl.ds(h * size, size)], TN))
-            ds = s_ref[h, qs, r].astype(jnp.bfloat16)
-            put(3, h, r, mm(ds, act_ref[qs, col(2, h)], TN) * scale)
+            put(1, h, r, mm(p_ref[h, qs, r], da_ref[qs, head(h)], TN))
+            put(3, h, r, mm(ds_ref[h, qs, r], act_ref[qs, col(2, h)], TN) * scale)
     keep_ref[...] = g_ref[0]
     send_ref[...] = g_ref[1]
 
@@ -111,23 +143,28 @@
     wide = w.shape[1]
     vmem = pl.BlockSpec(memory_space=pltpu.VMEM)
     smem = pl.BlockSpec(memory_space=pltpu.SMEM)
+    hbm = pl.BlockSpec(memory_space=pl.ANY)
     return pl.pallas_call(
         grads_kernel,
         out_shape=[jax.ShapeDtypeStruct((rows, wide // 2), jnp.bfloat16)] * 2,
-        in_specs=[smem, smem, vmem, pl.BlockSpec(memory_space=pl.ANY), vmem],
+        in_specs=[smem, smem, hbm, hbm, hbm],
         out_specs=[vmem, vmem],
         scratch_shapes=[
+            pltpu.VMEM((rows, d), jnp.bfloat16),
             pltpu.VMEM((d, wide), jnp.bfloat16),
+            pltpu.VMEM((rows, width), jnp.bfloat16),
             pltpu.VMEM((rows, wide), jnp.float32),
             pltpu.VMEM((rows, wide), jnp.bfloat16),
+            pltpu.VMEM((rows, rows), jnp.float32),
             pltpu.VMEM((HEADS, rows, rows), jnp.bfloat16),
             pltpu.VMEM((HEADS, rows, rows), jnp.float32),
+            pltpu.VMEM((HEADS, rows, rows), jnp.bfloat16),
             pltpu.VMEM((rows, width), jnp.float32),
             pltpu.VMEM((rows, width), jnp.bfloat16),
             pltpu.VMEM((2, rows, wide // 2), jnp.bfloat16),
-            pltpu.SemaphoreType.DMA((4,)),
+            pltpu.SemaphoreType.DMA((6,)),
         ],
-        compiler_params=pltpu.CompilerParams(vmem_limit_bytes=40 * 2**20),
+        compiler_params=pltpu.CompilerParams(vmem_limit_bytes=60 * 2**20),
         cost_estimate=pl.CostEstimate(flops=4 * 10**9, bytes_accessed=8 * 10**6, transcendentals=2 * 10**6),
         name="uvqk_grads",
     )(core, lengths, x, w, cot)
@@ -211,25 +248,26 @@
     )(core, keep, send, w)
 
 
-def place_kernel(where_ref, mine_ref, other_ref, out_ref):
+def place_kernel(where_ref, p0, p1, p2, p3, out_ref):
     core, y = where_ref[0], where_ref[3]
-    for i, ref in enumerate((mine_ref, other_ref)):
-        for k in range(4):
-            s = lax.rem(y + 4 - k, 4)
+    for k, ref in enumerate((p0, p1, p2, p3)):
+        s = lax.rem(y + 4 - k, 4)
+        for i in range(2):
             cols = pl.ds(pl.multiple_of(s * 512 + (core ^ i) * 256, 256), 256)
-            out_ref[:, cols] = ref[k]
-
-
-def place(where, mine, other):
+            out_ref[:, cols] = ref[i]
+
+
+def place(where, parts):
     vmem = pl.BlockSpec(memory_space=pltpu.VMEM)
     smem = pl.BlockSpec(memory_space=pltpu.SMEM)
     return pl.pallas_call(
         place_kernel,
-        out_shape=jax.ShapeDtypeStruct((mine.shape[1], 2048), jnp.float32),
-        in_specs=[smem, vmem, vmem],
+        out_shape=jax.ShapeDtypeStruct((parts[0].shape[1], 2048), jnp.float32),
+        in_specs=[smem] + [vmem] * 4,
         out_specs=vmem,
+        compiler_params=pltpu.CompilerParams(vmem_limit_bytes=4 * 2**20),
         name="place_columns",
-    )(where, mine, other)
+    )(where, *parts)
 
 
 AXES = ("group", "member")
@@ -289,6 +327,7 @@
     parts = weights(where, xt, keep, recv)
     moved = [permute(parts[k], first_axis(k)) for k in (1, 2, 3)]
     grad_rows = row_grads(where, keep, send, w_in)
+    *moved, grad_rows = lax.optimization_barrier((*moved, grad_rows))
     summed = [f32(parts[0][l]) + f32(moved[0][l]) + f32(moved[1][l]) + f32(moved[2][l]) for l in range(4)]
     moved = [permute(summed[k].astype(jnp.bfloat16), second_axis(k)) for k in (1, 2, 3)]
     block = summed[0] + f32(moved[0]) + f32(moved[1]) + f32(moved[2])
@@ -298,8 +337,8 @@
     block = lax.all_to_all(block, "member", 0, 0, tiled=True, axis_index_groups=nz)
     block = jnp.sum(f32(block), axis=0)
 
-    gathered = jnp.stack([block] + [permute(block, along_y(k)) for k in (1, 2, 3)])
-    grad_w = place(where, gathered, permute(gathered, other_core))
+    both = jnp.stack([block, permute(block, other_core)])
+    grad_w = place(where, [both] + [permute(both, along_y(k)) for k in (1, 2, 3)])
     return (grad_rows, grad_w)
 
 

time: 84.6 us -> 75.3 us (0.89)
  local copies, waits for them, and re-layouts: 5.76 us -> 0.02 us
  starting transfers between devices: 18 us -> 16.2 us
  waiting for transfers between devices: 23.3 us -> 21.8 us
  Pallas kernels: 21.3 us -> 20.3 us
    unnamed x14 -> x10, local copies, waits for them, and re-layouts: 5.76 us -> 0.02 us
    ppermute x12, starting transfers between devices: 18 us -> 16.2 us  [permute(): return lax.ppermute(value, AXES, pairs(move))]
    ppermute x12, waiting for transfers between devices: 23.3 us -> 21.8 us  [permute(): return lax.ppermute(value, AXES, pairs(move))]
  transfers between devices with their start and end apart: 12 -> 12, of which waited for: 8 -> 10; matrix products, arithmetic and copies ran while one was open for 0% -> 1% of each run, Pallas kernels for 20% -> 21%
where the time goes in v2:
time: 75.3 us; the launch traced here: 74.8 us
  waiting for transfers between devices  21.8 us (29%)
  Pallas kernels  20.3 us (27%)
  starting transfers between devices  16.2 us (22%)
  blocking collectives  14.8 us (20%)
  other arithmetic  1.01 us (1%)
    ppermute x12, waiting for transfers between devices, permute(): return lax.ppermute(value, AXES, pairs(move))  21.8 us
    ppermute x12, starting transfers between devices, permute(): return lax.ppermute(value, AXES, pairs(move))  16.2 us
    all_to_all x1, blocking collectives, shards(): lax.all_to_all(block, 'member', 0, 0, tiled=True, axis_index_groups=nz)  14.8 us
    pallas_call x1, Pallas kernels, grads(): pl.pallas_call(grads_kernel, out_shape=[jax.ShapeDtypeStruct((rows, wide...  11.5 us
    pallas_call x1, Pallas kernels, row_grads(): pl.pallas_call(rows_kernel, out_shape=jax.ShapeDtypeStruct((keep.shape[0]...  3.89 us
    pallas_call x1, Pallas kernels, weights(): pl.pallas_call(weights_kernel, out_shape=[jax.ShapeDtypeStruct((4, 256, 2...  2.96 us
  transfers between devices with their start and end apart: 12, of which 10 were waited for; matrix products, arithmetic and copies ran while one was open for 1% of the time, Pallas kernels for 21%

profile of v2, /device:TPU:1, one launch (start us, length us, event | category | flops | bytes accessed | tf_op | source)
XLA Modules:
  0.0 74.8 jit_solution(9694802958986956322)
XLA Ops:
  0.6 3.3 %collective-permute-start = (bf16[512,1024]{1,0:T(8,128)(2,1)}, bf16[512,1024]{1,0:T(8,128)(2,1)S(1)}, u32[]{:S(2)}, u32[]{:S(2)}) collective-permute-start(bf16[512,1024]{1,0:T(8,128)(2,1)} %x_hbm.1), channel_id=1, source_target_pairs={{0,32},{1,33},{2,34},{3,35},{4,36},{5,37},{6,38},{7,39},{8,40},{9,... | collective-permute-start | bytes 3145736 | tf_op jit(solution)/shard_map/ppermute | solution.py:289
  4.0 0.7 pad_add_fusion.core_ref.where_ref
  4.6 11.5 %uvqk_grads.1 = (bf16[512,1024]{1,0:T(8,128)(2,1)}, bf16[512,1024]{1,0:T(8,128)(2,1)}) custom-call(s32[4]{0:T(128)} %pad_add_fusion.core_ref.where_ref, s32[2]{0:T(128)} %len_ref.1, bf16[512,1024]{1,0:T(8,128)(2,1)} %x_hbm.1, bf16[1024,2048]{1,0:T(8,128)(2,1)} %w_ref.1, bf16[512,512]{1,0:T(8,128)(2,1)} %cot_hbm.1), custom_call_target="tpu_custom_call" | custom-call | flops 4000000000 | bytes 8000000 | tf_op jit(solution)/shard_map/uvqk_grads/pallas_call | solution.py:147
  16.2 0.1 collective-permute-start.1
  16.3 0.6 transpose_rows.1.xt_ref
  16.9 0.0 copy-start.2
  17.0 2.2 %collective-permute-done.1.recv_ref = bf16[512,1024]{1,0:T(8,128)(2,1)S(1)} collective-permute-done((bf16[512,1024]{1,0:T(8,128)(2,1)}, bf16[512,1024]{1,0:T(8,128)(2,1)S(1)}, u32[]{:S(2)}, u32[]{:S(2)}) %collective-permute-start.1) | collective-permute-done | bytes 1048608 | tf_op jit(solution)/shard_map/ppermute | solution.py:289
  19.1 3.0 %weight_grads.1 = (bf16[4,256,256]{2,1,0:T(8,128)(2,1)S(1)}, bf16[4,256,256]{2,1,0:T(8,128)(2,1)S(1)}, bf16[4,256,256]{2,1,0:T(8,128)(2,1)S(1)}, bf16[4,256,256]{2,1,0:T(8,128)(2,1)S(1)}) custom-call(s32[4]{0:T(128)S(1)} %copy-done.1, bf16[1024,1024]{1,0:T(8,128)(2,1)S(1)} %transpose_rows.1.xt_ref, bf16[512,1024]{1,0:T(8,128)(2,1)S(1)} %copy-done.4, ...), custom_call_target="tpu_custom_call" | custom-call | flops 2147483648 | bytes 6291456 | tf_op jit(solution)/shard_map/weight_grads/pallas_call | solution.py:214
  22.1 0.1 collective-permute-start.2
  22.2 2.2 %collective-permute-start.3 = (bf16[4,256,256]{2,1,0:T(8,128)(2,1)S(1)}, bf16[4,256,256]{2,1,0:T(8,128)(2,1)S(1)}, u32[]{:S(2)}, u32[]{:S(2)}) collective-permute-start(bf16[4,256,256]{2,1,0:T(8,128)(2,1)S(1)} %get-tuple-element.15), channel_id=1, source_target_pairs={{0,16},{1,17},{2,18},{3,19},{4,20},{5,21},{6,22},{7,23},{8,24},{9,... | collective-permute-start | bytes 1572872 | tf_op jit(solution)/shard_map/ppermute | solution.py:289
  24.4 1.1 %collective-permute-start.4 = (bf16[4,256,256]{2,1,0:T(8,128)(2,1)S(1)}, bf16[4,256,256]{2,1,0:T(8,128)(2,1)S(1)}, u32[]{:S(2)}, u32[]{:S(2)}) collective-permute-start(bf16[4,256,256]{2,1,0:T(8,128)(2,1)S(1)} %get-tuple-element.16), channel_id=1, source_target_pairs={{0,24},{1,25},{2,26},{3,27},{4,28},{5,29},{6,30},{7,31},{8,0},{9,1... | collective-permute-start | bytes 1572872 | tf_op jit(solution)/shard_map/ppermute | solution.py:289
  25.4 3.9 %row_grads.1 = bf16[512,1024]{1,0:T(8,128)(2,1)} custom-call(s32[4]{0:T(128)S(1)} %copy-done.1, bf16[512,1024]{1,0:T(8,128)(2,1)S(1)} %copy-done.4, bf16[512,1024]{1,0:T(8,128)(2,1)S(1)} %copy-done.3, bf16[1024,2048]{1,0:T(8,128)(2,1)S(1)} %copy-done.2), custom_call_target="tpu_custom_call" | custom-call | flops 2147483648 | bytes 7340032 | tf_op jit(solution)/shard_map/row_grads/pallas_call | solution.py:240
  29.3 8.0 %collective-permute-done.2 = bf16[4,256,256]{2,1,0:T(8,128)(2,1)S(1)} collective-permute-done((bf16[4,256,256]{2,1,0:T(8,128)(2,1)S(1)}, bf16[4,256,256]{2,1,0:T(8,128)(2,1)S(1)}, u32[]{:S(2)}, u32[]{:S(2)}) %collective-permute-start.2) | collective-permute-done | bytes 524320 | tf_op jit(solution)/shard_map/ppermute | solution.py:289
  37.3 0.6 collective-permute-done.4
  38.0 0.2 fusion.3
  38.2 0.1 collective-permute-start.5
  38.3 2.7 %collective-permute-start.7 = (bf16[256,256]{1,0:T(8,128)(2,1)S(1)}, bf16[256,256]{1,0:T(8,128)(2,1)S(1)}, u32[]{:S(2)}, u32[]{:S(2)}) collective-permute-start(bf16[256,256]{1,0:T(8,128)(2,1)S(1)} %get-tuple-element.23), channel_id=1, source_target_pairs={{0,192},{1,193},{2,194},{3,195},{4,196},{5,197},{6,198},{7,199},{8... | collective-permute-start | bytes 393224 | tf_op jit(solution)/shard_map/ppermute | solution.py:289
  40.9 0.1 collective-permute-start.6
  41.1 2.2 %collective-permute-done.5 = bf16[256,256]{1,0:T(8,128)(2,1)S(1)} collective-permute-done((bf16[256,256]{1,0:T(8,128)(2,1)S(1)}, bf16[256,256]{1,0:T(8,128)(2,1)S(1)}, u32[]{:S(2)}, u32[]{:S(2)}) %collective-permute-start.5) | collective-permute-done | bytes 131104 | tf_op jit(solution)/shard_map/ppermute | solution.py:289
  43.3 1.0 %collective-permute-done.7 = bf16[256,256]{1,0:T(8,128)(2,1)S(1)} collective-permute-done((bf16[256,256]{1,0:T(8,128)(2,1)S(1)}, bf16[256,256]{1,0:T(8,128)(2,1)S(1)}, u32[]{:S(2)}, u32[]{:S(2)}) %collective-permute-start.7) | collective-permute-done | bytes 131104 | tf_op jit(solution)/shard_map/ppermute | solution.py:289
  44.2 2.0 %collective-permute-done.6 = bf16[256,256]{1,0:T(8,128)(2,1)S(1)} collective-permute-done((bf16[256,256]{1,0:T(8,128)(2,1)S(1)}, bf16[256,256]{1,0:T(8,128)(2,1)S(1)}, u32[]{:S(2)}, u32[]{:S(2)}) %collective-permute-start.6) | collective-permute-done | bytes 131104 | tf_op jit(solution)/shard_map/ppermute | solution.py:289
  46.2 0.1 fusion.2
  46.4 14.8 %all_to_all.5 = bf16[8,32,256]{2,1,0:T(8,128)(2,1)S(1)} all-to-all(bf16[8,32,256]{2,1,0:T(8,128)(2,1)S(1)} %bitcast.21), channel_id=1, replica_groups={{0,1,2,3,4,5,6,7},{8,9,10,11,12,13,14,15},{16,17,18,19,20,21,22,23},{24..., dimensions={0} | all-to-all | bytes 262144 | tf_op jit(solution)/shard_map/all_to_all | solution.py:337
  61.2 4.0 %collective-permute-start.8 = (f32[32,256]{1,0:T(8,128)S(1)}, f32[32,256]{1,0:T(8,128)S(1)}, u32[]{:S(2)}, u32[]{:S(2)}) collective-permute-start(f32[32,256]{1,0:T(8,128)S(1)} %convert_reduce_fusion), channel_id=1, source_target_pairs={{0,32},{1,33},{2,34},{3,35},{4,36},{5,37},{6,38},{7,39},{8,40},{9,... | collective-permute-start | bytes 98312 | tf_op jit(solution)/shard_map/ppermute | solution.py:289
  65.2 0.9 %collective-permute-done.8 = f32[32,256]{1,0:T(8,128)S(1)} collective-permute-done((f32[32,256]{1,0:T(8,128)S(1)}, f32[32,256]{1,0:T(8,128)S(1)}, u32[]{:S(2)}, u32[]{:S(2)}) %collective-permute-start.8) | collective-permute-done | bytes 32800 | tf_op jit(solution)/shard_map/ppermute | solution.py:289
  66.0 1.5 %collective-permute-start.11 = (f32[2,32,256]{2,1,0:T(8,128)S(1)}, f32[2,32,256]{2,1,0:T(8,128)S(1)}, u32[]{:S(2)}, u32[]{:S(2)}) collective-permute-start(f32[2,32,256]{2,1,0:T(8,128)S(1)} %pad_maximum_fusion.p0), channel_id=1, source_target_pairs={{0,192},{1,193},{2,194},{3,195},{4,196},{5,197},{6,198},{7,199},{8... | collective-permute-start | bytes 196616 | tf_op jit(solution)/shard_map/ppermute | solution.py:289
  67.5 0.5 collective-permute-start.10
  68.1 0.5 collective-permute-start.9
  68.6 0.6 collective-permute-done.11.p3
  69.1 3.1 %collective-permute-done.10.p2 = f32[2,32,256]{2,1,0:T(8,128)S(1)} collective-permute-done((f32[2,32,256]{2,1,0:T(8,128)S(1)}, f32[2,32,256]{2,1,0:T(8,128)S(1)}, u32[]{:S(2)}, u32[]{:S(2)}) %collective-permute-start.10) | collective-permute-done | bytes 65568 | tf_op jit(solution)/shard_map/ppermute | solution.py:289
  72.2 1.3 %collective-permute-done.9.p1 = f32[2,32,256]{2,1,0:T(8,128)S(1)} collective-permute-done((f32[2,32,256]{2,1,0:T(8,128)S(1)}, f32[2,32,256]{2,1,0:T(8,128)S(1)}, u32[]{:S(2)}, u32[]{:S(2)}) %collective-permute-start.9) | collective-permute-done | bytes 65568 | tf_op jit(solution)/shard_map/ppermute | solution.py:289
  73.5 1.3 %place_columns.1 = f32[32,2048]{1,0:T(8,128)} custom-call(s32[4]{0:T(128)S(1)} %copy-done.1, f32[2,32,256]{2,1,0:T(8,128)S(1)} %pad_maximum_fusion.p0, f32[2,32,256]{2,1,0:T(8,128)S(1)} %collective-permute-done.9.p1, f32[2,32,256]{2,1,0:T(8,128)S(1)} %collective-permute-done.10.p2, f32[2,32,256]{2,1,0:T(8,128)S(1)} %collective-permute-done.11.p3), custom_call_target="tpu_custom_call" | custom-call | tf_op jit(solution)/shard_map/place_columns/pallas_call | solution.py:263
  (13 shorter events, 0.1 us)
Async XLA Ops:
  0.6 15.7 %collective-permute-start = (bf16[512,1024]{1,0:T(8,128)(2,1)}, bf16[512,1024]{1,0:T(8,128)(2,1)S(1)}, u32[]{:S(2)}, u32[]{:S(2)}) collective-permute-start(bf16[512,1024]{1,0:T(8,128)(2,1)} %x_hbm.1), channel_id=1, source_target_pairs={{0,32},{1,33},{2,34},{3,35},{4,36},{5,37},{6,38},{7,39},{8,40},{9,... | collective-permute-start | bytes 3145736 | tf_op jit(solution)/shard_map/ppermute | solution.py:289
  4.6 11.7 %copy-start = (bf16[512,1024]{1,0:T(8,128)(2,1)S(1)}, bf16[512,1024]{1,0:T(8,128)(2,1)}, u32[]{:S(2)}) copy-start(bf16[512,1024]{1,0:T(8,128)(2,1)} %x_hbm.1) | copy-start | bytes 3145732
  16.1 3.0 %copy-start.1 = (s32[4]{0:T(128)S(1)}, s32[4]{0:T(128)}, u32[]{:S(2)}) copy-start(s32[4]{0:T(128)} %pad_add_fusion.core_ref.where_ref) | copy-start | bytes 52
  16.2 3.0 %copy-start.4 = (bf16[512,1024]{1,0:T(8,128)(2,1)S(1)}, bf16[512,1024]{1,0:T(8,128)(2,1)}, u32[]{:S(2)}) copy-start(bf16[512,1024]{1,0:T(8,128)(2,1)} %get-tuple-element.12.keep_ref) | copy-start | bytes 3145732
  16.2 3.0 %collective-permute-start.1 = (bf16[512,1024]{1,0:T(8,128)(2,1)}, bf16[512,1024]{1,0:T(8,128)(2,1)S(1)}, u32[]{:S(2)}, u32[]{:S(2)}) collective-permute-start(bf16[512,1024]{1,0:T(8,128)(2,1)} %get-tuple-element.13.send_ref), channel_id=1, source_target_pairs={{0,32},{1,33},{2,34},{3,35},{4,36},{5,37},{6,38},{7,39},{8,40},{9,... | collective-permute-start | bytes 3145736 | tf_op jit(solution)/shard_map/ppermute | solution.py:289
  16.9 8.5 %copy-start.2 = (bf16[1024,2048]{1,0:T(8,128)(2,1)S(1)}, bf16[1024,2048]{1,0:T(8,128)(2,1)}, u32[]{:S(2)}) copy-start(bf16[1024,2048]{1,0:T(8,128)(2,1)} %w_ref.1) | copy-start | bytes 12582916
  17.0 8.5 %copy-start.3 = (bf16[512,1024]{1,0:T(8,128)(2,1)S(1)}, bf16[512,1024]{1,0:T(8,128)(2,1)}, u32[]{:S(2)}) copy-start(bf16[512,1024]{1,0:T(8,128)(2,1)} %get-tuple-element.13.send_ref) | copy-start | bytes 3145732
  22.1 15.2 %collective-permute-start.2 = (bf16[4,256,256]{2,1,0:T(8,128)(2,1)S(1)}, bf16[4,256,256]{2,1,0:T(8,128)(2,1)S(1)}, u32[]{:S(2)}, u32[]{:S(2)}) collective-permute-start(bf16[4,256,256]{2,1,0:T(8,128)(2,1)S(1)} %get-tuple-element.14), channel_id=1, source_target_pairs={{0,8},{1,9},{2,10},{3,11},{4,12},{5,13},{6,14},{7,15},{8,16},{9,17... | collective-permute-start | bytes 1572872 | tf_op jit(solution)/shard_map/ppermute | solution.py:289
  22.2 15.1 %collective-permute-start.3 = (bf16[4,256,256]{2,1,0:T(8,128)(2,1)S(1)}, bf16[4,256,256]{2,1,0:T(8,128)(2,1)S(1)}, u32[]{:S(2)}, u32[]{:S(2)}) collective-permute-start(bf16[4,256,256]{2,1,0:T(8,128)(2,1)S(1)} %get-tuple-element.15), channel_id=1, source_target_pairs={{0,16},{1,17},{2,18},{3,19},{4,20},{5,21},{6,22},{7,23},{8,24},{9,... | collective-permute-start | bytes 1572872 | tf_op jit(solution)/shard_map/ppermute | solution.py:289
  24.4 13.6 %collective-permute-start.4 = (bf16[4,256,256]{2,1,0:T(8,128)(2,1)S(1)}, bf16[4,256,256]{2,1,0:T(8,128)(2,1)S(1)}, u32[]{:S(2)}, u32[]{:S(2)}) collective-permute-start(bf16[4,256,256]{2,1,0:T(8,128)(2,1)S(1)} %get-tuple-element.16), channel_id=1, source_target_pairs={{0,24},{1,25},{2,26},{3,27},{4,28},{5,29},{6,30},{7,31},{8,0},{9,1... | collective-permute-start | bytes 1572872 | tf_op jit(solution)/shard_map/ppermute | solution.py:289
  38.2 5.1 %collective-permute-start.5 = (bf16[256,256]{1,0:T(8,128)(2,1)S(1)}, bf16[256,256]{1,0:T(8,128)(2,1)S(1)}, u32[]{:S(2)}, u32[]{:S(2)}) collective-permute-start(bf16[256,256]{1,0:T(8,128)(2,1)S(1)} %get-tuple-element.22), channel_id=1, source_target_pairs={{0,64},{1,65},{2,66},{3,67},{4,68},{5,69},{6,70},{7,71},{8,72},{9,... | collective-permute-start | bytes 393224 | tf_op jit(solution)/shard_map/ppermute | solution.py:289
  38.3 6.0 %collective-permute-start.7 = (bf16[256,256]{1,0:T(8,128)(2,1)S(1)}, bf16[256,256]{1,0:T(8,128)(2,1)S(1)}, u32[]{:S(2)}, u32[]{:S(2)}) collective-permute-start(bf16[256,256]{1,0:T(8,128)(2,1)S(1)} %get-tuple-element.23), channel_id=1, source_target_pairs={{0,192},{1,193},{2,194},{3,195},{4,196},{5,197},{6,198},{7,199},{8... | collective-permute-start | bytes 393224 | tf_op jit(solution)/shard_map/ppermute | solution.py:289
  40.9 5.3 %collective-permute-start.6 = (bf16[256,256]{1,0:T(8,128)(2,1)S(1)}, bf16[256,256]{1,0:T(8,128)(2,1)S(1)}, u32[]{:S(2)}, u32[]{:S(2)}) collective-permute-start(bf16[256,256]{1,0:T(8,128)(2,1)S(1)} %get-tuple-element.24), channel_id=1, source_target_pairs={{0,128},{1,129},{2,130},{3,131},{4,132},{5,133},{6,134},{7,135},{8... | collective-permute-start | bytes 393224 | tf_op jit(solution)/shard_map/ppermute | solution.py:289
  61.2 4.8 %collective-permute-start.8 = (f32[32,256]{1,0:T(8,128)S(1)}, f32[32,256]{1,0:T(8,128)S(1)}, u32[]{:S(2)}, u32[]{:S(2)}) collective-permute-start(f32[32,256]{1,0:T(8,128)S(1)} %convert_reduce_fusion), channel_id=1, source_target_pairs={{0,32},{1,33},{2,34},{3,35},{4,36},{5,37},{6,38},{7,39},{8,40},{9,... | collective-permute-start | bytes 98312 | tf_op jit(solution)/shard_map/ppermute | solution.py:289
  66.0 3.1 %collective-permute-start.11 = (f32[2,32,256]{2,1,0:T(8,128)S(1)}, f32[2,32,256]{2,1,0:T(8,128)S(1)}, u32[]{:S(2)}, u32[]{:S(2)}) collective-permute-start(f32[2,32,256]{2,1,0:T(8,128)S(1)} %pad_maximum_fusion.p0), channel_id=1, source_target_pairs={{0,192},{1,193},{2,194},{3,195},{4,196},{5,197},{6,198},{7,199},{8... | collective-permute-start | bytes 196616 | tf_op jit(solution)/shard_map/ppermute | solution.py:289
  67.5 4.7 %collective-permute-start.10 = (f32[2,32,256]{2,1,0:T(8,128)S(1)}, f32[2,32,256]{2,1,0:T(8,128)S(1)}, u32[]{:S(2)}, u32[]{:S(2)}) collective-permute-start(f32[2,32,256]{2,1,0:T(8,128)S(1)} %pad_maximum_fusion.p0), channel_id=1, source_target_pairs={{0,128},{1,129},{2,130},{3,131},{4,132},{5,133},{6,134},{7,135},{8... | collective-permute-start | bytes 196616 | tf_op jit(solution)/shard_map/ppermute | solution.py:289
  68.1 5.5 %collective-permute-start.9 = (f32[2,32,256]{2,1,0:T(8,128)S(1)}, f32[2,32,256]{2,1,0:T(8,128)S(1)}, u32[]{:S(2)}, u32[]{:S(2)}) collective-permute-start(f32[2,32,256]{2,1,0:T(8,128)S(1)} %pad_maximum_fusion.p0), channel_id=1, source_target_pairs={{0,64},{1,65},{2,66},{3,67},{4,68},{5,69},{6,70},{7,71},{8,72},{9,... | collective-permute-start | bytes 196616 | tf_op jit(solution)/shard_map/ppermute | solution.py:289

commit v3 on v2

--- a/solution.py
+++ b/solution.py
@@ -7,6 +7,8 @@
 
 HEADS = 4
 BLOCK = 128
+AXES = ("group", "member")
+NY, NX, NZ = 4, 4, 8
 NT = (((1,), (1,)), ((), ()))
 TN = (((0,), (0,)), ((), ()))
 
@@ -15,8 +17,13 @@
     return lax.dot_general(a, b, dims, preferred_element_type=jnp.float32)
 
 
-def grads_kernel(core_ref, len_ref, x_hbm, w_hbm, cot_hbm, keep_ref, send_ref,
-                 x_ref, w_ref, cot_ref, slope_ref, act_ref, mask_ref, p_ref, s_ref, ds_ref,
+def position():
+    group, member = lax.axis_index("group"), lax.axis_index("member")
+    return group // 2, group % 2, member // NZ, member % NZ
+
+
+def grads_kernel(len_hbm, x_hbm, w_hbm, cot_hbm, keep_ref, send_ref,
+                 len_ref, x_ref, w_ref, cot_ref, slope_ref, act_ref, mask_ref, p_ref, s_ref, ds_ref,
                  att_ref, da_ref, g_ref, sems):
     rows, width = cot_ref.shape
     nblocks = rows // BLOCK
@@ -32,9 +39,12 @@
              for s in range(4)}
     load_x = pltpu.make_async_copy(x_hbm, x_ref, sems.at[4])
     load_cot = pltpu.make_async_copy(cot_hbm, cot_ref, sems.at[5])
+    load_len = pltpu.make_async_copy(len_hbm, len_ref, sems.at[6])
+    load_len.start()
     load_x.start()
     loads[2].start()
     loads[3].start()
+    load_len.wait()
 
     l0 = len_ref[0]
     l1 = len_ref[1]
@@ -74,7 +84,7 @@
     def head(h):
         return pl.ds(h * size, size)
 
-    core = core_ref[0]
+    core = position()[1]
 
     def put(s, h, r, grad):
         value = grad.astype(bf16).astype(jnp.float32) * slope_ref[r, col(s, h)]
@@ -137,19 +147,19 @@
     send_ref[...] = g_ref[1]
 
 
-def grads(core, lengths, x, w, cot):
+def grads(lengths, x, w, cot):
     rows, d = x.shape
     width = cot.shape[1]
     wide = w.shape[1]
     vmem = pl.BlockSpec(memory_space=pltpu.VMEM)
-    smem = pl.BlockSpec(memory_space=pltpu.SMEM)
     hbm = pl.BlockSpec(memory_space=pl.ANY)
     return pl.pallas_call(
         grads_kernel,
-        out_shape=[jax.ShapeDtypeStruct((rows, wide // 2), jnp.bfloat16)] * 2,
-        in_specs=[smem, smem, hbm, hbm, hbm],
+        out_shape=[pltpu.VMEM((rows, wide // 2), jnp.bfloat16)] * 2,
+        in_specs=[hbm] * 4,
         out_specs=[vmem, vmem],
         scratch_shapes=[
+            pltpu.SMEM((2,), jnp.int32),
             pltpu.VMEM((rows, d), jnp.bfloat16),
             pltpu.VMEM((d, wide), jnp.bfloat16),
             pltpu.VMEM((rows, width), jnp.bfloat16),
@@ -162,68 +172,81 @@
             pltpu.VMEM((rows, width), jnp.float32),
             pltpu.VMEM((rows, width), jnp.bfloat16),
             pltpu.VMEM((2, rows, wide // 2), jnp.bfloat16),
-            pltpu.SemaphoreType.DMA((6,)),
+            pltpu.SemaphoreType.DMA((7,)),
         ],
-        compiler_params=pltpu.CompilerParams(vmem_limit_bytes=60 * 2**20),
+        compiler_params=pltpu.CompilerParams(vmem_limit_bytes=40 * 2**20),
         cost_estimate=pl.CostEstimate(flops=4 * 10**9, bytes_accessed=8 * 10**6, transcendentals=2 * 10**6),
         name="uvqk_grads",
-    )(core, lengths, x, w, cot)
-
-
-def transpose_kernel(x_ref, y_ref, xt_ref):
-    rows, d = x_ref.shape
-    for i, ref in enumerate((x_ref, y_ref)):
-        for b in range(0, d, 256):
-            for r in range(0, rows, 256):
-                xt_ref[pl.ds(b, 256), pl.ds(i * rows + r, 256)] = ref[pl.ds(r, 256), pl.ds(b, 256)].T
-
-
-def transposed(x, y):
-    rows, d = x.shape
-    vmem = pl.BlockSpec(memory_space=pltpu.VMEM)
-    return pl.pallas_call(
-        transpose_kernel,
-        out_shape=jax.ShapeDtypeStruct((d, 2 * rows), jnp.bfloat16),
-        in_specs=[vmem, vmem],
-        out_specs=vmem,
-        compiler_params=pltpu.CompilerParams(vmem_limit_bytes=16 * 2**20),
-        cost_estimate=pl.CostEstimate(flops=0, bytes_accessed=4 * 2**20, transcendentals=0),
-        name="transpose_rows",
-    )(x, y)
-
-
-def weights_kernel(where_ref, xt_ref, keep_ref, recv_ref, o0, o1, o2, o3):
-    core, first, second = where_ref[0], where_ref[1], where_ref[2]
-    rows = keep_ref.shape[0]
-    for k, out in enumerate((o0, o1, o2, o3)):
+    )(*[pltpu.with_memory_space_constraint(v, pltpu.HBM) for v in (lengths, x, w, cot)])
+
+
+def flip(ref, out_ref):
+    rows, d = ref.shape
+    z = position()[3]
+    for b in range(0, d, 256):
+        for r in range(0, rows, 256):
+            block = ref[pl.ds(r, 256), pl.ds(b, 256)].T
+            for j in range(NZ):
+                at = pl.multiple_of(b + (j ^ z) * 32, 32)
+                out_ref[pl.ds(at, 32), pl.ds(r, 256)] = block[j * 32:(j + 1) * 32]
+
+
+def blocks_of():
+    y, core, x, _ = position()
+    first = jnp.where(core == 0, x, y)
+    second = jnp.where(core == 0, y, x)
+    for k in range(4):
         for l in range(4):
-            a = lax.rem(first + k, 4)
-            b = lax.rem(second + l, 4)
+            a = first ^ k
+            b = second ^ l
             rb = jnp.where(core == 0, a, b)
             cb = jnp.where(core == 0, b, a)
-            rs = pl.ds(pl.multiple_of(rb * 256, 256), 256)
-            cs = pl.ds(pl.multiple_of(cb * 256, 256), 256)
-            total = mm(xt_ref[rs, pl.ds(0, rows)], keep_ref[:, cs])
-            total += mm(xt_ref[rs, pl.ds(rows, rows)], recv_ref[:, cs])
-            out[l] = total.astype(jnp.bfloat16)
-
-
-def weights(where, xt, keep, recv):
-    vmem = pl.BlockSpec(memory_space=pltpu.VMEM)
-    smem = pl.BlockSpec(memory_space=pltpu.SMEM)
-    return pl.pallas_call(
-        weights_kernel,
+            yield k, l, pl.ds(pl.multiple_of(rb * 256, 256), 256), pl.ds(pl.multiple_of(cb * 256, 256), 256)
+
+
+def own_kernel(x_ref, theirs_ref, keep_ref, acc_ref, xt_ref, own_ref):
+    flip(x_ref, own_ref)
+    for k, l, rs, cs in blocks_of():
+        acc_ref[k, l] = mm(own_ref[rs, :], keep_ref[:, cs])
+    flip(theirs_ref, xt_ref)
+
+
+def own_part(x, theirs, keep):
+    rows, d = x.shape
+    vmem = pl.BlockSpec(memory_space=pltpu.VMEM)
+    return pl.pallas_call(
+        own_kernel,
+        out_shape=[jax.ShapeDtypeStruct((4, 4, 256, 256), jnp.float32), jax.ShapeDtypeStruct((d, rows), jnp.bfloat16)],
+        in_specs=[vmem] * 3,
+        out_specs=[vmem, vmem],
+        scratch_shapes=[pltpu.VMEM((d, rows), jnp.bfloat16)],
+        compiler_params=pltpu.CompilerParams(vmem_limit_bytes=24 * 2**20),
+        cost_estimate=pl.CostEstimate(flops=2**30, bytes_accessed=6 * 2**20, transcendentals=0),
+        name="own_weight_grads",
+    )(x, theirs, keep)
+
+
+def pair_kernel(acc_ref, xt_ref, recv_ref, o0, o1, o2, o3):
+    outs = (o0, o1, o2, o3)
+    for k, l, rs, cs in blocks_of():
+        outs[k][l] = (acc_ref[k, l] + mm(xt_ref[rs, :], recv_ref[:, cs])).astype(jnp.bfloat16)
+
+
+def pair_part(acc, xt, recv):
+    vmem = pl.BlockSpec(memory_space=pltpu.VMEM)
+    return pl.pallas_call(
+        pair_kernel,
         out_shape=[jax.ShapeDtypeStruct((4, 256, 256), jnp.bfloat16)] * 4,
-        in_specs=[smem, vmem, vmem, vmem],
+        in_specs=[vmem] * 3,
         out_specs=[vmem] * 4,
         compiler_params=pltpu.CompilerParams(vmem_limit_bytes=24 * 2**20),
-        cost_estimate=pl.CostEstimate(flops=2 * 2**30, bytes_accessed=6 * 2**20, transcendentals=0),
-        name="weight_grads",
-    )(where, xt, keep, recv)
-
-
-def rows_kernel(core_ref, keep_ref, send_ref, w_ref, out_ref):
-    core = core_ref[0]
+        cost_estimate=pl.CostEstimate(flops=2**30, bytes_accessed=6 * 2**20, transcendentals=0),
+        name="pair_weight_grads",
+    )(acc, xt, recv)
+
+
+def rows_kernel(keep_ref, send_ref, w_ref, out_ref):
+    core = position()[1]
     rows = keep_ref.shape[0]
     for r in range(0, rows, 256):
         total = jnp.zeros((256, w_ref.shape[0]), jnp.float32)
@@ -234,44 +257,38 @@
         out_ref[pl.ds(r, 256), :] = total.astype(jnp.bfloat16)
 
 
-def row_grads(core, keep, send, w):
-    vmem = pl.BlockSpec(memory_space=pltpu.VMEM)
-    smem = pl.BlockSpec(memory_space=pltpu.SMEM)
+def row_grads(keep, send, w):
+    vmem = pl.BlockSpec(memory_space=pltpu.VMEM)
     return pl.pallas_call(
         rows_kernel,
         out_shape=jax.ShapeDtypeStruct((keep.shape[0], w.shape[0]), jnp.bfloat16),
-        in_specs=[smem, vmem, vmem, vmem],
+        in_specs=[vmem] * 3,
         out_specs=vmem,
         compiler_params=pltpu.CompilerParams(vmem_limit_bytes=24 * 2**20),
         cost_estimate=pl.CostEstimate(flops=2 * 2**30, bytes_accessed=7 * 2**20, transcendentals=0),
         name="row_grads",
-    )(core, keep, send, w)
-
-
-def place_kernel(where_ref, p0, p1, p2, p3, out_ref):
-    core, y = where_ref[0], where_ref[3]
+    )(keep, send, w)
+
+
+def place_kernel(p0, p1, p2, p3, out_ref):
+    y, core, _, _ = position()
     for k, ref in enumerate((p0, p1, p2, p3)):
-        s = lax.rem(y + 4 - k, 4)
+        s = y ^ k
         for i in range(2):
             cols = pl.ds(pl.multiple_of(s * 512 + (core ^ i) * 256, 256), 256)
             out_ref[:, cols] = ref[i]
 
 
-def place(where, parts):
-    vmem = pl.BlockSpec(memory_space=pltpu.VMEM)
-    smem = pl.BlockSpec(memory_space=pltpu.SMEM)
+def place(parts):
+    vmem = pl.BlockSpec(memory_space=pltpu.VMEM)
     return pl.pallas_call(
         place_kernel,
         out_shape=jax.ShapeDtypeStruct((parts[0].shape[1], 2048), jnp.float32),
-        in_specs=[smem] + [vmem] * 4,
+        in_specs=[vmem] * 4,
         out_specs=vmem,
         compiler_params=pltpu.CompilerParams(vmem_limit_bytes=4 * 2**20),
         name="place_columns",
-    )(where, *parts)
-
-
-AXES = ("group", "member")
-NY, NX, NZ = 4, 4, 8
+    )(*parts)
 
 
 def pairs(move):
@@ -294,19 +311,19 @@
 
 
 def first_axis(k):
-    return lambda y, c, x, z: (y, c, x + k, z) if c == 0 else (y + k, c, x, z)
+    return lambda y, c, x, z: (y, c, x ^ k, z) if c == 0 else (y ^ k, c, x, z)
 
 
 def second_axis(k):
-    return lambda y, c, x, z: (y + k, c, x, z) if c == 0 else (y, c, x + k, z)
+    return lambda y, c, x, z: (y ^ k, c, x, z) if c == 0 else (y, c, x ^ k, z)
 
 
 def along_y(k):
-    return lambda y, c, x, z: (y + k, c, x, z)
+    return lambda y, c, x, z: (y ^ k, c, x, z)
 
 
 def along_z(k):
-    return lambda y, c, x, z: (y, c, x, z + k)
+    return lambda y, c, x, z: (y, c, x, z ^ k)
 
 
 def f32(value):
@@ -314,31 +331,25 @@
 
 
 def shards(histories, lengths, cotangent, w_in):
-    group, member = lax.axis_index("group"), lax.axis_index("member")
-    y, core = group // 2, group % 2
-    x, z = member // NZ, member % NZ
-    first = jnp.where(core == 0, x, y)
-    second = jnp.where(core == 0, y, x)
-    where = jnp.stack([core, first, second, y]).astype(jnp.int32)
     theirs = permute(histories, other_core)
-    keep, send = grads(where, lengths, histories, w_in, cotangent)
+    keep, send = grads(lengths, histories, w_in, cotangent)
     recv = permute(send, other_core)
-    xt = transposed(histories, theirs)
-    parts = weights(where, xt, keep, recv)
-    moved = [permute(parts[k], first_axis(k)) for k in (1, 2, 3)]
-    grad_rows = row_grads(where, keep, send, w_in)
+    acc, xt = own_part(histories, theirs, keep)
+    parts = pair_part(acc, xt, recv)
+    moved = [permute(parts[k], first_axis(k)) for k in (1, 3, 2)]
+    grad_rows = row_grads(keep, send, w_in)
     *moved, grad_rows = lax.optimization_barrier((*moved, grad_rows))
     summed = [f32(parts[0][l]) + f32(moved[0][l]) + f32(moved[1][l]) + f32(moved[2][l]) for l in range(4)]
     moved = [permute(summed[k].astype(jnp.bfloat16), second_axis(k)) for k in (1, 2, 3)]
     block = summed[0] + f32(moved[0]) + f32(moved[1]) + f32(moved[2])
-
-    block = block.astype(jnp.bfloat16).reshape(NZ, 32, 256)
-    nz = [[g * NZ + i for i in range(NZ)] for g in range(NX)]
-    block = lax.all_to_all(block, "member", 0, 0, tiled=True, axis_index_groups=nz)
-    block = jnp.sum(f32(block), axis=0)
+    block = block.reshape(NZ, 32, 256)
+    ends = jnp.stack([block[0], block[7]])
+    moved = [permute(jnp.stack([block[m], block[7 - m]]).astype(jnp.bfloat16), along_z(m)) for m in (1, 2, 3)]
+    ends = ends + f32(moved[0]) + f32(moved[1]) + f32(moved[2])
+    block = ends[0] + permute(ends[1], along_z(7))
 
     both = jnp.stack([block, permute(block, other_core)])
-    grad_w = place(where, [both] + [permute(both, along_y(k)) for k in (1, 2, 3)])
+    grad_w = place([both] + [permute(both, along_y(k)) for k in (1, 2, 3)])
     return (grad_rows, grad_w)
 
 

time: 75.3 us -> 67.6 us (0.90)
  blocking collectives: 14.8 us -> 0 us
  starting transfers between devices: 16.2 us -> 28.1 us
  Pallas kernels: 20.3 us -> 16.5 us
    all_to_all x1 -> x0, blocking collectives: 14.8 us -> none  [shards(): lax.all_to_all(block, 'member', 0, 0, tiled=True, axis_index_groups=nz)]
    ppermute x12 -> x16, starting transfers between devices: 16.2 us -> 28.1 us  [permute(): return lax.ppermute(value, AXES, pairs(move))]
    pallas_call x3, Pallas kernels: 15.1 us -> 12.5 us  [the longest x1 9.47 us: grads(): pl.pallas_call(grads_kernel, out_shape=[pltpu.VMEM((rows, wide // 2), jnp...]
    ppermute x12 -> x16, waiting for transfers between devices: 21.8 us -> 21.8 us  [permute(): return lax.ppermute(value, AXES, pairs(move))]
  transfers between devices with their start and end apart: 12 -> 16, of which waited for: 10 -> 12; matrix products, arithmetic and copies ran while one was open for 1% -> 0% of each run, Pallas kernels for 21% -> 21%
where the time goes in v3:
time: 67.6 us; the launch traced here: 67.5 us
  starting transfers between devices  28.1 us (42%)
  waiting for transfers between devices  21.8 us (32%)
  Pallas kernels  16.5 us (24%)
  between operations  0.72 us (1%)
    ppermute x16, starting transfers between devices, permute(): return lax.ppermute(value, AXES, pairs(move))  28.1 us
    ppermute x16, waiting for transfers between devices, permute(): return lax.ppermute(value, AXES, pairs(move))  21.8 us
    pallas_call x1, Pallas kernels, grads(): pl.pallas_call(grads_kernel, out_shape=[pltpu.VMEM((rows, wide // 2), jnp...  9.47 us
    pallas_call x1, Pallas kernels, row_grads(): pl.pallas_call(rows_kernel, out_shape=jax.ShapeDtypeStruct((keep.shape[0]...  3.35 us
    pallas_call x1, Pallas kernels, own_part(): pl.pallas_call(own_kernel, out_shape=[jax.ShapeDtypeStruct((4, 4, 256, 25...  1.61 us
    pallas_call x1, Pallas kernels, pair_part(): pl.pallas_call(pair_kernel, out_shape=[jax.ShapeDtypeStruct((4, 256, 256)...  1.39 us
  transfers between devices with their start and end apart: 16, of which 12 were waited for; matrix products, arithmetic and copies ran while one was open for 0% of the time, Pallas kernels for 21%

profile of v3, /device:TPU:1, one launch (start us, length us, event | category | flops | bytes accessed | tf_op | source)
XLA Modules:
  0.0 67.5 jit_solution(15416162585111203458)
XLA Ops:
  0.6 3.3 %collective-permute-start = (bf16[512,1024]{1,0:T(8,128)(2,1)}, bf16[512,1024]{1,0:T(8,128)(2,1)S(1)}, u32[]{:S(2)}, u32[]{:S(2)}) collective-permute-start(bf16[512,1024]{1,0:T(8,128)(2,1)} %x_ref.1), channel_id=1, source_target_pairs={{0,32},{1,33},{2,34},{3,35},{4,36},{5,37},{6,38},{7,39},{8,40},{9,... | collective-permute-start | bytes 3145736 | tf_op jit(solution)/shard_map/ppermute | solution.py:306
  4.0 9.5 %uvqk_grads.1 = (bf16[512,1024]{1,0:T(8,128)(2,1)S(1)}, bf16[512,1024]{1,0:T(8,128)(2,1)S(1)}) custom-call(s32[2]{0:T(128)} %len_hbm.1, bf16[512,1024]{1,0:T(8,128)(2,1)} %x_ref.1, bf16[1024,2048]{1,0:T(8,128)(2,1)} %w_ref.1, bf16[512,512]{1,0:T(8,128)(2,1)} %cot_hbm.1), custom_call_target="tpu_custom_call" | custom-call | flops 4000000000 | bytes 8000000 | tf_op jit(solution)/shard_map/uvqk_grads/pallas_call | solution.py:156
  13.6 1.6 %own_weight_grads.1 = (f32[4,4,256,256]{3,2,1,0:T(8,128)S(1)}, bf16[1024,512]{1,0:T(8,128)(2,1)S(1)}) custom-call(bf16[512,1024]{1,0:T(8,128)(2,1)S(1)} %copy-done.1, bf16[512,1024]{1,0:T(8,128)(2,1)S(1)} %collective-permute-done.theirs_ref, bf16[512,1024]{1,0:T(8,128)(2,1)S(1)} %get-tuple-element.14.keep_ref), custom_call_target="tpu_custom_call" | custom-call | flops 1073741824 | bytes 6291456 | tf_op jit(solution)/shard_map/own_weight_grads/pallas_call | solution.py:217
  15.2 1.0 %collective-permute-done.1.recv_ref = bf16[512,1024]{1,0:T(8,128)(2,1)S(1)} collective-permute-done((bf16[512,1024]{1,0:T(8,128)(2,1)S(1)}, bf16[512,1024]{1,0:T(8,128)(2,1)S(1)}, u32[]{:S(2)}, u32[]{:S(2)}) %collective-permute-start.1) | collective-permute-done | bytes 1048608 | tf_op jit(solution)/shard_map/ppermute | solution.py:306
  16.2 1.4 %pair_weight_grads.1 = (bf16[4,256,256]{2,1,0:T(8,128)(2,1)S(1)}, bf16[4,256,256]{2,1,0:T(8,128)(2,1)S(1)}, bf16[4,256,256]{2,1,0:T(8,128)(2,1)S(1)}, bf16[4,256,256]{2,1,0:T(8,128)(2,1)S(1)}) custom-call(f32[4,4,256,256]{3,2,1,0:T(8,128)S(1)} %get-tuple-element.15.acc_ref, bf16[1024,512]{1,0:T(8,128)(2,1)S(1)} %get-tuple-element.16.xt_ref, ...), custom_call_target="tpu_custom_call" | custom-call | flops 1073741824 | bytes 6291456 | tf_op jit(solution)/shard_map/pair_weight_grads/pallas_call | solution.py:237
  17.7 1.4 %collective-permute-start.3 = (bf16[4,256,256]{2,1,0:T(8,128)(2,1)S(1)}, bf16[4,256,256]{2,1,0:T(8,128)(2,1)S(1)}, u32[]{:S(2)}, u32[]{:S(2)}) collective-permute-start(bf16[4,256,256]{2,1,0:T(8,128)(2,1)S(1)} %get-tuple-element.19), channel_id=1, source_target_pairs={{0,24},{1,25},{2,26},{3,27},{4,28},{5,29},{6,30},{7,31},{8,16},{9,... | collective-permute-start | bytes 1572872 | tf_op jit(solution)/shard_map/ppermute | solution.py:306
  19.1 1.8 %collective-permute-start.4 = (bf16[4,256,256]{2,1,0:T(8,128)(2,1)S(1)}, bf16[4,256,256]{2,1,0:T(8,128)(2,1)S(1)}, u32[]{:S(2)}, u32[]{:S(2)}) collective-permute-start(bf16[4,256,256]{2,1,0:T(8,128)(2,1)S(1)} %get-tuple-element.20), channel_id=1, source_target_pairs={{0,16},{1,17},{2,18},{3,19},{4,20},{5,21},{6,22},{7,23},{8,24},{9,... | collective-permute-start | bytes 1572872 | tf_op jit(solution)/shard_map/ppermute | solution.py:306
  20.9 3.4 %row_grads.1 = bf16[512,1024]{1,0:T(8,128)(2,1)} custom-call(bf16[512,1024]{1,0:T(8,128)(2,1)S(1)} %get-tuple-element.14.keep_ref, bf16[512,1024]{1,0:T(8,128)(2,1)S(1)} %get-tuple-element.17.send_ref, bf16[1024,2048]{1,0:T(8,128)(2,1)S(1)} %copy-done), custom_call_target="tpu_custom_call" | custom-call | flops 2147483648 | bytes 7340032 | tf_op jit(solution)/shard_map/row_grads/pallas_call | solution.py:262
  24.3 1.7 %collective-permute-done.2 = bf16[4,256,256]{2,1,0:T(8,128)(2,1)S(1)} collective-permute-done((bf16[4,256,256]{2,1,0:T(8,128)(2,1)S(1)}, bf16[4,256,256]{2,1,0:T(8,128)(2,1)S(1)}, u32[]{:S(2)}, u32[]{:S(2)}) %collective-permute-start.2) | collective-permute-done | bytes 524320 | tf_op jit(solution)/shard_map/ppermute | solution.py:306
  26.0 6.9 %collective-permute-done.3 = bf16[4,256,256]{2,1,0:T(8,128)(2,1)S(1)} collective-permute-done((bf16[4,256,256]{2,1,0:T(8,128)(2,1)S(1)}, bf16[4,256,256]{2,1,0:T(8,128)(2,1)S(1)}, u32[]{:S(2)}, u32[]{:S(2)}) %collective-permute-start.3) | collective-permute-done | bytes 524320 | tf_op jit(solution)/shard_map/ppermute | solution.py:306
  32.9 0.2 fusion.2
  33.1 0.4 collective-permute-start.5
  33.6 1.8 %collective-permute-start.7 = (bf16[256,256]{1,0:T(8,128)(2,1)S(1)}, bf16[256,256]{1,0:T(8,128)(2,1)S(1)}, u32[]{:S(2)}, u32[]{:S(2)}) collective-permute-start(bf16[256,256]{1,0:T(8,128)(2,1)S(1)} %get-tuple-element.29), channel_id=1, source_target_pairs={{0,192},{1,193},{2,194},{3,195},{4,196},{5,197},{6,198},{7,199},{8... | collective-permute-start | bytes 393224 | tf_op jit(solution)/shard_map/ppermute | solution.py:306
  35.4 1.1 %collective-permute-start.6 = (bf16[256,256]{1,0:T(8,128)(2,1)S(1)}, bf16[256,256]{1,0:T(8,128)(2,1)S(1)}, u32[]{:S(2)}, u32[]{:S(2)}) collective-permute-start(bf16[256,256]{1,0:T(8,128)(2,1)S(1)} %get-tuple-element.30), channel_id=1, source_target_pairs={{0,128},{1,129},{2,130},{3,131},{4,132},{5,133},{6,134},{7,135},{8... | collective-permute-start | bytes 393224 | tf_op jit(solution)/shard_map/ppermute | solution.py:306
  36.5 0.6 collective-permute-done.5
  37.0 1.6 %collective-permute-done.7 = bf16[256,256]{1,0:T(8,128)(2,1)S(1)} collective-permute-done((bf16[256,256]{1,0:T(8,128)(2,1)S(1)}, bf16[256,256]{1,0:T(8,128)(2,1)S(1)}, u32[]{:S(2)}, u32[]{:S(2)}) %collective-permute-start.7) | collective-permute-done | bytes 131104 | tf_op jit(solution)/shard_map/ppermute | solution.py:306
  38.6 2.1 %collective-permute-done.6 = bf16[256,256]{1,0:T(8,128)(2,1)S(1)} collective-permute-done((bf16[256,256]{1,0:T(8,128)(2,1)S(1)}, bf16[256,256]{1,0:T(8,128)(2,1)S(1)}, u32[]{:S(2)}, u32[]{:S(2)}) %collective-permute-start.6) | collective-permute-done | bytes 131104 | tf_op jit(solution)/shard_map/ppermute | solution.py:306
  40.8 3.1 %collective-permute-start.9 = (bf16[2,32,256]{2,1,0:T(8,128)(2,1)S(1)}, bf16[2,32,256]{2,1,0:T(8,128)(2,1)S(1)}, u32[]{:S(2)}, u32[]{:S(2)}) collective-permute-start(bf16[2,32,256]{2,1,0:T(8,128)(2,1)S(1)} %pad_maximum_fusion.2), channel_id=1, source_target_pairs={{0,2},{1,3},{2,0},{3,1},{4,6},{5,7},{6,4},{7,5},{8,10},{9,11},{10,... | collective-permute-start | bytes 98312 | tf_op jit(solution)/shard_map/ppermute | solution.py:306
  43.9 1.5 %collective-permute-start.10 = (bf16[2,32,256]{2,1,0:T(8,128)(2,1)S(1)}, bf16[2,32,256]{2,1,0:T(8,128)(2,1)S(1)}, u32[]{:S(2)}, u32[]{:S(2)}) collective-permute-start(bf16[2,32,256]{2,1,0:T(8,128)(2,1)S(1)} %pad_maximum_fusion.3), channel_id=1, source_target_pairs={{0,3},{1,2},{2,1},{3,0},{4,7},{5,6},{6,5},{7,4},{8,11},{9,10},{10,... | collective-permute-start | bytes 98312 | tf_op jit(solution)/shard_map/ppermute | solution.py:306
  45.4 0.3 collective-permute-start.8
  45.7 2.8 %collective-permute-done.10 = bf16[2,32,256]{2,1,0:T(8,128)(2,1)S(1)} collective-permute-done((bf16[2,32,256]{2,1,0:T(8,128)(2,1)S(1)}, bf16[2,32,256]{2,1,0:T(8,128)(2,1)S(1)}, u32[]{:S(2)}, u32[]{:S(2)}) %collective-permute-start.10) | collective-permute-done | bytes 32800 | tf_op jit(solution)/shard_map/ppermute | solution.py:306
  48.6 4.0 %collective-permute-start.11 = (f32[32,256]{1,0:T(8,128)S(1)}, f32[32,256]{1,0:T(8,128)S(1)}, u32[]{:S(2)}, u32[]{:S(2)}) collective-permute-start(f32[32,256]{1,0:T(8,128)S(1)} %slice_bitcast_fusion), channel_id=1, source_target_pairs={{0,7},{1,6},{2,5},{3,4},{4,3},{5,2},{6,1},{7,0},{8,15},{9,14},{10,... | collective-permute-start | bytes 98312 | tf_op jit(solution)/shard_map/ppermute | solution.py:306
  52.6 1.3 %collective-permute-done.11 = f32[32,256]{1,0:T(8,128)S(1)} collective-permute-done((f32[32,256]{1,0:T(8,128)S(1)}, f32[32,256]{1,0:T(8,128)S(1)}, u32[]{:S(2)}, u32[]{:S(2)}) %collective-permute-start.11) | collective-permute-done | bytes 32800 | tf_op jit(solution)/shard_map/ppermute | solution.py:306
  53.9 5.8 %collective-permute-start.12 = (f32[32,256]{1,0:T(8,128)S(1)}, f32[32,256]{1,0:T(8,128)S(1)}, u32[]{:S(2)}, u32[]{:S(2)}) collective-permute-start(f32[32,256]{1,0:T(8,128)S(1)} %fusion.7), channel_id=1, source_target_pairs={{0,32},{1,33},{2,34},{3,35},{4,36},{5,37},{6,38},{7,39},{8,40},{9,... | collective-permute-start | bytes 98312 | tf_op jit(solution)/shard_map/ppermute | solution.py:306
  59.7 0.9 %collective-permute-done.12 = f32[32,256]{1,0:T(8,128)S(1)} collective-permute-done((f32[32,256]{1,0:T(8,128)S(1)}, f32[32,256]{1,0:T(8,128)S(1)}, u32[]{:S(2)}, u32[]{:S(2)}) %collective-permute-start.12) | collective-permute-done | bytes 32800 | tf_op jit(solution)/shard_map/ppermute | solution.py:306
  60.6 0.8 %collective-permute-start.15 = (f32[2,32,256]{2,1,0:T(8,128)S(1)}, f32[2,32,256]{2,1,0:T(8,128)S(1)}, u32[]{:S(2)}, u32[]{:S(2)}) collective-permute-start(f32[2,32,256]{2,1,0:T(8,128)S(1)} %pad_maximum_fusion.p0), channel_id=1, source_target_pairs={{0,192},{1,193},{2,194},{3,195},{4,196},{5,197},{6,198},{7,199},{8... | collective-permute-start | bytes 196616 | tf_op jit(solution)/shard_map/ppermute | solution.py:306
  61.4 1.3 %collective-permute-start.14 = (f32[2,32,256]{2,1,0:T(8,128)S(1)}, f32[2,32,256]{2,1,0:T(8,128)S(1)}, u32[]{:S(2)}, u32[]{:S(2)}) collective-permute-start(f32[2,32,256]{2,1,0:T(8,128)S(1)} %pad_maximum_fusion.p0), channel_id=1, source_target_pairs={{0,128},{1,129},{2,130},{3,131},{4,132},{5,133},{6,134},{7,135},{8... | collective-permute-start | bytes 196616 | tf_op jit(solution)/shard_map/ppermute | solution.py:306
  62.8 1.1 %collective-permute-start.13 = (f32[2,32,256]{2,1,0:T(8,128)S(1)}, f32[2,32,256]{2,1,0:T(8,128)S(1)}, u32[]{:S(2)}, u32[]{:S(2)}) collective-permute-start(f32[2,32,256]{2,1,0:T(8,128)S(1)} %pad_maximum_fusion.p0), channel_id=1, source_target_pairs={{0,64},{1,65},{2,66},{3,67},{4,68},{5,69},{6,70},{7,71},{8,72},{9,... | collective-permute-start | bytes 196616 | tf_op jit(solution)/shard_map/ppermute | solution.py:306
  63.8 1.1 %collective-permute-done.15.p3 = f32[2,32,256]{2,1,0:T(8,128)S(1)} collective-permute-done((f32[2,32,256]{2,1,0:T(8,128)S(1)}, f32[2,32,256]{2,1,0:T(8,128)S(1)}, u32[]{:S(2)}, u32[]{:S(2)}) %collective-permute-start.15) | collective-permute-done | bytes 65568 | tf_op jit(solution)/shard_map/ppermute | solution.py:306
  64.9 1.2 %collective-permute-done.14.p2 = f32[2,32,256]{2,1,0:T(8,128)S(1)} collective-permute-done((f32[2,32,256]{2,1,0:T(8,128)S(1)}, f32[2,32,256]{2,1,0:T(8,128)S(1)}, u32[]{:S(2)}, u32[]{:S(2)}) %collective-permute-start.14) | collective-permute-done | bytes 65568 | tf_op jit(solution)/shard_map/ppermute | solution.py:306
  66.1 0.6 collective-permute-done.13.p1
  66.8 0.7 %place_columns.1 = f32[32,2048]{1,0:T(8,128)} custom-call(f32[2,32,256]{2,1,0:T(8,128)S(1)} %pad_maximum_fusion.p0, f32[2,32,256]{2,1,0:T(8,128)S(1)} %collective-permute-done.13.p1, f32[2,32,256]{2,1,0:T(8,128)S(1)} %collective-permute-done.14.p2, f32[2,32,256]{2,1,0:T(8,128)S(1)} %collective-permute-done.15.p3), custom_call_target="tpu_custom_call" | custom-call | tf_op jit(solution)/shard_map/place_columns/pallas_call | solution.py:284
  (20 shorter events, 0.5 us)
Async XLA Ops:
  0.6 13.0 %copy-start.1 = (bf16[512,1024]{1,0:T(8,128)(2,1)S(1)}, bf16[512,1024]{1,0:T(8,128)(2,1)}, u32[]{:S(2)}) copy-start(bf16[512,1024]{1,0:T(8,128)(2,1)} %x_ref.1) | copy-start | bytes 3145732
  0.6 13.0 %collective-permute-start = (bf16[512,1024]{1,0:T(8,128)(2,1)}, bf16[512,1024]{1,0:T(8,128)(2,1)S(1)}, u32[]{:S(2)}, u32[]{:S(2)}) collective-permute-start(bf16[512,1024]{1,0:T(8,128)(2,1)} %x_ref.1), channel_id=1, source_target_pairs={{0,32},{1,33},{2,34},{3,35},{4,36},{5,37},{6,38},{7,39},{8,40},{9,... | collective-permute-start | bytes 3145736 | tf_op jit(solution)/shard_map/ppermute | solution.py:306
  13.4 2.7 %collective-permute-start.1 = (bf16[512,1024]{1,0:T(8,128)(2,1)S(1)}, bf16[512,1024]{1,0:T(8,128)(2,1)S(1)}, u32[]{:S(2)}, u32[]{:S(2)}) collective-permute-start(bf16[512,1024]{1,0:T(8,128)(2,1)S(1)} %get-tuple-element.17.send_ref), channel_id=1, source_target_pairs={{0,32},{1,33},{2,34},{3,35},{4,36},{5,37},{6,38},{7,39},{8,40},{9,... | collective-permute-start | bytes 3145736 | tf_op jit(solution)/shard_map/ppermute | solution.py:306
  13.6 7.3 %copy-start = (bf16[1024,2048]{1,0:T(8,128)(2,1)S(1)}, bf16[1024,2048]{1,0:T(8,128)(2,1)}, u32[]{:S(2)}) copy-start(bf16[1024,2048]{1,0:T(8,128)(2,1)} %w_ref.1) | copy-start | bytes 12582916
  17.6 8.4 %collective-permute-start.2 = (bf16[4,256,256]{2,1,0:T(8,128)(2,1)S(1)}, bf16[4,256,256]{2,1,0:T(8,128)(2,1)S(1)}, u32[]{:S(2)}, u32[]{:S(2)}) collective-permute-start(bf16[4,256,256]{2,1,0:T(8,128)(2,1)S(1)} %get-tuple-element.18), channel_id=1, source_target_pairs={{0,8},{1,9},{2,10},{3,11},{4,12},{5,13},{6,14},{7,15},{8,0},{9,1},... | collective-permute-start | bytes 1572872 | tf_op jit(solution)/shard_map/ppermute | solution.py:306
  17.7 15.2 %collective-permute-start.3 = (bf16[4,256,256]{2,1,0:T(8,128)(2,1)S(1)}, bf16[4,256,256]{2,1,0:T(8,128)(2,1)S(1)}, u32[]{:S(2)}, u32[]{:S(2)}) collective-permute-start(bf16[4,256,256]{2,1,0:T(8,128)(2,1)S(1)} %get-tuple-element.19), channel_id=1, source_target_pairs={{0,24},{1,25},{2,26},{3,27},{4,28},{5,29},{6,30},{7,31},{8,16},{9,... | collective-permute-start | bytes 1572872 | tf_op jit(solution)/shard_map/ppermute | solution.py:306
  19.1 13.8 %collective-permute-start.4 = (bf16[4,256,256]{2,1,0:T(8,128)(2,1)S(1)}, bf16[4,256,256]{2,1,0:T(8,128)(2,1)S(1)}, u32[]{:S(2)}, u32[]{:S(2)}) collective-permute-start(bf16[4,256,256]{2,1,0:T(8,128)(2,1)S(1)} %get-tuple-element.20), channel_id=1, source_target_pairs={{0,16},{1,17},{2,18},{3,19},{4,20},{5,21},{6,22},{7,23},{8,24},{9,... | collective-permute-start | bytes 1572872 | tf_op jit(solution)/shard_map/ppermute | solution.py:306
  33.1 3.9 %collective-permute-start.5 = (bf16[256,256]{1,0:T(8,128)(2,1)S(1)}, bf16[256,256]{1,0:T(8,128)(2,1)S(1)}, u32[]{:S(2)}, u32[]{:S(2)}) collective-permute-start(bf16[256,256]{1,0:T(8,128)(2,1)S(1)} %get-tuple-element.28), channel_id=1, source_target_pairs={{0,64},{1,65},{2,66},{3,67},{4,68},{5,69},{6,70},{7,71},{8,72},{9,... | collective-permute-start | bytes 393224 | tf_op jit(solution)/shard_map/ppermute | solution.py:306
  33.6 5.0 %collective-permute-start.7 = (bf16[256,256]{1,0:T(8,128)(2,1)S(1)}, bf16[256,256]{1,0:T(8,128)(2,1)S(1)}, u32[]{:S(2)}, u32[]{:S(2)}) collective-permute-start(bf16[256,256]{1,0:T(8,128)(2,1)S(1)} %get-tuple-element.29), channel_id=1, source_target_pairs={{0,192},{1,193},{2,194},{3,195},{4,196},{5,197},{6,198},{7,199},{8... | collective-permute-start | bytes 393224 | tf_op jit(solution)/shard_map/ppermute | solution.py:306
  35.4 5.3 %collective-permute-start.6 = (bf16[256,256]{1,0:T(8,128)(2,1)S(1)}, bf16[256,256]{1,0:T(8,128)(2,1)S(1)}, u32[]{:S(2)}, u32[]{:S(2)}) collective-permute-start(bf16[256,256]{1,0:T(8,128)(2,1)S(1)} %get-tuple-element.30), channel_id=1, source_target_pairs={{0,128},{1,129},{2,130},{3,131},{4,132},{5,133},{6,134},{7,135},{8... | collective-permute-start | bytes 393224 | tf_op jit(solution)/shard_map/ppermute | solution.py:306
  40.8 4.8 %collective-permute-start.9 = (bf16[2,32,256]{2,1,0:T(8,128)(2,1)S(1)}, bf16[2,32,256]{2,1,0:T(8,128)(2,1)S(1)}, u32[]{:S(2)}, u32[]{:S(2)}) collective-permute-start(bf16[2,32,256]{2,1,0:T(8,128)(2,1)S(1)} %pad_maximum_fusion.2), channel_id=1, source_target_pairs={{0,2},{1,3},{2,0},{3,1},{4,6},{5,7},{6,4},{7,5},{8,10},{9,11},{10,... | collective-permute-start | bytes 98312 | tf_op jit(solution)/shard_map/ppermute | solution.py:306
  43.9 4.6 %collective-permute-start.10 = (bf16[2,32,256]{2,1,0:T(8,128)(2,1)S(1)}, bf16[2,32,256]{2,1,0:T(8,128)(2,1)S(1)}, u32[]{:S(2)}, u32[]{:S(2)}) collective-permute-start(bf16[2,32,256]{2,1,0:T(8,128)(2,1)S(1)} %pad_maximum_fusion.3), channel_id=1, source_target_pairs={{0,3},{1,2},{2,1},{3,0},{4,7},{5,6},{6,5},{7,4},{8,11},{9,10},{10,... | collective-permute-start | bytes 98312 | tf_op jit(solution)/shard_map/ppermute | solution.py:306
  45.4 3.1 %collective-permute-start.8 = (bf16[2,32,256]{2,1,0:T(8,128)(2,1)S(1)}, bf16[2,32,256]{2,1,0:T(8,128)(2,1)S(1)}, u32[]{:S(2)}, u32[]{:S(2)}) collective-permute-start(bf16[2,32,256]{2,1,0:T(8,128)(2,1)S(1)} %pad_maximum_fusion.1), channel_id=1, source_target_pairs={{0,1},{1,0},{2,3},{3,2},{4,5},{5,4},{6,7},{7,6},{8,9},{9,8},{10,11... | collective-permute-start | bytes 98312 | tf_op jit(solution)/shard_map/ppermute | solution.py:306
  48.6 5.3 %collective-permute-start.11 = (f32[32,256]{1,0:T(8,128)S(1)}, f32[32,256]{1,0:T(8,128)S(1)}, u32[]{:S(2)}, u32[]{:S(2)}) collective-permute-start(f32[32,256]{1,0:T(8,128)S(1)} %slice_bitcast_fusion), channel_id=1, source_target_pairs={{0,7},{1,6},{2,5},{3,4},{4,3},{5,2},{6,1},{7,0},{8,15},{9,14},{10,... | collective-permute-start | bytes 98312 | tf_op jit(solution)/shard_map/ppermute | solution.py:306
  53.9 6.7 %collective-permute-start.12 = (f32[32,256]{1,0:T(8,128)S(1)}, f32[32,256]{1,0:T(8,128)S(1)}, u32[]{:S(2)}, u32[]{:S(2)}) collective-permute-start(f32[32,256]{1,0:T(8,128)S(1)} %fusion.7), channel_id=1, source_target_pairs={{0,32},{1,33},{2,34},{3,35},{4,36},{5,37},{6,38},{7,39},{8,40},{9,... | collective-permute-start | bytes 98312 | tf_op jit(solution)/shard_map/ppermute | solution.py:306
  60.6 4.3 %collective-permute-start.15 = (f32[2,32,256]{2,1,0:T(8,128)S(1)}, f32[2,32,256]{2,1,0:T(8,128)S(1)}, u32[]{:S(2)}, u32[]{:S(2)}) collective-permute-start(f32[2,32,256]{2,1,0:T(8,128)S(1)} %pad_maximum_fusion.p0), channel_id=1, source_target_pairs={{0,192},{1,193},{2,194},{3,195},{4,196},{5,197},{6,198},{7,199},{8... | collective-permute-start | bytes 196616 | tf_op jit(solution)/shard_map/ppermute | solution.py:306
  61.4 4.7 %collective-permute-start.14 = (f32[2,32,256]{2,1,0:T(8,128)S(1)}, f32[2,32,256]{2,1,0:T(8,128)S(1)}, u32[]{:S(2)}, u32[]{:S(2)}) collective-permute-start(f32[2,32,256]{2,1,0:T(8,128)S(1)} %pad_maximum_fusion.p0), channel_id=1, source_target_pairs={{0,128},{1,129},{2,130},{3,131},{4,132},{5,133},{6,134},{7,135},{8... | collective-permute-start | bytes 196616 | tf_op jit(solution)/shard_map/ppermute | solution.py:306
  62.8 4.0 %collective-permute-start.13 = (f32[2,32,256]{2,1,0:T(8,128)S(1)}, f32[2,32,256]{2,1,0:T(8,128)S(1)}, u32[]{:S(2)}, u32[]{:S(2)}) collective-permute-start(f32[2,32,256]{2,1,0:T(8,128)S(1)} %pad_maximum_fusion.p0), channel_id=1, source_target_pairs={{0,64},{1,65},{2,66},{3,67},{4,68},{5,69},{6,70},{7,71},{8,72},{9,... | collective-permute-start | bytes 196616 | tf_op jit(solution)/shard_map/ppermute | solution.py:306

commit v4 on v3

--- a/solution.py
+++ b/solution.py
@@ -1,3 +1,5 @@
+import functools
+
 import jax
 import jax.numpy as jnp
 from jax import lax
@@ -106,14 +108,12 @@
             p_ref[h, r, keys] = (p * mask_ref[r, keys]).astype(bf16)
             s_ref[h, r, keys] = (sig + p * (1.0 - sig)) * mask_ref[r, keys]
     project(1)
-    for i in range(nblocks):
-        r, keys, _ = spans(i)
-        for h in range(HEADS):
-            att_ref[r, head(h)] = mm(p_ref[h, r, keys], act_ref[keys, col(1, h)])
     project(0)
     load_cot.wait()
     for i in range(nblocks):
-        r, _, _ = spans(i)
+        r, keys, _ = spans(i)
+        for h in range(HEADS):
+            att_ref[r, head(h)] = mm(p_ref[h, r, keys], act_ref[keys, col(1, h)])
         _, in0, in1 = row_facts(i)
         att = att_ref[r, :]
         cen = att - jnp.mean(att, axis=1, keepdims=True)
@@ -204,10 +204,11 @@
             yield k, l, pl.ds(pl.multiple_of(rb * 256, 256), 256), pl.ds(pl.multiple_of(cb * 256, 256), 256)
 
 
-def own_kernel(x_ref, theirs_ref, keep_ref, acc_ref, xt_ref, own_ref):
+def own_kernel(x_ref, theirs_ref, keep_ref, a0, a1, a2, a3, xt_ref, own_ref):
     flip(x_ref, own_ref)
+    sums = (a0, a1, a2, a3)
     for k, l, rs, cs in blocks_of():
-        acc_ref[k, l] = mm(own_ref[rs, :], keep_ref[:, cs])
+        sums[k][l] = mm(own_ref[rs, :], keep_ref[:, cs])
     flip(theirs_ref, xt_ref)
 
 
@@ -216,9 +217,9 @@
     vmem = pl.BlockSpec(memory_space=pltpu.VMEM)
     return pl.pallas_call(
         own_kernel,
-        out_shape=[jax.ShapeDtypeStruct((4, 4, 256, 256), jnp.float32), jax.ShapeDtypeStruct((d, rows), jnp.bfloat16)],
+        out_shape=[pltpu.VMEM((4, 256, 256), jnp.float32)] * 4 + [pltpu.VMEM((d, rows), jnp.bfloat16)],
         in_specs=[vmem] * 3,
-        out_specs=[vmem, vmem],
+        out_specs=[vmem] * 5,
         scratch_shapes=[pltpu.VMEM((d, rows), jnp.bfloat16)],
         compiler_params=pltpu.CompilerParams(vmem_limit_bytes=24 * 2**20),
         cost_estimate=pl.CostEstimate(flops=2**30, bytes_accessed=6 * 2**20, transcendentals=0),
@@ -226,23 +227,28 @@
     )(x, theirs, keep)
 
 
-def pair_kernel(acc_ref, xt_ref, recv_ref, o0, o1, o2, o3):
-    outs = (o0, o1, o2, o3)
+def pair_kernel(ks, *refs):
+    n = len(ks)
+    xt_ref, recv_ref = refs[n:n + 2]
     for k, l, rs, cs in blocks_of():
-        outs[k][l] = (acc_ref[k, l] + mm(xt_ref[rs, :], recv_ref[:, cs])).astype(jnp.bfloat16)
-
-
-def pair_part(acc, xt, recv):
-    vmem = pl.BlockSpec(memory_space=pltpu.VMEM)
-    return pl.pallas_call(
-        pair_kernel,
-        out_shape=[jax.ShapeDtypeStruct((4, 256, 256), jnp.bfloat16)] * 4,
-        in_specs=[vmem] * 3,
-        out_specs=[vmem] * 4,
+        if k in ks:
+            at = ks.index(k)
+            total = refs[at][l] + mm(xt_ref[rs, :], recv_ref[:, cs])
+            refs[n + 2 + at][l] = total.astype(jnp.bfloat16)
+
+
+def pair_part(ks, sums, xt, recv):
+    vmem = pl.BlockSpec(memory_space=pltpu.VMEM)
+    n = len(ks)
+    return pl.pallas_call(
+        functools.partial(pair_kernel, ks),
+        out_shape=[pltpu.VMEM((4, 256, 256), jnp.bfloat16)] * n,
+        in_specs=[vmem] * (n + 2),
+        out_specs=[vmem] * n,
         compiler_params=pltpu.CompilerParams(vmem_limit_bytes=24 * 2**20),
-        cost_estimate=pl.CostEstimate(flops=2**30, bytes_accessed=6 * 2**20, transcendentals=0),
+        cost_estimate=pl.CostEstimate(flops=n * 2**28, bytes_accessed=(2 * n + 2) * 2**20, transcendentals=0),
         name="pair_weight_grads",
-    )(acc, xt, recv)
+    )(*[sums[k] for k in ks], xt, recv)
 
 
 def rows_kernel(keep_ref, send_ref, w_ref, out_ref):
@@ -276,7 +282,7 @@
         s = y ^ k
         for i in range(2):
             cols = pl.ds(pl.multiple_of(s * 512 + (core ^ i) * 256, 256), 256)
-            out_ref[:, cols] = ref[i]
+            out_ref[:, cols] = ref[i].astype(jnp.float32)
 
 
 def place(parts):
@@ -334,13 +340,15 @@
     theirs = permute(histories, other_core)
     keep, send = grads(lengths, histories, w_in, cotangent)
     recv = permute(send, other_core)
-    acc, xt = own_part(histories, theirs, keep)
-    parts = pair_part(acc, xt, recv)
-    moved = [permute(parts[k], first_axis(k)) for k in (1, 3, 2)]
+    *sums, xt = own_part(histories, theirs, keep)
+    far, = pair_part((2,), sums, xt, recv)
+    near, last = pair_part((1, 3), sums, xt, recv)
+    moved = [permute(part, first_axis(k)) for k, part in ((2, far), (1, near), (3, last))]
+    mine, = pair_part((0,), sums, xt, recv)
     grad_rows = row_grads(keep, send, w_in)
-    *moved, grad_rows = lax.optimization_barrier((*moved, grad_rows))
-    summed = [f32(parts[0][l]) + f32(moved[0][l]) + f32(moved[1][l]) + f32(moved[2][l]) for l in range(4)]
-    moved = [permute(summed[k].astype(jnp.bfloat16), second_axis(k)) for k in (1, 2, 3)]
+    *moved, mine, grad_rows = lax.optimization_barrier((*moved, mine, grad_rows))
+    summed = [f32(mine[l]) + f32(moved[0][l]) + f32(moved[1][l]) + f32(moved[2][l]) for l in range(4)]
+    moved = [permute(summed[k].astype(jnp.bfloat16), second_axis(k)) for k in (1, 3, 2)]
     block = summed[0] + f32(moved[0]) + f32(moved[1]) + f32(moved[2])
     block = block.reshape(NZ, 32, 256)
     ends = jnp.stack([block[0], block[7]])
@@ -348,8 +356,10 @@
     ends = ends + f32(moved[0]) + f32(moved[1]) + f32(moved[2])
     block = ends[0] + permute(ends[1], along_z(7))
 
+    block = block.astype(jnp.bfloat16)
     both = jnp.stack([block, permute(block, other_core)])
-    grad_w = place([both] + [permute(both, along_y(k)) for k in (1, 2, 3)])
+    gathered = {k: permute(both, along_y(k)) for k in (2, 1, 3)}
+    grad_w = place([both, gathered[1], gathered[2], gathered[3]])
     return (grad_rows, grad_w)
 
 

time: 67.6 us -> 65.7 us (0.972); the launches traced: 67.5 us -> 64.5 us
  starting transfers between devices: 28.1 us -> 24.9 us
    ppermute x16, starting transfers between devices: 28.1 us -> 24.9 us  [permute(): return lax.ppermute(value, AXES, pairs(move))]
    pallas_call x2 -> x4, Pallas kernels: 2.99 us -> 3.3 us  [the longest x3 1.69 us: pair_part(): pl.pallas_call(functools.partial(pair_kernel, ks), out_shape=[pltpu.VMEM(...]
  transfers between devices with their start and end apart: 16 -> 16, of which waited for: 12 -> 12; matrix products, arithmetic and copies ran while one was open for 0% -> 0% of each run, Pallas kernels for 21% -> 24%
where the time goes in v4:
time: 65.7 us; the launch traced here: 64.5 us
  starting transfers between devices  24.9 us (38%)
  waiting for transfers between devices  21.8 us (33%)
  Pallas kernels  16.7 us (25%)
  between operations  0.74 us (1%)
    ppermute x16, starting transfers between devices, permute(): return lax.ppermute(value, AXES, pairs(move))  24.9 us
    ppermute x16, waiting for transfers between devices, permute(): return lax.ppermute(value, AXES, pairs(move))  21.8 us
    pallas_call x1, Pallas kernels, grads(): pl.pallas_call(grads_kernel, out_shape=[pltpu.VMEM((rows, wide // 2), jnp...  9.33 us
    pallas_call x1, Pallas kernels, row_grads(): pl.pallas_call(rows_kernel, out_shape=jax.ShapeDtypeStruct((keep.shape[0]...  3.35 us
    pallas_call x3, Pallas kernels, pair_part(): pl.pallas_call(functools.partial(pair_kernel, ks), out_shape=[pltpu.VMEM(...  1.69 us
    pallas_call x1, Pallas kernels, own_part(): pl.pallas_call(own_kernel, out_shape=[pltpu.VMEM((4, 256, 256), jnp.float...  1.61 us
  transfers between devices with their start and end apart: 16, of which 12 were waited for; matrix products, arithmetic and copies ran while one was open for 0% of the time, Pallas kernels for 24%

profile of v4, /device:TPU:1, one launch (start us, length us, event | category | flops | bytes accessed | tf_op | source)
XLA Modules:
  0.0 64.5 jit_solution(17139363110867838063)
XLA Ops:
  0.6 3.3 %collective-permute-start = (bf16[512,1024]{1,0:T(8,128)(2,1)}, bf16[512,1024]{1,0:T(8,128)(2,1)S(1)}, u32[]{:S(2)}, u32[]{:S(2)}) collective-permute-start(bf16[512,1024]{1,0:T(8,128)(2,1)} %x_ref.1), channel_id=1, source_target_pairs={{0,32},{1,33},{2,34},{3,35},{4,36},{5,37},{6,38},{7,39},{8,40},{9,... | collective-permute-start | bytes 3145736 | tf_op jit(solution)/shard_map/ppermute | solution.py:312
  4.0 9.3 %uvqk_grads.1 = (bf16[512,1024]{1,0:T(8,128)(2,1)S(1)}, bf16[512,1024]{1,0:T(8,128)(2,1)S(1)}) custom-call(s32[2]{0:T(128)} %len_hbm.1, bf16[512,1024]{1,0:T(8,128)(2,1)} %x_ref.1, bf16[1024,2048]{1,0:T(8,128)(2,1)} %w_ref.1, bf16[512,512]{1,0:T(8,128)(2,1)} %cot_hbm.1), custom_call_target="tpu_custom_call" | custom-call | flops 4000000000 | bytes 8000000 | tf_op jit(solution)/shard_map/uvqk_grads/pallas_call | solution.py:156
  13.5 1.6 %own_weight_grads.1 = (f32[4,256,256]{2,1,0:T(8,128)S(1)}, f32[4,256,256]{2,1,0:T(8,128)S(1)}, f32[4,256,256]{2,1,0:T(8,128)S(1)}, f32[4,256,256]{2,1,0:T(8,128)S(1)}, bf16[1024,512]{1,0:T(8,128)(2,1)S(1)}) custom-call(bf16[512,1024]{1,0:T(8,128)(2,1)S(1)} %copy-done.1, bf16[512,1024]{1,0:T(8,128)(2,1)S(1)} %collective-permute-done.theirs_ref, ...), custom_call_target="tpu_custom_call" | custom-call | flops 1073741824 | bytes 6291456 | tf_op jit(solution)/shard_map/own_weight_grads/pallas_call | solution.py:218
  15.1 0.9 %collective-permute-done.1.refs_2_.refs_3_ = bf16[512,1024]{1,0:T(8,128)(2,1)S(1)} collective-permute-done((bf16[512,1024]{1,0:T(8,128)(2,1)S(1)}, bf16[512,1024]{1,0:T(8,128)(2,1)S(1)}, u32[]{:S(2)}, u32[]{:S(2)}) %collective-permute-start.1) | collective-permute-done | bytes 1048608 | tf_op jit(solution)/shard_map/ppermute | solution.py:312
  16.1 0.5 pair_weight_grads.3
  16.5 1.3 %collective-permute-start.2 = (bf16[4,256,256]{2,1,0:T(8,128)(2,1)S(1)}, bf16[4,256,256]{2,1,0:T(8,128)(2,1)S(1)}, u32[]{:S(2)}, u32[]{:S(2)}) collective-permute-start(bf16[4,256,256]{2,1,0:T(8,128)(2,1)S(1)} %pair_weight_grads.3), channel_id=1, source_target_pairs={{0,16},{1,17},{2,18},{3,19},{4,20},{5,21},{6,22},{7,23},{8,24},{9,... | collective-permute-start | bytes 1572872 | tf_op jit(solution)/shard_map/ppermute | solution.py:312
  17.8 0.8 %pair_weight_grads.4 = (bf16[4,256,256]{2,1,0:T(8,128)(2,1)S(1)}, bf16[4,256,256]{2,1,0:T(8,128)(2,1)S(1)}) custom-call(f32[4,256,256]{2,1,0:T(8,128)S(1)} %get-tuple-element.20.refs_0_, f32[4,256,256]{2,1,0:T(8,128)S(1)} %get-tuple-element.21.refs_1_, bf16[1024,512]{1,0:T(8,128)(2,1)S(1)} %get-tuple-element.18.refs_1_.refs_2_, ...), custom_call_target="tpu_custom_call" | custom-call | flops 536870912 | bytes 6291456 | tf_op jit(solution)/shard_map/pair_weight_grads/pallas_call | solution.py:243
  18.6 0.5 collective-permute-start.3
  19.0 1.7 %collective-permute-start.4 = (bf16[4,256,256]{2,1,0:T(8,128)(2,1)S(1)}, bf16[4,256,256]{2,1,0:T(8,128)(2,1)S(1)}, u32[]{:S(2)}, u32[]{:S(2)}) collective-permute-start(bf16[4,256,256]{2,1,0:T(8,128)(2,1)S(1)} %get-tuple-element.23), channel_id=1, source_target_pairs={{0,24},{1,25},{2,26},{3,27},{4,28},{5,29},{6,30},{7,31},{8,16},{9,... | collective-permute-start | bytes 1572872 | tf_op jit(solution)/shard_map/ppermute | solution.py:312
  20.7 3.3 %row_grads.1 = bf16[512,1024]{1,0:T(8,128)(2,1)} custom-call(bf16[512,1024]{1,0:T(8,128)(2,1)S(1)} %get-tuple-element.16.keep_ref, bf16[512,1024]{1,0:T(8,128)(2,1)S(1)} %get-tuple-element.19.send_ref, bf16[1024,2048]{1,0:T(8,128)(2,1)S(1)} %copy-done), custom_call_target="tpu_custom_call" | custom-call | flops 2147483648 | bytes 7340032 | tf_op jit(solution)/shard_map/row_grads/pallas_call | solution.py:268
  24.1 0.5 pair_weight_grads.5
  24.5 1.9 %collective-permute-done.2 = bf16[4,256,256]{2,1,0:T(8,128)(2,1)S(1)} collective-permute-done((bf16[4,256,256]{2,1,0:T(8,128)(2,1)S(1)}, bf16[4,256,256]{2,1,0:T(8,128)(2,1)S(1)}, u32[]{:S(2)}, u32[]{:S(2)}) %collective-permute-start.2) | collective-permute-done | bytes 524320 | tf_op jit(solution)/shard_map/ppermute | solution.py:312
  26.5 4.2 %collective-permute-done.3 = bf16[4,256,256]{2,1,0:T(8,128)(2,1)S(1)} collective-permute-done((bf16[4,256,256]{2,1,0:T(8,128)(2,1)S(1)}, bf16[4,256,256]{2,1,0:T(8,128)(2,1)S(1)}, u32[]{:S(2)}, u32[]{:S(2)}) %collective-permute-start.3) | collective-permute-done | bytes 524320 | tf_op jit(solution)/shard_map/ppermute | solution.py:312
  30.7 1.3 %collective-permute-done.4 = bf16[4,256,256]{2,1,0:T(8,128)(2,1)S(1)} collective-permute-done((bf16[4,256,256]{2,1,0:T(8,128)(2,1)S(1)}, bf16[4,256,256]{2,1,0:T(8,128)(2,1)S(1)}, u32[]{:S(2)}, u32[]{:S(2)}) %collective-permute-start.4) | collective-permute-done | bytes 524320 | tf_op jit(solution)/shard_map/ppermute | solution.py:312
  32.2 1.5 %collective-permute-start.7 = (bf16[256,256]{1,0:T(8,128)(2,1)S(1)}, bf16[256,256]{1,0:T(8,128)(2,1)S(1)}, u32[]{:S(2)}, u32[]{:S(2)}) collective-permute-start(bf16[256,256]{1,0:T(8,128)(2,1)S(1)} %get-tuple-element.33), channel_id=1, source_target_pairs={{0,128},{1,129},{2,130},{3,131},{4,132},{5,133},{6,134},{7,135},{8... | collective-permute-start | bytes 393224 | tf_op jit(solution)/shard_map/ppermute | solution.py:312
  33.7 0.9 %collective-permute-start.6 = (bf16[256,256]{1,0:T(8,128)(2,1)S(1)}, bf16[256,256]{1,0:T(8,128)(2,1)S(1)}, u32[]{:S(2)}, u32[]{:S(2)}) collective-permute-start(bf16[256,256]{1,0:T(8,128)(2,1)S(1)} %get-tuple-element.34), channel_id=1, source_target_pairs={{0,192},{1,193},{2,194},{3,195},{4,196},{5,197},{6,198},{7,199},{8... | collective-permute-start | bytes 393224 | tf_op jit(solution)/shard_map/ppermute | solution.py:312
  34.6 0.4 collective-permute-start.5
  35.0 2.7 %collective-permute-done.7 = bf16[256,256]{1,0:T(8,128)(2,1)S(1)} collective-permute-done((bf16[256,256]{1,0:T(8,128)(2,1)S(1)}, bf16[256,256]{1,0:T(8,128)(2,1)S(1)}, u32[]{:S(2)}, u32[]{:S(2)}) %collective-permute-start.7) | collective-permute-done | bytes 131104 | tf_op jit(solution)/shard_map/ppermute | solution.py:312
  37.7 1.7 %collective-permute-done.6 = bf16[256,256]{1,0:T(8,128)(2,1)S(1)} collective-permute-done((bf16[256,256]{1,0:T(8,128)(2,1)S(1)}, bf16[256,256]{1,0:T(8,128)(2,1)S(1)}, u32[]{:S(2)}, u32[]{:S(2)}) %collective-permute-start.6) | collective-permute-done | bytes 131104 | tf_op jit(solution)/shard_map/ppermute | solution.py:312
  39.5 3.8 %collective-permute-start.10 = (bf16[2,32,256]{2,1,0:T(8,128)(2,1)S(1)}, bf16[2,32,256]{2,1,0:T(8,128)(2,1)S(1)}, u32[]{:S(2)}, u32[]{:S(2)}) collective-permute-start(bf16[2,32,256]{2,1,0:T(8,128)(2,1)S(1)} %pad_maximum_fusion.2), channel_id=1, source_target_pairs={{0,3},{1,2},{2,1},{3,0},{4,7},{5,6},{6,5},{7,4},{8,11},{9,10},{10,... | collective-permute-start | bytes 98312 | tf_op jit(solution)/shard_map/ppermute | solution.py:312
  43.4 0.4 collective-permute-start.8
  43.8 0.9 %collective-permute-done.10 = bf16[2,32,256]{2,1,0:T(8,128)(2,1)S(1)} collective-permute-done((bf16[2,32,256]{2,1,0:T(8,128)(2,1)S(1)}, bf16[2,32,256]{2,1,0:T(8,128)(2,1)S(1)}, u32[]{:S(2)}, u32[]{:S(2)}) %collective-permute-start.10) | collective-permute-done | bytes 32800 | tf_op jit(solution)/shard_map/ppermute | solution.py:312
  44.7 2.8 %collective-permute-done.9 = bf16[2,32,256]{2,1,0:T(8,128)(2,1)S(1)} collective-permute-done((bf16[2,32,256]{2,1,0:T(8,128)(2,1)S(1)}, bf16[2,32,256]{2,1,0:T(8,128)(2,1)S(1)}, u32[]{:S(2)}, u32[]{:S(2)}) %collective-permute-start.9) | collective-permute-done | bytes 32800 | tf_op jit(solution)/shard_map/ppermute | solution.py:312
  47.5 2.5 %collective-permute-start.11 = (f32[32,256]{1,0:T(8,128)S(1)}, f32[32,256]{1,0:T(8,128)S(1)}, u32[]{:S(2)}, u32[]{:S(2)}) collective-permute-start(f32[32,256]{1,0:T(8,128)S(1)} %slice_bitcast_fusion), channel_id=1, source_target_pairs={{0,7},{1,6},{2,5},{3,4},{4,3},{5,2},{6,1},{7,0},{8,15},{9,14},{10,... | collective-permute-start | bytes 98312 | tf_op jit(solution)/shard_map/ppermute | solution.py:312
  50.0 1.6 %collective-permute-done.11 = f32[32,256]{1,0:T(8,128)S(1)} collective-permute-done((f32[32,256]{1,0:T(8,128)S(1)}, f32[32,256]{1,0:T(8,128)S(1)}, u32[]{:S(2)}, u32[]{:S(2)}) %collective-permute-start.11) | collective-permute-done | bytes 32800 | tf_op jit(solution)/shard_map/ppermute | solution.py:312
  51.6 4.7 %collective-permute-start.12 = (bf16[32,256]{1,0:T(8,128)(2,1)S(1)}, bf16[32,256]{1,0:T(8,128)(2,1)S(1)}, u32[]{:S(2)}, u32[]{:S(2)}) collective-permute-start(bf16[32,256]{1,0:T(8,128)(2,1)S(1)} %fusion.8), channel_id=1, source_target_pairs={{0,32},{1,33},{2,34},{3,35},{4,36},{5,37},{6,38},{7,39},{8,40},{9,... | collective-permute-start | bytes 49160 | tf_op jit(solution)/shard_map/ppermute | solution.py:312
  56.3 0.8 %collective-permute-done.12 = bf16[32,256]{1,0:T(8,128)(2,1)S(1)} collective-permute-done((bf16[32,256]{1,0:T(8,128)(2,1)S(1)}, bf16[32,256]{1,0:T(8,128)(2,1)S(1)}, u32[]{:S(2)}, u32[]{:S(2)}) %collective-permute-start.12) | collective-permute-done | bytes 16416 | tf_op jit(solution)/shard_map/ppermute | solution.py:312
  57.1 2.7 %collective-permute-start.14 = (bf16[2,32,256]{2,1,0:T(8,128)(2,1)S(1)}, bf16[2,32,256]{2,1,0:T(8,128)(2,1)S(1)}, u32[]{:S(2)}, u32[]{:S(2)}) collective-permute-start(bf16[2,32,256]{2,1,0:T(8,128)(2,1)S(1)} %pad_maximum_fusion.3.p0), channel_id=1, source_target_pairs={{0,128},{1,129},{2,130},{3,131},{4,132},{5,133},{6,134},{7,135},{8... | collective-permute-start | bytes 98312 | tf_op jit(solution)/shard_map/ppermute | solution.py:312
  59.8 1.2 %collective-permute-start.15 = (bf16[2,32,256]{2,1,0:T(8,128)(2,1)S(1)}, bf16[2,32,256]{2,1,0:T(8,128)(2,1)S(1)}, u32[]{:S(2)}, u32[]{:S(2)}) collective-permute-start(bf16[2,32,256]{2,1,0:T(8,128)(2,1)S(1)} %pad_maximum_fusion.3.p0), channel_id=1, source_target_pairs={{0,192},{1,193},{2,194},{3,195},{4,196},{5,197},{6,198},{7,199},{8... | collective-permute-start | bytes 98312 | tf_op jit(solution)/shard_map/ppermute | solution.py:312
  61.0 0.5 collective-permute-done.14.p2
  61.5 2.3 %collective-permute-done.15.p3 = bf16[2,32,256]{2,1,0:T(8,128)(2,1)S(1)} collective-permute-done((bf16[2,32,256]{2,1,0:T(8,128)(2,1)S(1)}, bf16[2,32,256]{2,1,0:T(8,128)(2,1)S(1)}, u32[]{:S(2)}, u32[]{:S(2)}) %collective-permute-start.15) | collective-permute-done | bytes 32800 | tf_op jit(solution)/shard_map/ppermute | solution.py:312
  63.8 0.7 %place_columns.1 = f32[32,2048]{1,0:T(8,128)} custom-call(bf16[2,32,256]{2,1,0:T(8,128)(2,1)S(1)} %pad_maximum_fusion.3.p0, bf16[2,32,256]{2,1,0:T(8,128)(2,1)S(1)} %collective-permute-done.13.p1, bf16[2,32,256]{2,1,0:T(8,128)(2,1)S(1)} %collective-permute-done.14.p2, bf16[2,32,256]{2,1,0:T(8,128)(2,1)S(1)} %collective-permute-done.15.p3), custom_call_target="tpu_custom_call" | custom-call | tf_op jit(solution)/shard_map/place_columns/pallas_call | solution.py:290
  (22 shorter events, 0.6 us)
Async XLA Ops:
  0.6 12.9 %copy-start.1 = (bf16[512,1024]{1,0:T(8,128)(2,1)S(1)}, bf16[512,1024]{1,0:T(8,128)(2,1)}, u32[]{:S(2)}) copy-start(bf16[512,1024]{1,0:T(8,128)(2,1)} %x_ref.1) | copy-start | bytes 3145732
  0.6 12.8 %collective-permute-start = (bf16[512,1024]{1,0:T(8,128)(2,1)}, bf16[512,1024]{1,0:T(8,128)(2,1)S(1)}, u32[]{:S(2)}, u32[]{:S(2)}) collective-permute-start(bf16[512,1024]{1,0:T(8,128)(2,1)} %x_ref.1), channel_id=1, source_target_pairs={{0,32},{1,33},{2,34},{3,35},{4,36},{5,37},{6,38},{7,39},{8,40},{9,... | collective-permute-start | bytes 3145736 | tf_op jit(solution)/shard_map/ppermute | solution.py:312
  13.3 2.7 %collective-permute-start.1 = (bf16[512,1024]{1,0:T(8,128)(2,1)S(1)}, bf16[512,1024]{1,0:T(8,128)(2,1)S(1)}, u32[]{:S(2)}, u32[]{:S(2)}) collective-permute-start(bf16[512,1024]{1,0:T(8,128)(2,1)S(1)} %get-tuple-element.19.send_ref), channel_id=1, source_target_pairs={{0,32},{1,33},{2,34},{3,35},{4,36},{5,37},{6,38},{7,39},{8,40},{9,... | collective-permute-start | bytes 3145736 | tf_op jit(solution)/shard_map/ppermute | solution.py:312
  15.1 5.6 %copy-start = (bf16[1024,2048]{1,0:T(8,128)(2,1)S(1)}, bf16[1024,2048]{1,0:T(8,128)(2,1)}, u32[]{:S(2)}) copy-start(bf16[1024,2048]{1,0:T(8,128)(2,1)} %w_ref.1) | copy-start | bytes 12582916
  16.5 10.0 %collective-permute-start.2 = (bf16[4,256,256]{2,1,0:T(8,128)(2,1)S(1)}, bf16[4,256,256]{2,1,0:T(8,128)(2,1)S(1)}, u32[]{:S(2)}, u32[]{:S(2)}) collective-permute-start(bf16[4,256,256]{2,1,0:T(8,128)(2,1)S(1)} %pair_weight_grads.3), channel_id=1, source_target_pairs={{0,16},{1,17},{2,18},{3,19},{4,20},{5,21},{6,22},{7,23},{8,24},{9,... | collective-permute-start | bytes 1572872 | tf_op jit(solution)/shard_map/ppermute | solution.py:312
  18.6 12.1 %collective-permute-start.3 = (bf16[4,256,256]{2,1,0:T(8,128)(2,1)S(1)}, bf16[4,256,256]{2,1,0:T(8,128)(2,1)S(1)}, u32[]{:S(2)}, u32[]{:S(2)}) collective-permute-start(bf16[4,256,256]{2,1,0:T(8,128)(2,1)S(1)} %get-tuple-element.22), channel_id=1, source_target_pairs={{0,8},{1,9},{2,10},{3,11},{4,12},{5,13},{6,14},{7,15},{8,0},{9,1},... | collective-permute-start | bytes 1572872 | tf_op jit(solution)/shard_map/ppermute | solution.py:312
  19.0 13.0 %collective-permute-start.4 = (bf16[4,256,256]{2,1,0:T(8,128)(2,1)S(1)}, bf16[4,256,256]{2,1,0:T(8,128)(2,1)S(1)}, u32[]{:S(2)}, u32[]{:S(2)}) collective-permute-start(bf16[4,256,256]{2,1,0:T(8,128)(2,1)S(1)} %get-tuple-element.23), channel_id=1, source_target_pairs={{0,24},{1,25},{2,26},{3,27},{4,28},{5,29},{6,30},{7,31},{8,16},{9,... | collective-permute-start | bytes 1572872 | tf_op jit(solution)/shard_map/ppermute | solution.py:312
  32.2 5.4 %collective-permute-start.7 = (bf16[256,256]{1,0:T(8,128)(2,1)S(1)}, bf16[256,256]{1,0:T(8,128)(2,1)S(1)}, u32[]{:S(2)}, u32[]{:S(2)}) collective-permute-start(bf16[256,256]{1,0:T(8,128)(2,1)S(1)} %get-tuple-element.33), channel_id=1, source_target_pairs={{0,128},{1,129},{2,130},{3,131},{4,132},{5,133},{6,134},{7,135},{8... | collective-permute-start | bytes 393224 | tf_op jit(solution)/shard_map/ppermute | solution.py:312
  33.7 5.6 %collective-permute-start.6 = (bf16[256,256]{1,0:T(8,128)(2,1)S(1)}, bf16[256,256]{1,0:T(8,128)(2,1)S(1)}, u32[]{:S(2)}, u32[]{:S(2)}) collective-permute-start(bf16[256,256]{1,0:T(8,128)(2,1)S(1)} %get-tuple-element.34), channel_id=1, source_target_pairs={{0,192},{1,193},{2,194},{3,195},{4,196},{5,197},{6,198},{7,199},{8... | collective-permute-start | bytes 393224 | tf_op jit(solution)/shard_map/ppermute | solution.py:312
  34.6 4.8 %collective-permute-start.5 = (bf16[256,256]{1,0:T(8,128)(2,1)S(1)}, bf16[256,256]{1,0:T(8,128)(2,1)S(1)}, u32[]{:S(2)}, u32[]{:S(2)}) collective-permute-start(bf16[256,256]{1,0:T(8,128)(2,1)S(1)} %get-tuple-element.32), channel_id=1, source_target_pairs={{0,64},{1,65},{2,66},{3,67},{4,68},{5,69},{6,70},{7,71},{8,72},{9,... | collective-permute-start | bytes 393224 | tf_op jit(solution)/shard_map/ppermute | solution.py:312
  39.5 5.1 %collective-permute-start.10 = (bf16[2,32,256]{2,1,0:T(8,128)(2,1)S(1)}, bf16[2,32,256]{2,1,0:T(8,128)(2,1)S(1)}, u32[]{:S(2)}, u32[]{:S(2)}) collective-permute-start(bf16[2,32,256]{2,1,0:T(8,128)(2,1)S(1)} %pad_maximum_fusion.2), channel_id=1, source_target_pairs={{0,3},{1,2},{2,1},{3,0},{4,7},{5,6},{6,5},{7,4},{8,11},{9,10},{10,... | collective-permute-start | bytes 98312 | tf_op jit(solution)/shard_map/ppermute | solution.py:312
  43.4 4.1 %collective-permute-start.9 = (bf16[2,32,256]{2,1,0:T(8,128)(2,1)S(1)}, bf16[2,32,256]{2,1,0:T(8,128)(2,1)S(1)}, u32[]{:S(2)}, u32[]{:S(2)}) collective-permute-start(bf16[2,32,256]{2,1,0:T(8,128)(2,1)S(1)} %pad_maximum_fusion.1), channel_id=1, source_target_pairs={{0,2},{1,3},{2,0},{3,1},{4,6},{5,7},{6,4},{7,5},{8,10},{9,11},{10,... | collective-permute-start | bytes 98312 | tf_op jit(solution)/shard_map/ppermute | solution.py:312
  43.4 4.1 %collective-permute-start.8 = (bf16[2,32,256]{2,1,0:T(8,128)(2,1)S(1)}, bf16[2,32,256]{2,1,0:T(8,128)(2,1)S(1)}, u32[]{:S(2)}, u32[]{:S(2)}) collective-permute-start(bf16[2,32,256]{2,1,0:T(8,128)(2,1)S(1)} %pad_maximum_fusion), channel_id=1, source_target_pairs={{0,1},{1,0},{2,3},{3,2},{4,5},{5,4},{6,7},{7,6},{8,9},{9,8},{10,11... | collective-permute-start | bytes 98312 | tf_op jit(solution)/shard_map/ppermute | solution.py:312
  47.5 4.1 %collective-permute-start.11 = (f32[32,256]{1,0:T(8,128)S(1)}, f32[32,256]{1,0:T(8,128)S(1)}, u32[]{:S(2)}, u32[]{:S(2)}) collective-permute-start(f32[32,256]{1,0:T(8,128)S(1)} %slice_bitcast_fusion), channel_id=1, source_target_pairs={{0,7},{1,6},{2,5},{3,4},{4,3},{5,2},{6,1},{7,0},{8,15},{9,14},{10,... | collective-permute-start | bytes 98312 | tf_op jit(solution)/shard_map/ppermute | solution.py:312
  51.6 5.5 %collective-permute-start.12 = (bf16[32,256]{1,0:T(8,128)(2,1)S(1)}, bf16[32,256]{1,0:T(8,128)(2,1)S(1)}, u32[]{:S(2)}, u32[]{:S(2)}) collective-permute-start(bf16[32,256]{1,0:T(8,128)(2,1)S(1)} %fusion.8), channel_id=1, source_target_pairs={{0,32},{1,33},{2,34},{3,35},{4,36},{5,37},{6,38},{7,39},{8,40},{9,... | collective-permute-start | bytes 49160 | tf_op jit(solution)/shard_map/ppermute | solution.py:312
  57.1 3.9 %collective-permute-start.13 = (bf16[2,32,256]{2,1,0:T(8,128)(2,1)S(1)}, bf16[2,32,256]{2,1,0:T(8,128)(2,1)S(1)}, u32[]{:S(2)}, u32[]{:S(2)}) collective-permute-start(bf16[2,32,256]{2,1,0:T(8,128)(2,1)S(1)} %pad_maximum_fusion.3.p0), channel_id=1, source_target_pairs={{0,64},{1,65},{2,66},{3,67},{4,68},{5,69},{6,70},{7,71},{8,72},{9,... | collective-permute-start | bytes 98312 | tf_op jit(solution)/shard_map/ppermute | solution.py:312
  57.1 4.4 %collective-permute-start.14 = (bf16[2,32,256]{2,1,0:T(8,128)(2,1)S(1)}, bf16[2,32,256]{2,1,0:T(8,128)(2,1)S(1)}, u32[]{:S(2)}, u32[]{:S(2)}) collective-permute-start(bf16[2,32,256]{2,1,0:T(8,128)(2,1)S(1)} %pad_maximum_fusion.3.p0), channel_id=1, source_target_pairs={{0,128},{1,129},{2,130},{3,131},{4,132},{5,133},{6,134},{7,135},{8... | collective-permute-start | bytes 98312 | tf_op jit(solution)/shard_map/ppermute | solution.py:312
  59.8 4.0 %collective-permute-start.15 = (bf16[2,32,256]{2,1,0:T(8,128)(2,1)S(1)}, bf16[2,32,256]{2,1,0:T(8,128)(2,1)S(1)}, u32[]{:S(2)}, u32[]{:S(2)}) collective-permute-start(bf16[2,32,256]{2,1,0:T(8,128)(2,1)S(1)} %pad_maximum_fusion.3.p0), channel_id=1, source_target_pairs={{0,192},{1,193},{2,194},{3,195},{4,196},{5,197},{6,198},{7,199},{8... | collective-permute-start | bytes 98312 | tf_op jit(solution)/shard_map/ppermute | solution.py:312

commit v5 on v4

--- a/solution.py
+++ b/solution.py
@@ -24,9 +24,53 @@
     return group // 2, group % 2, member // NZ, member % NZ
 
 
-def grads_kernel(len_hbm, x_hbm, w_hbm, cot_hbm, keep_ref, send_ref,
-                 len_ref, x_ref, w_ref, cot_ref, slope_ref, act_ref, mask_ref, p_ref, s_ref, ds_ref,
-                 att_ref, da_ref, g_ref, sems):
+def spans(i):
+    first = max(0, i - 2)
+    return pl.ds(i * BLOCK, BLOCK), pl.ds(first * BLOCK, (i + 1 - first) * BLOCK), first
+
+
+def col(s, h):
+    return pl.ds(pl.multiple_of((s * HEADS + h) * BLOCK, BLOCK), BLOCK)
+
+
+def head(h):
+    return col(0, h)
+
+
+def store(s, j, out_ref, h, r, slope_ref, grad):
+    if s == 0:
+        grad = grad[r, head(h)]
+    value = grad.astype(jnp.bfloat16).astype(jnp.float32) * slope_ref[r, col(s, h)]
+    out_ref[r, pl.ds((s * (HEADS // 2) + j) * BLOCK, BLOCK)] = value.astype(jnp.bfloat16)
+
+
+def backward(side, out_ref, slope_ref, act_ref, p_ref, s_ref, ds_ref, da_ref):
+    nblocks = act_ref.shape[0] // BLOCK
+    scale = BLOCK ** -0.5
+    heads = [(j, side * (HEADS // 2) + j) for j in range(HEADS // 2)]
+    for i in range(nblocks):
+        r, keys, _ = spans(i)
+        for j, h in heads:
+            dp = mm(da_ref[r, head(h)], act_ref[keys, col(1, h)], NT)
+            ds_ref[j, r, keys] = (dp * s_ref[h, r, keys]).astype(jnp.bfloat16)
+    for i in range(nblocks):
+        r, keys, _ = spans(i)
+        for j, h in heads:
+            dq = mm(ds_ref[j, r, keys], act_ref[keys, col(3, h)]) * scale
+            store(2, j, out_ref, h, r, slope_ref, dq)
+    for b in range(nblocks):
+        last = min(nblocks, b + 3)
+        r = pl.ds(b * BLOCK, BLOCK)
+        qs = pl.ds(b * BLOCK, (last - b) * BLOCK)
+        for j, h in heads:
+            dv = mm(p_ref[h, qs, r], da_ref[qs, head(h)], TN)
+            store(1, j, out_ref, h, r, slope_ref, dv)
+            dk = mm(ds_ref[j, qs, r], act_ref[qs, col(2, h)], TN) * scale
+            store(3, j, out_ref, h, r, slope_ref, dk)
+
+
+def grads_kernel(len_hbm, x_hbm, w_hbm, cot_hbm, send_ref, keep_u_ref, slope_ref, act_ref, p_ref, s_ref, da_ref,
+                 len_ref, x_ref, w_ref, cot_ref, mask_ref, ds_ref, att_ref, sems):
     rows, width = cot_ref.shape
     nblocks = rows // BLOCK
     size = width // HEADS
@@ -52,10 +96,6 @@
     l1 = len_ref[1]
     start1 = ((l0 + (BLOCK - 1)) // BLOCK) * BLOCK
 
-    def spans(i):
-        first = max(0, i - 2)
-        return pl.ds(i * BLOCK, BLOCK), pl.ds(first * BLOCK, (i + 1 - first) * BLOCK), first
-
     def row_facts(i):
         row = i * BLOCK + lax.broadcasted_iota(jnp.int32, (BLOCK, 1), 0)
         in0 = row < l0
@@ -80,18 +120,7 @@
         act_ref[:, section(s)] = act.astype(bf16)
         slope_ref[:, section(s)] = sig + act * (1.0 - sig)
 
-    def col(s, h):
-        return pl.ds(s * width + h * size, size)
-
-    def head(h):
-        return pl.ds(h * size, size)
-
     core = position()[1]
-
-    def put(s, h, r, grad):
-        value = grad.astype(bf16).astype(jnp.float32) * slope_ref[r, col(s, h)]
-        to = s * half + (h % (HEADS // 2)) * size
-        g_ref[(h // (HEADS // 2)) ^ core, r, pl.ds(to, size)] = value.astype(bf16)
 
     load_x.wait()
     loads[1].start()
@@ -125,26 +154,11 @@
         m2 = jnp.mean(dz * z, axis=1, keepdims=True)
         da_ref[r, :] = ((dz - m1 - z * m2) * rstd).astype(bf16)
         du = up * z
-        for h in range(HEADS):
-            put(0, h, r, du[:, h * size:(h + 1) * size])
-    for i in range(nblocks):
-        r, keys, _ = spans(i)
-        for h in range(HEADS):
-            dp = mm(da_ref[r, head(h)], act_ref[keys, col(1, h)], NT)
-            ds_ref[h, r, keys] = (dp * s_ref[h, r, keys]).astype(bf16)
-    for i in range(nblocks):
-        r, keys, _ = spans(i)
-        for h in range(HEADS):
-            put(2, h, r, mm(ds_ref[h, r, keys], act_ref[keys, col(3, h)]) * scale)
-    for j in range(nblocks):
-        last = min(nblocks, j + 3)
-        r = pl.ds(j * BLOCK, BLOCK)
-        qs = pl.ds(j * BLOCK, (last - j) * BLOCK)
-        for h in range(HEADS):
-            put(1, h, r, mm(p_ref[h, qs, r], da_ref[qs, head(h)], TN))
-            put(3, h, r, mm(ds_ref[h, qs, r], act_ref[qs, col(2, h)], TN) * scale)
-    keep_ref[...] = g_ref[0]
-    send_ref[...] = g_ref[1]
+        att_ref[r, :] = up * z
+    for j in range(HEADS // 2):
+        store(0, j, send_ref, (1 - core) * (HEADS // 2) + j, pl.ds(0, rows), slope_ref, att_ref)
+        store(0, j, keep_u_ref, core * (HEADS // 2) + j, pl.ds(0, rows), slope_ref, att_ref)
+    backward(1 - core, send_ref, slope_ref, act_ref, p_ref, s_ref, ds_ref, da_ref)
 
 
 def grads(lengths, x, w, cot):
@@ -155,26 +169,28 @@
     hbm = pl.BlockSpec(memory_space=pl.ANY)
     return pl.pallas_call(
         grads_kernel,
-        out_shape=[pltpu.VMEM((rows, wide // 2), jnp.bfloat16)] * 2,
+        out_shape=[
+            pltpu.VMEM((rows, wide // 2), jnp.bfloat16),
+            pltpu.VMEM((rows, width // 2), jnp.bfloat16),
+            pltpu.VMEM((rows, wide), jnp.float32),
+            pltpu.VMEM((rows, wide), jnp.bfloat16),
+            pltpu.VMEM((HEADS, rows, rows), jnp.bfloat16),
+            pltpu.VMEM((HEADS, rows, rows), jnp.float32),
+            pltpu.VMEM((rows, width), jnp.bfloat16),
+        ],
         in_specs=[hbm] * 4,
-        out_specs=[vmem, vmem],
+        out_specs=[vmem] * 7,
         scratch_shapes=[
             pltpu.SMEM((2,), jnp.int32),
             pltpu.VMEM((rows, d), jnp.bfloat16),
             pltpu.VMEM((d, wide), jnp.bfloat16),
             pltpu.VMEM((rows, width), jnp.bfloat16),
-            pltpu.VMEM((rows, wide), jnp.float32),
-            pltpu.VMEM((rows, wide), jnp.bfloat16),
             pltpu.VMEM((rows, rows), jnp.float32),
-            pltpu.VMEM((HEADS, rows, rows), jnp.bfloat16),
-            pltpu.VMEM((HEADS, rows, rows), jnp.float32),
-            pltpu.VMEM((HEADS, rows, rows), jnp.bfloat16),
+            pltpu.VMEM((HEADS // 2, rows, rows), jnp.bfloat16),
             pltpu.VMEM((rows, width), jnp.float32),
-            pltpu.VMEM((rows, width), jnp.bfloat16),
-            pltpu.VMEM((2, rows, wide // 2), jnp.bfloat16),
             pltpu.SemaphoreType.DMA((7,)),
         ],
-        compiler_params=pltpu.CompilerParams(vmem_limit_bytes=40 * 2**20),
+        compiler_params=pltpu.CompilerParams(vmem_limit_bytes=32 * 2**20),
         cost_estimate=pl.CostEstimate(flops=4 * 10**9, bytes_accessed=8 * 10**6, transcendentals=2 * 10**6),
         name="uvqk_grads",
     )(*[pltpu.with_memory_space_constraint(v, pltpu.HBM) for v in (lengths, x, w, cot)])
@@ -204,27 +220,36 @@
             yield k, l, pl.ds(pl.multiple_of(rb * 256, 256), 256), pl.ds(pl.multiple_of(cb * 256, 256), 256)
 
 
-def own_kernel(x_ref, theirs_ref, keep_ref, a0, a1, a2, a3, xt_ref, own_ref):
+def own_kernel(x_ref, theirs_ref, keep_u_ref, slope_ref, act_ref, p_ref, s_ref, da_ref,
+               keep_ref, a0, a1, a2, a3, xt_ref, own_ref, ds_ref):
     flip(x_ref, own_ref)
+    core = position()[1]
+    keep_ref[:, pl.ds(0, keep_u_ref.shape[1])] = keep_u_ref[...]
+    backward(core, keep_ref, slope_ref, act_ref, p_ref, s_ref, ds_ref, da_ref)
     sums = (a0, a1, a2, a3)
     for k, l, rs, cs in blocks_of():
         sums[k][l] = mm(own_ref[rs, :], keep_ref[:, cs])
     flip(theirs_ref, xt_ref)
 
 
-def own_part(x, theirs, keep):
+def own_part(x, theirs, *state):
     rows, d = x.shape
     vmem = pl.BlockSpec(memory_space=pltpu.VMEM)
     return pl.pallas_call(
         own_kernel,
-        out_shape=[pltpu.VMEM((4, 256, 256), jnp.float32)] * 4 + [pltpu.VMEM((d, rows), jnp.bfloat16)],
-        in_specs=[vmem] * 3,
-        out_specs=[vmem] * 5,
-        scratch_shapes=[pltpu.VMEM((d, rows), jnp.bfloat16)],
-        compiler_params=pltpu.CompilerParams(vmem_limit_bytes=24 * 2**20),
-        cost_estimate=pl.CostEstimate(flops=2**30, bytes_accessed=6 * 2**20, transcendentals=0),
+        out_shape=[pltpu.VMEM((rows, d), jnp.bfloat16)]
+        + [pltpu.VMEM((4, 256, 256), jnp.float32)] * 4
+        + [pltpu.VMEM((d, rows), jnp.bfloat16)],
+        in_specs=[vmem] * 8,
+        out_specs=[vmem] * 6,
+        scratch_shapes=[
+            pltpu.VMEM((d, rows), jnp.bfloat16),
+            pltpu.VMEM((HEADS // 2, rows, rows), jnp.bfloat16),
+        ],
+        compiler_params=pltpu.CompilerParams(vmem_limit_bytes=32 * 2**20),
+        cost_estimate=pl.CostEstimate(flops=14 * 10**8, bytes_accessed=20 * 2**20, transcendentals=0),
         name="own_weight_grads",
-    )(x, theirs, keep)
+    )(x, theirs, *state)
 
 
 def pair_kernel(ks, *refs):
@@ -338,21 +363,22 @@
 
 def shards(histories, lengths, cotangent, w_in):
     theirs = permute(histories, other_core)
-    keep, send = grads(lengths, histories, w_in, cotangent)
+    send, *state = grads(lengths, histories, w_in, cotangent)
     recv = permute(send, other_core)
-    *sums, xt = own_part(histories, theirs, keep)
+    keep, *sums, xt = own_part(histories, theirs, *state)
     far, = pair_part((2,), sums, xt, recv)
-    near, last = pair_part((1, 3), sums, xt, recv)
+    near, = pair_part((1,), sums, xt, recv)
+    last, = pair_part((3,), sums, xt, recv)
     moved = [permute(part, first_axis(k)) for k, part in ((2, far), (1, near), (3, last))]
     mine, = pair_part((0,), sums, xt, recv)
     grad_rows = row_grads(keep, send, w_in)
     *moved, mine, grad_rows = lax.optimization_barrier((*moved, mine, grad_rows))
     summed = [f32(mine[l]) + f32(moved[0][l]) + f32(moved[1][l]) + f32(moved[2][l]) for l in range(4)]
-    moved = [permute(summed[k].astype(jnp.bfloat16), second_axis(k)) for k in (1, 3, 2)]
+    moved = [permute(summed[k].astype(jnp.bfloat16), second_axis(k)) for k in (2, 1, 3)]
     block = summed[0] + f32(moved[0]) + f32(moved[1]) + f32(moved[2])
     block = block.reshape(NZ, 32, 256)
     ends = jnp.stack([block[0], block[7]])
-    moved = [permute(jnp.stack([block[m], block[7 - m]]).astype(jnp.bfloat16), along_z(m)) for m in (1, 2, 3)]
+    moved = [permute(jnp.stack([block[m], block[7 - m]]).astype(jnp.bfloat16), along_z(m)) for m in (1, 3, 2)]
     ends = ends + f32(moved[0]) + f32(moved[1]) + f32(moved[2])
     block = ends[0] + permute(ends[1], along_z(7))
 

time: 65.7 us -> 64.2 us (0.977)
  waiting for transfers between devices: 21.8 us -> 20.2 us
    ppermute x16, waiting for transfers between devices: 21.8 us -> 20.2 us  [permute(): return lax.ppermute(value, AXES, pairs(move))]
    pallas_call x1, Pallas kernels: 1.61 us -> 2.57 us  [own_part(): pl.pallas_call(own_kernel, out_shape=[pltpu.VMEM((rows, d), jnp.bfloat16)...]
    pallas_call x3 -> x4, Pallas kernels: 1.69 us -> 1.85 us  [pair_part(): pl.pallas_call(functools.partial(pair_kernel, ks), out_shape=[pltpu.VMEM(...]
  transfers between devices with their start and end apart: 16 -> 16, of which waited for: 12 -> 11; matrix products, arithmetic and copies ran while one was open for 0% -> 0% of each run, Pallas kernels for 24% -> 25%
where the time goes in v5:
time: 64.2 us; the launch traced here: 63.5 us
  starting transfers between devices  24.9 us (39%)
  waiting for transfers between devices  20.2 us (31%)
  Pallas kernels  17.2 us (27%)
  between operations  0.76 us (1%)
    ppermute x16, starting transfers between devices, permute(): return lax.ppermute(value, AXES, pairs(move))  24.9 us
    ppermute x16, waiting for transfers between devices, permute(): return lax.ppermute(value, AXES, pairs(move))  20.2 us
    pallas_call x1, Pallas kernels, grads(): pl.pallas_call(grads_kernel, out_shape=[pltpu.VMEM((rows, wide // 2), jnp...  8.69 us
    pallas_call x1, Pallas kernels, row_grads(): pl.pallas_call(rows_kernel, out_shape=jax.ShapeDtypeStruct((keep.shape[0]...  3.36 us
    pallas_call x1, Pallas kernels, own_part(): pl.pallas_call(own_kernel, out_shape=[pltpu.VMEM((rows, d), jnp.bfloat16)...  2.57 us
    pallas_call x4, Pallas kernels, pair_part(): pl.pallas_call(functools.partial(pair_kernel, ks), out_shape=[pltpu.VMEM(...  1.85 us
  transfers between devices with their start and end apart: 16, of which 11 were waited for; matrix products, arithmetic and copies ran while one was open for 0% of the time, Pallas kernels for 25%

profile of v5, /device:TPU:1, one launch (start us, length us, event | category | flops | bytes accessed | tf_op | source)
XLA Modules:
  0.0 63.5 jit_solution(7113090020928757093)
XLA Ops:
  0.6 3.3 %collective-permute-start = (bf16[512,1024]{1,0:T(8,128)(2,1)}, bf16[512,1024]{1,0:T(8,128)(2,1)S(1)}, u32[]{:S(2)}, u32[]{:S(2)}) collective-permute-start(bf16[512,1024]{1,0:T(8,128)(2,1)} %x_ref.1), channel_id=1, source_target_pairs={{0,32},{1,33},{2,34},{3,35},{4,36},{5,37},{6,38},{7,39},{8,40},{9,... | collective-permute-start | bytes 3145736 | tf_op jit(solution)/shard_map/ppermute | solution.py:337
  4.0 8.7 %uvqk_grads.1 = (bf16[512,1024]{1,0:T(8,128)(2,1)S(1)}, bf16[512,256]{1,0:T(8,128)(2,1)S(1)}, f32[512,2048]{1,0:T(8,128)S(1)}, bf16[512,2048]{1,0:T(8,128)(2,1)S...) custom-call(s32[2]{0:T(128)} %len_hbm.1, ...), custom_call_target="tpu_custom_call" | custom-call | flops 4000000000 | bytes 8000000 | tf_op jit(solution)/shard_map/uvqk_grads/pallas_call | solution.py:170
  12.9 2.6 %own_weight_grads.1 = (bf16[512,1024]{1,0:T(8,128)(2,1)S(1)}, f32[4,256,256]{2,1,0:T(8,128)S(1)}, f32[4,256,256]{2,1,0:T(8,128)S(1)}, f32[4,256,256]{2,1,0:T(8,1...) custom-call(bf16[512,1024]{1,0:T(8,128)(2,1)S(1)} %copy-done, ...), custom_call_target="tpu_custom_call" | custom-call | flops 1400000000 | bytes 20971520 | tf_op jit(solution)/shard_map/own_weight_grads/pallas_call | solution.py:238
  15.4 0.5 pair_weight_grads.4
  15.9 1.3 %collective-permute-start.2 = (bf16[4,256,256]{2,1,0:T(8,128)(2,1)S(1)}, bf16[4,256,256]{2,1,0:T(8,128)(2,1)S(1)}, u32[]{:S(2)}, u32[]{:S(2)}) collective-permute-start(bf16[4,256,256]{2,1,0:T(8,128)(2,1)S(1)} %pair_weight_grads.4), channel_id=1, source_target_pairs={{0,16},{1,17},{2,18},{3,19},{4,20},{5,21},{6,22},{7,23},{8,24},{9,... | collective-permute-start | bytes 1572872 | tf_op jit(solution)/shard_map/ppermute | solution.py:337
  17.2 0.5 pair_weight_grads.5
  17.7 0.4 collective-permute-start.3
  18.1 0.5 pair_weight_grads.6
  18.6 2.0 %collective-permute-start.4 = (bf16[4,256,256]{2,1,0:T(8,128)(2,1)S(1)}, bf16[4,256,256]{2,1,0:T(8,128)(2,1)S(1)}, u32[]{:S(2)}, u32[]{:S(2)}) collective-permute-start(bf16[4,256,256]{2,1,0:T(8,128)(2,1)S(1)} %pair_weight_grads.6), channel_id=1, source_target_pairs={{0,24},{1,25},{2,26},{3,27},{4,28},{5,29},{6,30},{7,31},{8,16},{9,... | collective-permute-start | bytes 1572872 | tf_op jit(solution)/shard_map/ppermute | solution.py:337
  20.6 0.5 pair_weight_grads.7
  21.0 3.4 %row_grads.1 = bf16[512,1024]{1,0:T(8,128)(2,1)} custom-call(bf16[512,1024]{1,0:T(8,128)(2,1)S(1)} %get-tuple-element.32.keep_ref, bf16[512,1024]{1,0:T(8,128)(2,1)S(1)} %get-tuple-element.28.send_ref, bf16[1024,2048]{1,0:T(8,128)(2,1)S(1)} %copy-done.1), custom_call_target="tpu_custom_call" | custom-call | flops 2147483648 | bytes 7340032 | tf_op jit(solution)/shard_map/row_grads/pallas_call | solution.py:293
  24.4 1.5 %collective-permute-done.2 = bf16[4,256,256]{2,1,0:T(8,128)(2,1)S(1)} collective-permute-done((bf16[4,256,256]{2,1,0:T(8,128)(2,1)S(1)}, bf16[4,256,256]{2,1,0:T(8,128)(2,1)S(1)}, u32[]{:S(2)}, u32[]{:S(2)}) %collective-permute-start.2) | collective-permute-done | bytes 524320 | tf_op jit(solution)/shard_map/ppermute | solution.py:337
  25.9 4.2 %collective-permute-done.3 = bf16[4,256,256]{2,1,0:T(8,128)(2,1)S(1)} collective-permute-done((bf16[4,256,256]{2,1,0:T(8,128)(2,1)S(1)}, bf16[4,256,256]{2,1,0:T(8,128)(2,1)S(1)}, u32[]{:S(2)}, u32[]{:S(2)}) %collective-permute-start.3) | collective-permute-done | bytes 524320 | tf_op jit(solution)/shard_map/ppermute | solution.py:337
  30.1 1.4 %collective-permute-done.4 = bf16[4,256,256]{2,1,0:T(8,128)(2,1)S(1)} collective-permute-done((bf16[4,256,256]{2,1,0:T(8,128)(2,1)S(1)}, bf16[4,256,256]{2,1,0:T(8,128)(2,1)S(1)}, u32[]{:S(2)}, u32[]{:S(2)}) %collective-permute-start.4) | collective-permute-done | bytes 524320 | tf_op jit(solution)/shard_map/ppermute | solution.py:337
  31.7 1.5 %collective-permute-start.5 = (bf16[256,256]{1,0:T(8,128)(2,1)S(1)}, bf16[256,256]{1,0:T(8,128)(2,1)S(1)}, u32[]{:S(2)}, u32[]{:S(2)}) collective-permute-start(bf16[256,256]{1,0:T(8,128)(2,1)S(1)} %get-tuple-element.40), channel_id=1, source_target_pairs={{0,128},{1,129},{2,130},{3,131},{4,132},{5,133},{6,134},{7,135},{8... | collective-permute-start | bytes 393224 | tf_op jit(solution)/shard_map/ppermute | solution.py:337
  33.1 0.9 %collective-permute-start.7 = (bf16[256,256]{1,0:T(8,128)(2,1)S(1)}, bf16[256,256]{1,0:T(8,128)(2,1)S(1)}, u32[]{:S(2)}, u32[]{:S(2)}) collective-permute-start(bf16[256,256]{1,0:T(8,128)(2,1)S(1)} %get-tuple-element.41), channel_id=1, source_target_pairs={{0,192},{1,193},{2,194},{3,195},{4,196},{5,197},{6,198},{7,199},{8... | collective-permute-start | bytes 393224 | tf_op jit(solution)/shard_map/ppermute | solution.py:337
  34.0 0.4 collective-permute-start.6
  34.4 2.7 %collective-permute-done.5 = bf16[256,256]{1,0:T(8,128)(2,1)S(1)} collective-permute-done((bf16[256,256]{1,0:T(8,128)(2,1)S(1)}, bf16[256,256]{1,0:T(8,128)(2,1)S(1)}, u32[]{:S(2)}, u32[]{:S(2)}) %collective-permute-start.5) | collective-permute-done | bytes 131104 | tf_op jit(solution)/shard_map/ppermute | solution.py:337
  37.1 1.7 %collective-permute-done.7 = bf16[256,256]{1,0:T(8,128)(2,1)S(1)} collective-permute-done((bf16[256,256]{1,0:T(8,128)(2,1)S(1)}, bf16[256,256]{1,0:T(8,128)(2,1)S(1)}, u32[]{:S(2)}, u32[]{:S(2)}) %collective-permute-start.7) | collective-permute-done | bytes 131104 | tf_op jit(solution)/shard_map/ppermute | solution.py:337
  38.9 3.8 %collective-permute-start.9 = (bf16[2,32,256]{2,1,0:T(8,128)(2,1)S(1)}, bf16[2,32,256]{2,1,0:T(8,128)(2,1)S(1)}, u32[]{:S(2)}, u32[]{:S(2)}) collective-permute-start(bf16[2,32,256]{2,1,0:T(8,128)(2,1)S(1)} %pad_maximum_fusion.1), channel_id=1, source_target_pairs={{0,3},{1,2},{2,1},{3,0},{4,7},{5,6},{6,5},{7,4},{8,11},{9,10},{10,... | collective-permute-start | bytes 98312 | tf_op jit(solution)/shard_map/ppermute | solution.py:337
  42.8 0.4 collective-permute-start.8
  43.2 0.9 %collective-permute-done.9 = bf16[2,32,256]{2,1,0:T(8,128)(2,1)S(1)} collective-permute-done((bf16[2,32,256]{2,1,0:T(8,128)(2,1)S(1)}, bf16[2,32,256]{2,1,0:T(8,128)(2,1)S(1)}, u32[]{:S(2)}, u32[]{:S(2)}) %collective-permute-start.9) | collective-permute-done | bytes 32800 | tf_op jit(solution)/shard_map/ppermute | solution.py:337
  44.1 2.7 %collective-permute-done.10 = bf16[2,32,256]{2,1,0:T(8,128)(2,1)S(1)} collective-permute-done((bf16[2,32,256]{2,1,0:T(8,128)(2,1)S(1)}, bf16[2,32,256]{2,1,0:T(8,128)(2,1)S(1)}, u32[]{:S(2)}, u32[]{:S(2)}) %collective-permute-start.10) | collective-permute-done | bytes 32800 | tf_op jit(solution)/shard_map/ppermute | solution.py:337
  46.8 2.6 %collective-permute-start.11 = (f32[32,256]{1,0:T(8,128)S(1)}, f32[32,256]{1,0:T(8,128)S(1)}, u32[]{:S(2)}, u32[]{:S(2)}) collective-permute-start(f32[32,256]{1,0:T(8,128)S(1)} %slice_bitcast_fusion), channel_id=1, source_target_pairs={{0,7},{1,6},{2,5},{3,4},{4,3},{5,2},{6,1},{7,0},{8,15},{9,14},{10,... | collective-permute-start | bytes 98312 | tf_op jit(solution)/shard_map/ppermute | solution.py:337
  49.4 1.4 %collective-permute-done.11 = f32[32,256]{1,0:T(8,128)S(1)} collective-permute-done((f32[32,256]{1,0:T(8,128)S(1)}, f32[32,256]{1,0:T(8,128)S(1)}, u32[]{:S(2)}, u32[]{:S(2)}) %collective-permute-start.11) | collective-permute-done | bytes 32800 | tf_op jit(solution)/shard_map/ppermute | solution.py:337
  50.8 4.9 %collective-permute-start.12 = (bf16[32,256]{1,0:T(8,128)(2,1)S(1)}, bf16[32,256]{1,0:T(8,128)(2,1)S(1)}, u32[]{:S(2)}, u32[]{:S(2)}) collective-permute-start(bf16[32,256]{1,0:T(8,128)(2,1)S(1)} %fusion.8), channel_id=1, source_target_pairs={{0,32},{1,33},{2,34},{3,35},{4,36},{5,37},{6,38},{7,39},{8,40},{9,... | collective-permute-start | bytes 49160 | tf_op jit(solution)/shard_map/ppermute | solution.py:337
  55.7 0.8 %collective-permute-done.12 = bf16[32,256]{1,0:T(8,128)(2,1)S(1)} collective-permute-done((bf16[32,256]{1,0:T(8,128)(2,1)S(1)}, bf16[32,256]{1,0:T(8,128)(2,1)S(1)}, u32[]{:S(2)}, u32[]{:S(2)}) %collective-permute-start.12) | collective-permute-done | bytes 16416 | tf_op jit(solution)/shard_map/ppermute | solution.py:337
  56.6 2.0 %collective-permute-start.15 = (bf16[2,32,256]{2,1,0:T(8,128)(2,1)S(1)}, bf16[2,32,256]{2,1,0:T(8,128)(2,1)S(1)}, u32[]{:S(2)}, u32[]{:S(2)}) collective-permute-start(bf16[2,32,256]{2,1,0:T(8,128)(2,1)S(1)} %pad_maximum_fusion.3.p0), channel_id=1, source_target_pairs={{0,192},{1,193},{2,194},{3,195},{4,196},{5,197},{6,198},{7,199},{8... | collective-permute-start | bytes 98312 | tf_op jit(solution)/shard_map/ppermute | solution.py:337
  58.5 1.3 %collective-permute-start.13 = (bf16[2,32,256]{2,1,0:T(8,128)(2,1)S(1)}, bf16[2,32,256]{2,1,0:T(8,128)(2,1)S(1)}, u32[]{:S(2)}, u32[]{:S(2)}) collective-permute-start(bf16[2,32,256]{2,1,0:T(8,128)(2,1)S(1)} %pad_maximum_fusion.3.p0), channel_id=1, source_target_pairs={{0,64},{1,65},{2,66},{3,67},{4,68},{5,69},{6,70},{7,71},{8,72},{9,... | collective-permute-start | bytes 98312 | tf_op jit(solution)/shard_map/ppermute | solution.py:337
  59.8 0.7 %collective-permute-done.15.p3 = bf16[2,32,256]{2,1,0:T(8,128)(2,1)S(1)} collective-permute-done((bf16[2,32,256]{2,1,0:T(8,128)(2,1)S(1)}, bf16[2,32,256]{2,1,0:T(8,128)(2,1)S(1)}, u32[]{:S(2)}, u32[]{:S(2)}) %collective-permute-start.15) | collective-permute-done | bytes 32800 | tf_op jit(solution)/shard_map/ppermute | solution.py:337
  60.5 2.3 %collective-permute-done.14.p2 = bf16[2,32,256]{2,1,0:T(8,128)(2,1)S(1)} collective-permute-done((bf16[2,32,256]{2,1,0:T(8,128)(2,1)S(1)}, bf16[2,32,256]{2,1,0:T(8,128)(2,1)S(1)}, u32[]{:S(2)}, u32[]{:S(2)}) %collective-permute-start.14) | collective-permute-done | bytes 32800 | tf_op jit(solution)/shard_map/ppermute | solution.py:337
  62.8 0.7 %place_columns.1 = f32[32,2048]{1,0:T(8,128)} custom-call(bf16[2,32,256]{2,1,0:T(8,128)(2,1)S(1)} %pad_maximum_fusion.3.p0, bf16[2,32,256]{2,1,0:T(8,128)(2,1)S(1)} %collective-permute-done.13.p1, bf16[2,32,256]{2,1,0:T(8,128)(2,1)S(1)} %collective-permute-done.14.p2, bf16[2,32,256]{2,1,0:T(8,128)(2,1)S(1)} %collective-permute-done.15.p3), custom_call_target="tpu_custom_call" | custom-call | tf_op jit(solution)/shard_map/place_columns/pallas_call | solution.py:315
  (23 shorter events, 0.6 us)
Async XLA Ops:
  0.6 12.2 %copy-start = (bf16[512,1024]{1,0:T(8,128)(2,1)S(1)}, bf16[512,1024]{1,0:T(8,128)(2,1)}, u32[]{:S(2)}) copy-start(bf16[512,1024]{1,0:T(8,128)(2,1)} %x_ref.1) | copy-start | bytes 3145732
  0.6 12.2 %collective-permute-start = (bf16[512,1024]{1,0:T(8,128)(2,1)}, bf16[512,1024]{1,0:T(8,128)(2,1)S(1)}, u32[]{:S(2)}, u32[]{:S(2)}) collective-permute-start(bf16[512,1024]{1,0:T(8,128)(2,1)} %x_ref.1), channel_id=1, source_target_pairs={{0,32},{1,33},{2,34},{3,35},{4,36},{5,37},{6,38},{7,39},{8,40},{9,... | collective-permute-start | bytes 3145736 | tf_op jit(solution)/shard_map/ppermute | solution.py:337
  12.7 2.8 %collective-permute-start.1 = (bf16[512,1024]{1,0:T(8,128)(2,1)S(1)}, bf16[512,1024]{1,0:T(8,128)(2,1)S(1)}, u32[]{:S(2)}, u32[]{:S(2)}) collective-permute-start(bf16[512,1024]{1,0:T(8,128)(2,1)S(1)} %get-tuple-element.28.send_ref), channel_id=1, source_target_pairs={{0,32},{1,33},{2,34},{3,35},{4,36},{5,37},{6,38},{7,39},{8,40},{9,... | collective-permute-start | bytes 3145736 | tf_op jit(solution)/shard_map/ppermute | solution.py:337
  15.9 10.0 %collective-permute-start.2 = (bf16[4,256,256]{2,1,0:T(8,128)(2,1)S(1)}, bf16[4,256,256]{2,1,0:T(8,128)(2,1)S(1)}, u32[]{:S(2)}, u32[]{:S(2)}) collective-permute-start(bf16[4,256,256]{2,1,0:T(8,128)(2,1)S(1)} %pair_weight_grads.4), channel_id=1, source_target_pairs={{0,16},{1,17},{2,18},{3,19},{4,20},{5,21},{6,22},{7,23},{8,24},{9,... | collective-permute-start | bytes 1572872 | tf_op jit(solution)/shard_map/ppermute | solution.py:337
  17.7 3.4 %copy-start.1 = (bf16[1024,2048]{1,0:T(8,128)(2,1)S(1)}, bf16[1024,2048]{1,0:T(8,128)(2,1)}, u32[]{:S(2)}) copy-start(bf16[1024,2048]{1,0:T(8,128)(2,1)} %w_ref.1) | copy-start | bytes 12582916
  17.7 12.4 %collective-permute-start.3 = (bf16[4,256,256]{2,1,0:T(8,128)(2,1)S(1)}, bf16[4,256,256]{2,1,0:T(8,128)(2,1)S(1)}, u32[]{:S(2)}, u32[]{:S(2)}) collective-permute-start(bf16[4,256,256]{2,1,0:T(8,128)(2,1)S(1)} %pair_weight_grads.5), channel_id=1, source_target_pairs={{0,8},{1,9},{2,10},{3,11},{4,12},{5,13},{6,14},{7,15},{8,0},{9,1},... | collective-permute-start | bytes 1572872 | tf_op jit(solution)/shard_map/ppermute | solution.py:337
  18.6 12.9 %collective-permute-start.4 = (bf16[4,256,256]{2,1,0:T(8,128)(2,1)S(1)}, bf16[4,256,256]{2,1,0:T(8,128)(2,1)S(1)}, u32[]{:S(2)}, u32[]{:S(2)}) collective-permute-start(bf16[4,256,256]{2,1,0:T(8,128)(2,1)S(1)} %pair_weight_grads.6), channel_id=1, source_target_pairs={{0,24},{1,25},{2,26},{3,27},{4,28},{5,29},{6,30},{7,31},{8,16},{9,... | collective-permute-start | bytes 1572872 | tf_op jit(solution)/shard_map/ppermute | solution.py:337
  31.7 5.4 %collective-permute-start.5 = (bf16[256,256]{1,0:T(8,128)(2,1)S(1)}, bf16[256,256]{1,0:T(8,128)(2,1)S(1)}, u32[]{:S(2)}, u32[]{:S(2)}) collective-permute-start(bf16[256,256]{1,0:T(8,128)(2,1)S(1)} %get-tuple-element.40), channel_id=1, source_target_pairs={{0,128},{1,129},{2,130},{3,131},{4,132},{5,133},{6,134},{7,135},{8... | collective-permute-start | bytes 393224 | tf_op jit(solution)/shard_map/ppermute | solution.py:337
  33.1 5.6 %collective-permute-start.7 = (bf16[256,256]{1,0:T(8,128)(2,1)S(1)}, bf16[256,256]{1,0:T(8,128)(2,1)S(1)}, u32[]{:S(2)}, u32[]{:S(2)}) collective-permute-start(bf16[256,256]{1,0:T(8,128)(2,1)S(1)} %get-tuple-element.41), channel_id=1, source_target_pairs={{0,192},{1,193},{2,194},{3,195},{4,196},{5,197},{6,198},{7,199},{8... | collective-permute-start | bytes 393224 | tf_op jit(solution)/shard_map/ppermute | solution.py:337
  34.0 4.8 %collective-permute-start.6 = (bf16[256,256]{1,0:T(8,128)(2,1)S(1)}, bf16[256,256]{1,0:T(8,128)(2,1)S(1)}, u32[]{:S(2)}, u32[]{:S(2)}) collective-permute-start(bf16[256,256]{1,0:T(8,128)(2,1)S(1)} %get-tuple-element.42), channel_id=1, source_target_pairs={{0,64},{1,65},{2,66},{3,67},{4,68},{5,69},{6,70},{7,71},{8,72},{9,... | collective-permute-start | bytes 393224 | tf_op jit(solution)/shard_map/ppermute | solution.py:337
  38.9 5.1 %collective-permute-start.9 = (bf16[2,32,256]{2,1,0:T(8,128)(2,1)S(1)}, bf16[2,32,256]{2,1,0:T(8,128)(2,1)S(1)}, u32[]{:S(2)}, u32[]{:S(2)}) collective-permute-start(bf16[2,32,256]{2,1,0:T(8,128)(2,1)S(1)} %pad_maximum_fusion.1), channel_id=1, source_target_pairs={{0,3},{1,2},{2,1},{3,0},{4,7},{5,6},{6,5},{7,4},{8,11},{9,10},{10,... | collective-permute-start | bytes 98312 | tf_op jit(solution)/shard_map/ppermute | solution.py:337
  42.8 4.0 %collective-permute-start.10 = (bf16[2,32,256]{2,1,0:T(8,128)(2,1)S(1)}, bf16[2,32,256]{2,1,0:T(8,128)(2,1)S(1)}, u32[]{:S(2)}, u32[]{:S(2)}) collective-permute-start(bf16[2,32,256]{2,1,0:T(8,128)(2,1)S(1)} %pad_maximum_fusion.2), channel_id=1, source_target_pairs={{0,2},{1,3},{2,0},{3,1},{4,6},{5,7},{6,4},{7,5},{8,10},{9,11},{10,... | collective-permute-start | bytes 98312 | tf_op jit(solution)/shard_map/ppermute | solution.py:337
  42.8 3.9 %collective-permute-start.8 = (bf16[2,32,256]{2,1,0:T(8,128)(2,1)S(1)}, bf16[2,32,256]{2,1,0:T(8,128)(2,1)S(1)}, u32[]{:S(2)}, u32[]{:S(2)}) collective-permute-start(bf16[2,32,256]{2,1,0:T(8,128)(2,1)S(1)} %pad_maximum_fusion), channel_id=1, source_target_pairs={{0,1},{1,0},{2,3},{3,2},{4,5},{5,4},{6,7},{7,6},{8,9},{9,8},{10,11... | collective-permute-start | bytes 98312 | tf_op jit(solution)/shard_map/ppermute | solution.py:337
  46.8 4.1 %collective-permute-start.11 = (f32[32,256]{1,0:T(8,128)S(1)}, f32[32,256]{1,0:T(8,128)S(1)}, u32[]{:S(2)}, u32[]{:S(2)}) collective-permute-start(f32[32,256]{1,0:T(8,128)S(1)} %slice_bitcast_fusion), channel_id=1, source_target_pairs={{0,7},{1,6},{2,5},{3,4},{4,3},{5,2},{6,1},{7,0},{8,15},{9,14},{10,... | collective-permute-start | bytes 98312 | tf_op jit(solution)/shard_map/ppermute | solution.py:337
  50.8 5.7 %collective-permute-start.12 = (bf16[32,256]{1,0:T(8,128)(2,1)S(1)}, bf16[32,256]{1,0:T(8,128)(2,1)S(1)}, u32[]{:S(2)}, u32[]{:S(2)}) collective-permute-start(bf16[32,256]{1,0:T(8,128)(2,1)S(1)} %fusion.8), channel_id=1, source_target_pairs={{0,32},{1,33},{2,34},{3,35},{4,36},{5,37},{6,38},{7,39},{8,40},{9,... | collective-permute-start | bytes 49160 | tf_op jit(solution)/shard_map/ppermute | solution.py:337
  56.6 4.0 %collective-permute-start.15 = (bf16[2,32,256]{2,1,0:T(8,128)(2,1)S(1)}, bf16[2,32,256]{2,1,0:T(8,128)(2,1)S(1)}, u32[]{:S(2)}, u32[]{:S(2)}) collective-permute-start(bf16[2,32,256]{2,1,0:T(8,128)(2,1)S(1)} %pad_maximum_fusion.3.p0), channel_id=1, source_target_pairs={{0,192},{1,193},{2,194},{3,195},{4,196},{5,197},{6,198},{7,199},{8... | collective-permute-start | bytes 98312 | tf_op jit(solution)/shard_map/ppermute | solution.py:337
  58.5 4.3 %collective-permute-start.14 = (bf16[2,32,256]{2,1,0:T(8,128)(2,1)S(1)}, bf16[2,32,256]{2,1,0:T(8,128)(2,1)S(1)}, u32[]{:S(2)}, u32[]{:S(2)}) collective-permute-start(bf16[2,32,256]{2,1,0:T(8,128)(2,1)S(1)} %pad_maximum_fusion.3.p0), channel_id=1, source_target_pairs={{0,128},{1,129},{2,130},{3,131},{4,132},{5,133},{6,134},{7,135},{8... | collective-permute-start | bytes 98312 | tf_op jit(solution)/shard_map/ppermute | solution.py:337
  58.5 4.3 %collective-permute-start.13 = (bf16[2,32,256]{2,1,0:T(8,128)(2,1)S(1)}, bf16[2,32,256]{2,1,0:T(8,128)(2,1)S(1)}, u32[]{:S(2)}, u32[]{:S(2)}) collective-permute-start(bf16[2,32,256]{2,1,0:T(8,128)(2,1)S(1)} %pad_maximum_fusion.3.p0), channel_id=1, source_target_pairs={{0,64},{1,65},{2,66},{3,67},{4,68},{5,69},{6,70},{7,71},{8,72},{9,... | collective-permute-start | bytes 98312 | tf_op jit(solution)/shard_map/ppermute | solution.py:337

commit v6 on v5

--- a/solution.py
+++ b/solution.py
@@ -380,7 +380,7 @@
     ends = jnp.stack([block[0], block[7]])
     moved = [permute(jnp.stack([block[m], block[7 - m]]).astype(jnp.bfloat16), along_z(m)) for m in (1, 3, 2)]
     ends = ends + f32(moved[0]) + f32(moved[1]) + f32(moved[2])
-    block = ends[0] + permute(ends[1], along_z(7))
+    block = ends[0] + f32(permute(ends[1].astype(jnp.bfloat16), along_z(7)))
 
     block = block.astype(jnp.bfloat16)
     both = jnp.stack([block, permute(block, other_core)])

time: 64.2 us -> 64 us (level)
  no operation moved by 1% of the time
where the time goes in v6:
time: 64 us; the launch traced here: 63.2 us
  starting transfers between devices  24.9 us (39%)
  waiting for transfers between devices  19.9 us (31%)
  Pallas kernels  17.2 us (27%)
  between operations  0.76 us (1%)
    ppermute x16, starting transfers between devices, permute(): return lax.ppermute(value, AXES, pairs(move))  24.9 us
    ppermute x16, waiting for transfers between devices, permute(): return lax.ppermute(value, AXES, pairs(move))  19.9 us
    pallas_call x1, Pallas kernels, grads(): pl.pallas_call(grads_kernel, out_shape=[pltpu.VMEM((rows, wide // 2), jnp...  8.69 us
    pallas_call x1, Pallas kernels, row_grads(): pl.pallas_call(rows_kernel, out_shape=jax.ShapeDtypeStruct((keep.shape[0]...  3.36 us
    pallas_call x1, Pallas kernels, own_part(): pl.pallas_call(own_kernel, out_shape=[pltpu.VMEM((rows, d), jnp.bfloat16)...  2.57 us
    pallas_call x4, Pallas kernels, pair_part(): pl.pallas_call(functools.partial(pair_kernel, ks), out_shape=[pltpu.VMEM(...  1.85 us
  transfers between devices with their start and end apart: 16, of which 11 were waited for; matrix products, arithmetic and copies ran while one was open for 0% of the time, Pallas kernels for 25%

profile of v6, /device:TPU:1, one launch (start us, length us, event | category | flops | bytes accessed | tf_op | source)
XLA Modules:
  0.0 63.2 jit_solution(13959076745509143691)
XLA Ops:
  0.6 3.3 %collective-permute-start = (bf16[512,1024]{1,0:T(8,128)(2,1)}, bf16[512,1024]{1,0:T(8,128)(2,1)S(1)}, u32[]{:S(2)}, u32[]{:S(2)}) collective-permute-start(bf16[512,1024]{1,0:T(8,128)(2,1)} %x_ref.1), channel_id=1, source_target_pairs={{0,32},{1,33},{2,34},{3,35},{4,36},{5,37},{6,38},{7,39},{8,40},{9,... | collective-permute-start | bytes 3145736 | tf_op jit(solution)/shard_map/ppermute | solution.py:337
  4.0 8.7 %uvqk_grads.1 = (bf16[512,1024]{1,0:T(8,128)(2,1)S(1)}, bf16[512,256]{1,0:T(8,128)(2,1)S(1)}, f32[512,2048]{1,0:T(8,128)S(1)}, bf16[512,2048]{1,0:T(8,128)(2,1)S...) custom-call(s32[2]{0:T(128)} %len_hbm.1, ...), custom_call_target="tpu_custom_call" | custom-call | flops 4000000000 | bytes 8000000 | tf_op jit(solution)/shard_map/uvqk_grads/pallas_call | solution.py:170
  12.9 2.6 %own_weight_grads.1 = (bf16[512,1024]{1,0:T(8,128)(2,1)S(1)}, f32[4,256,256]{2,1,0:T(8,128)S(1)}, f32[4,256,256]{2,1,0:T(8,128)S(1)}, f32[4,256,256]{2,1,0:T(8,1...) custom-call(bf16[512,1024]{1,0:T(8,128)(2,1)S(1)} %copy-done, ...), custom_call_target="tpu_custom_call" | custom-call | flops 1400000000 | bytes 20971520 | tf_op jit(solution)/shard_map/own_weight_grads/pallas_call | solution.py:238
  15.4 0.5 pair_weight_grads.4
  15.9 1.3 %collective-permute-start.2 = (bf16[4,256,256]{2,1,0:T(8,128)(2,1)S(1)}, bf16[4,256,256]{2,1,0:T(8,128)(2,1)S(1)}, u32[]{:S(2)}, u32[]{:S(2)}) collective-permute-start(bf16[4,256,256]{2,1,0:T(8,128)(2,1)S(1)} %pair_weight_grads.4), channel_id=1, source_target_pairs={{0,16},{1,17},{2,18},{3,19},{4,20},{5,21},{6,22},{7,23},{8,24},{9,... | collective-permute-start | bytes 1572872 | tf_op jit(solution)/shard_map/ppermute | solution.py:337
  17.2 0.5 pair_weight_grads.5
  17.7 0.4 collective-permute-start.3
  18.1 0.5 pair_weight_grads.6
  18.6 2.0 %collective-permute-start.4 = (bf16[4,256,256]{2,1,0:T(8,128)(2,1)S(1)}, bf16[4,256,256]{2,1,0:T(8,128)(2,1)S(1)}, u32[]{:S(2)}, u32[]{:S(2)}) collective-permute-start(bf16[4,256,256]{2,1,0:T(8,128)(2,1)S(1)} %pair_weight_grads.6), channel_id=1, source_target_pairs={{0,24},{1,25},{2,26},{3,27},{4,28},{5,29},{6,30},{7,31},{8,16},{9,... | collective-permute-start | bytes 1572872 | tf_op jit(solution)/shard_map/ppermute | solution.py:337
  20.6 0.5 pair_weight_grads.7
  21.0 3.4 %row_grads.1 = bf16[512,1024]{1,0:T(8,128)(2,1)} custom-call(bf16[512,1024]{1,0:T(8,128)(2,1)S(1)} %get-tuple-element.32.keep_ref, bf16[512,1024]{1,0:T(8,128)(2,1)S(1)} %get-tuple-element.28.send_ref, bf16[1024,2048]{1,0:T(8,128)(2,1)S(1)} %copy-done.1), custom_call_target="tpu_custom_call" | custom-call | flops 2147483648 | bytes 7340032 | tf_op jit(solution)/shard_map/row_grads/pallas_call | solution.py:293
  24.4 1.5 %collective-permute-done.2 = bf16[4,256,256]{2,1,0:T(8,128)(2,1)S(1)} collective-permute-done((bf16[4,256,256]{2,1,0:T(8,128)(2,1)S(1)}, bf16[4,256,256]{2,1,0:T(8,128)(2,1)S(1)}, u32[]{:S(2)}, u32[]{:S(2)}) %collective-permute-start.2) | collective-permute-done | bytes 524320 | tf_op jit(solution)/shard_map/ppermute | solution.py:337
  25.9 4.2 %collective-permute-done.3 = bf16[4,256,256]{2,1,0:T(8,128)(2,1)S(1)} collective-permute-done((bf16[4,256,256]{2,1,0:T(8,128)(2,1)S(1)}, bf16[4,256,256]{2,1,0:T(8,128)(2,1)S(1)}, u32[]{:S(2)}, u32[]{:S(2)}) %collective-permute-start.3) | collective-permute-done | bytes 524320 | tf_op jit(solution)/shard_map/ppermute | solution.py:337
  30.1 1.4 %collective-permute-done.4 = bf16[4,256,256]{2,1,0:T(8,128)(2,1)S(1)} collective-permute-done((bf16[4,256,256]{2,1,0:T(8,128)(2,1)S(1)}, bf16[4,256,256]{2,1,0:T(8,128)(2,1)S(1)}, u32[]{:S(2)}, u32[]{:S(2)}) %collective-permute-start.4) | collective-permute-done | bytes 524320 | tf_op jit(solution)/shard_map/ppermute | solution.py:337
  31.7 1.5 %collective-permute-start.5 = (bf16[256,256]{1,0:T(8,128)(2,1)S(1)}, bf16[256,256]{1,0:T(8,128)(2,1)S(1)}, u32[]{:S(2)}, u32[]{:S(2)}) collective-permute-start(bf16[256,256]{1,0:T(8,128)(2,1)S(1)} %get-tuple-element.40), channel_id=1, source_target_pairs={{0,128},{1,129},{2,130},{3,131},{4,132},{5,133},{6,134},{7,135},{8... | collective-permute-start | bytes 393224 | tf_op jit(solution)/shard_map/ppermute | solution.py:337
  33.1 0.9 %collective-permute-start.7 = (bf16[256,256]{1,0:T(8,128)(2,1)S(1)}, bf16[256,256]{1,0:T(8,128)(2,1)S(1)}, u32[]{:S(2)}, u32[]{:S(2)}) collective-permute-start(bf16[256,256]{1,0:T(8,128)(2,1)S(1)} %get-tuple-element.41), channel_id=1, source_target_pairs={{0,192},{1,193},{2,194},{3,195},{4,196},{5,197},{6,198},{7,199},{8... | collective-permute-start | bytes 393224 | tf_op jit(solution)/shard_map/ppermute | solution.py:337
  34.0 0.4 collective-permute-start.6
  34.4 2.7 %collective-permute-done.5 = bf16[256,256]{1,0:T(8,128)(2,1)S(1)} collective-permute-done((bf16[256,256]{1,0:T(8,128)(2,1)S(1)}, bf16[256,256]{1,0:T(8,128)(2,1)S(1)}, u32[]{:S(2)}, u32[]{:S(2)}) %collective-permute-start.5) | collective-permute-done | bytes 131104 | tf_op jit(solution)/shard_map/ppermute | solution.py:337
  37.1 1.7 %collective-permute-done.7 = bf16[256,256]{1,0:T(8,128)(2,1)S(1)} collective-permute-done((bf16[256,256]{1,0:T(8,128)(2,1)S(1)}, bf16[256,256]{1,0:T(8,128)(2,1)S(1)}, u32[]{:S(2)}, u32[]{:S(2)}) %collective-permute-start.7) | collective-permute-done | bytes 131104 | tf_op jit(solution)/shard_map/ppermute | solution.py:337
  38.9 3.8 %collective-permute-start.9 = (bf16[2,32,256]{2,1,0:T(8,128)(2,1)S(1)}, bf16[2,32,256]{2,1,0:T(8,128)(2,1)S(1)}, u32[]{:S(2)}, u32[]{:S(2)}) collective-permute-start(bf16[2,32,256]{2,1,0:T(8,128)(2,1)S(1)} %pad_maximum_fusion.1), channel_id=1, source_target_pairs={{0,3},{1,2},{2,1},{3,0},{4,7},{5,6},{6,5},{7,4},{8,11},{9,10},{10,... | collective-permute-start | bytes 98312 | tf_op jit(solution)/shard_map/ppermute | solution.py:337
  42.8 0.4 collective-permute-start.8
  43.2 0.9 %collective-permute-done.9 = bf16[2,32,256]{2,1,0:T(8,128)(2,1)S(1)} collective-permute-done((bf16[2,32,256]{2,1,0:T(8,128)(2,1)S(1)}, bf16[2,32,256]{2,1,0:T(8,128)(2,1)S(1)}, u32[]{:S(2)}, u32[]{:S(2)}) %collective-permute-start.9) | collective-permute-done | bytes 32800 | tf_op jit(solution)/shard_map/ppermute | solution.py:337
  44.1 2.7 %collective-permute-done.10 = bf16[2,32,256]{2,1,0:T(8,128)(2,1)S(1)} collective-permute-done((bf16[2,32,256]{2,1,0:T(8,128)(2,1)S(1)}, bf16[2,32,256]{2,1,0:T(8,128)(2,1)S(1)}, u32[]{:S(2)}, u32[]{:S(2)}) %collective-permute-start.10) | collective-permute-done | bytes 32800 | tf_op jit(solution)/shard_map/ppermute | solution.py:337
  46.8 2.6 %collective-permute-start.11 = (bf16[32,256]{1,0:T(8,128)(2,1)S(1)}, bf16[32,256]{1,0:T(8,128)(2,1)S(1)}, u32[]{:S(2)}, u32[]{:S(2)}) collective-permute-start(bf16[32,256]{1,0:T(8,128)(2,1)S(1)} %fusion.9), channel_id=1, source_target_pairs={{0,7},{1,6},{2,5},{3,4},{4,3},{5,2},{6,1},{7,0},{8,15},{9,14},{10,... | collective-permute-start | bytes 49160 | tf_op jit(solution)/shard_map/ppermute | solution.py:337
  49.4 1.2 %collective-permute-done.11 = bf16[32,256]{1,0:T(8,128)(2,1)S(1)} collective-permute-done((bf16[32,256]{1,0:T(8,128)(2,1)S(1)}, bf16[32,256]{1,0:T(8,128)(2,1)S(1)}, u32[]{:S(2)}, u32[]{:S(2)}) %collective-permute-start.11) | collective-permute-done | bytes 16416 | tf_op jit(solution)/shard_map/ppermute | solution.py:337
  50.6 4.9 %collective-permute-start.12 = (bf16[32,256]{1,0:T(8,128)(2,1)S(1)}, bf16[32,256]{1,0:T(8,128)(2,1)S(1)}, u32[]{:S(2)}, u32[]{:S(2)}) collective-permute-start(bf16[32,256]{1,0:T(8,128)(2,1)S(1)} %fusion.8), channel_id=1, source_target_pairs={{0,32},{1,33},{2,34},{3,35},{4,36},{5,37},{6,38},{7,39},{8,40},{9,... | collective-permute-start | bytes 49160 | tf_op jit(solution)/shard_map/ppermute | solution.py:337
  55.5 0.8 %collective-permute-done.12 = bf16[32,256]{1,0:T(8,128)(2,1)S(1)} collective-permute-done((bf16[32,256]{1,0:T(8,128)(2,1)S(1)}, bf16[32,256]{1,0:T(8,128)(2,1)S(1)}, u32[]{:S(2)}, u32[]{:S(2)}) %collective-permute-start.12) | collective-permute-done | bytes 16416 | tf_op jit(solution)/shard_map/ppermute | solution.py:337
  56.4 1.9 %collective-permute-start.15 = (bf16[2,32,256]{2,1,0:T(8,128)(2,1)S(1)}, bf16[2,32,256]{2,1,0:T(8,128)(2,1)S(1)}, u32[]{:S(2)}, u32[]{:S(2)}) collective-permute-start(bf16[2,32,256]{2,1,0:T(8,128)(2,1)S(1)} %pad_maximum_fusion.3.p0), channel_id=1, source_target_pairs={{0,192},{1,193},{2,194},{3,195},{4,196},{5,197},{6,198},{7,199},{8... | collective-permute-start | bytes 98312 | tf_op jit(solution)/shard_map/ppermute | solution.py:337
  58.2 1.4 %collective-permute-start.13 = (bf16[2,32,256]{2,1,0:T(8,128)(2,1)S(1)}, bf16[2,32,256]{2,1,0:T(8,128)(2,1)S(1)}, u32[]{:S(2)}, u32[]{:S(2)}) collective-permute-start(bf16[2,32,256]{2,1,0:T(8,128)(2,1)S(1)} %pad_maximum_fusion.3.p0), channel_id=1, source_target_pairs={{0,64},{1,65},{2,66},{3,67},{4,68},{5,69},{6,70},{7,71},{8,72},{9,... | collective-permute-start | bytes 98312 | tf_op jit(solution)/shard_map/ppermute | solution.py:337
  59.6 0.7 %collective-permute-done.15.p3 = bf16[2,32,256]{2,1,0:T(8,128)(2,1)S(1)} collective-permute-done((bf16[2,32,256]{2,1,0:T(8,128)(2,1)S(1)}, bf16[2,32,256]{2,1,0:T(8,128)(2,1)S(1)}, u32[]{:S(2)}, u32[]{:S(2)}) %collective-permute-start.15) | collective-permute-done | bytes 32800 | tf_op jit(solution)/shard_map/ppermute | solution.py:337
  60.3 2.1 %collective-permute-done.14.p2 = bf16[2,32,256]{2,1,0:T(8,128)(2,1)S(1)} collective-permute-done((bf16[2,32,256]{2,1,0:T(8,128)(2,1)S(1)}, bf16[2,32,256]{2,1,0:T(8,128)(2,1)S(1)}, u32[]{:S(2)}, u32[]{:S(2)}) %collective-permute-start.14) | collective-permute-done | bytes 32800 | tf_op jit(solution)/shard_map/ppermute | solution.py:337
  62.5 0.7 %place_columns.1 = f32[32,2048]{1,0:T(8,128)} custom-call(bf16[2,32,256]{2,1,0:T(8,128)(2,1)S(1)} %pad_maximum_fusion.3.p0, bf16[2,32,256]{2,1,0:T(8,128)(2,1)S(1)} %collective-permute-done.13.p1, bf16[2,32,256]{2,1,0:T(8,128)(2,1)S(1)} %collective-permute-done.14.p2, bf16[2,32,256]{2,1,0:T(8,128)(2,1)S(1)} %collective-permute-done.15.p3), custom_call_target="tpu_custom_call" | custom-call | tf_op jit(solution)/shard_map/place_columns/pallas_call | solution.py:315
  (23 shorter events, 0.6 us)
Async XLA Ops:
  0.6 12.2 %copy-start = (bf16[512,1024]{1,0:T(8,128)(2,1)S(1)}, bf16[512,1024]{1,0:T(8,128)(2,1)}, u32[]{:S(2)}) copy-start(bf16[512,1024]{1,0:T(8,128)(2,1)} %x_ref.1) | copy-start | bytes 3145732
  0.6 12.2 %collective-permute-start = (bf16[512,1024]{1,0:T(8,128)(2,1)}, bf16[512,1024]{1,0:T(8,128)(2,1)S(1)}, u32[]{:S(2)}, u32[]{:S(2)}) collective-permute-start(bf16[512,1024]{1,0:T(8,128)(2,1)} %x_ref.1), channel_id=1, source_target_pairs={{0,32},{1,33},{2,34},{3,35},{4,36},{5,37},{6,38},{7,39},{8,40},{9,... | collective-permute-start | bytes 3145736 | tf_op jit(solution)/shard_map/ppermute | solution.py:337
  12.7 2.8 %collective-permute-start.1 = (bf16[512,1024]{1,0:T(8,128)(2,1)S(1)}, bf16[512,1024]{1,0:T(8,128)(2,1)S(1)}, u32[]{:S(2)}, u32[]{:S(2)}) collective-permute-start(bf16[512,1024]{1,0:T(8,128)(2,1)S(1)} %get-tuple-element.28.send_ref), channel_id=1, source_target_pairs={{0,32},{1,33},{2,34},{3,35},{4,36},{5,37},{6,38},{7,39},{8,40},{9,... | collective-permute-start | bytes 3145736 | tf_op jit(solution)/shard_map/ppermute | solution.py:337
  15.9 10.0 %collective-permute-start.2 = (bf16[4,256,256]{2,1,0:T(8,128)(2,1)S(1)}, bf16[4,256,256]{2,1,0:T(8,128)(2,1)S(1)}, u32[]{:S(2)}, u32[]{:S(2)}) collective-permute-start(bf16[4,256,256]{2,1,0:T(8,128)(2,1)S(1)} %pair_weight_grads.4), channel_id=1, source_target_pairs={{0,16},{1,17},{2,18},{3,19},{4,20},{5,21},{6,22},{7,23},{8,24},{9,... | collective-permute-start | bytes 1572872 | tf_op jit(solution)/shard_map/ppermute | solution.py:337
  17.7 3.4 %copy-start.1 = (bf16[1024,2048]{1,0:T(8,128)(2,1)S(1)}, bf16[1024,2048]{1,0:T(8,128)(2,1)}, u32[]{:S(2)}) copy-start(bf16[1024,2048]{1,0:T(8,128)(2,1)} %w_ref.1) | copy-start | bytes 12582916
  17.7 12.4 %collective-permute-start.3 = (bf16[4,256,256]{2,1,0:T(8,128)(2,1)S(1)}, bf16[4,256,256]{2,1,0:T(8,128)(2,1)S(1)}, u32[]{:S(2)}, u32[]{:S(2)}) collective-permute-start(bf16[4,256,256]{2,1,0:T(8,128)(2,1)S(1)} %pair_weight_grads.5), channel_id=1, source_target_pairs={{0,8},{1,9},{2,10},{3,11},{4,12},{5,13},{6,14},{7,15},{8,0},{9,1},... | collective-permute-start | bytes 1572872 | tf_op jit(solution)/shard_map/ppermute | solution.py:337
  18.6 12.9 %collective-permute-start.4 = (bf16[4,256,256]{2,1,0:T(8,128)(2,1)S(1)}, bf16[4,256,256]{2,1,0:T(8,128)(2,1)S(1)}, u32[]{:S(2)}, u32[]{:S(2)}) collective-permute-start(bf16[4,256,256]{2,1,0:T(8,128)(2,1)S(1)} %pair_weight_grads.6), channel_id=1, source_target_pairs={{0,24},{1,25},{2,26},{3,27},{4,28},{5,29},{6,30},{7,31},{8,16},{9,... | collective-permute-start | bytes 1572872 | tf_op jit(solution)/shard_map/ppermute | solution.py:337
  31.7 5.4 %collective-permute-start.5 = (bf16[256,256]{1,0:T(8,128)(2,1)S(1)}, bf16[256,256]{1,0:T(8,128)(2,1)S(1)}, u32[]{:S(2)}, u32[]{:S(2)}) collective-permute-start(bf16[256,256]{1,0:T(8,128)(2,1)S(1)} %get-tuple-element.40), channel_id=1, source_target_pairs={{0,128},{1,129},{2,130},{3,131},{4,132},{5,133},{6,134},{7,135},{8... | collective-permute-start | bytes 393224 | tf_op jit(solution)/shard_map/ppermute | solution.py:337
  33.1 5.6 %collective-permute-start.7 = (bf16[256,256]{1,0:T(8,128)(2,1)S(1)}, bf16[256,256]{1,0:T(8,128)(2,1)S(1)}, u32[]{:S(2)}, u32[]{:S(2)}) collective-permute-start(bf16[256,256]{1,0:T(8,128)(2,1)S(1)} %get-tuple-element.41), channel_id=1, source_target_pairs={{0,192},{1,193},{2,194},{3,195},{4,196},{5,197},{6,198},{7,199},{8... | collective-permute-start | bytes 393224 | tf_op jit(solution)/shard_map/ppermute | solution.py:337
  34.0 4.8 %collective-permute-start.6 = (bf16[256,256]{1,0:T(8,128)(2,1)S(1)}, bf16[256,256]{1,0:T(8,128)(2,1)S(1)}, u32[]{:S(2)}, u32[]{:S(2)}) collective-permute-start(bf16[256,256]{1,0:T(8,128)(2,1)S(1)} %get-tuple-element.42), channel_id=1, source_target_pairs={{0,64},{1,65},{2,66},{3,67},{4,68},{5,69},{6,70},{7,71},{8,72},{9,... | collective-permute-start | bytes 393224 | tf_op jit(solution)/shard_map/ppermute | solution.py:337
  38.9 5.1 %collective-permute-start.9 = (bf16[2,32,256]{2,1,0:T(8,128)(2,1)S(1)}, bf16[2,32,256]{2,1,0:T(8,128)(2,1)S(1)}, u32[]{:S(2)}, u32[]{:S(2)}) collective-permute-start(bf16[2,32,256]{2,1,0:T(8,128)(2,1)S(1)} %pad_maximum_fusion.1), channel_id=1, source_target_pairs={{0,3},{1,2},{2,1},{3,0},{4,7},{5,6},{6,5},{7,4},{8,11},{9,10},{10,... | collective-permute-start | bytes 98312 | tf_op jit(solution)/shard_map/ppermute | solution.py:337
  42.8 4.0 %collective-permute-start.10 = (bf16[2,32,256]{2,1,0:T(8,128)(2,1)S(1)}, bf16[2,32,256]{2,1,0:T(8,128)(2,1)S(1)}, u32[]{:S(2)}, u32[]{:S(2)}) collective-permute-start(bf16[2,32,256]{2,1,0:T(8,128)(2,1)S(1)} %pad_maximum_fusion.2), channel_id=1, source_target_pairs={{0,2},{1,3},{2,0},{3,1},{4,6},{5,7},{6,4},{7,5},{8,10},{9,11},{10,... | collective-permute-start | bytes 98312 | tf_op jit(solution)/shard_map/ppermute | solution.py:337
  42.8 3.9 %collective-permute-start.8 = (bf16[2,32,256]{2,1,0:T(8,128)(2,1)S(1)}, bf16[2,32,256]{2,1,0:T(8,128)(2,1)S(1)}, u32[]{:S(2)}, u32[]{:S(2)}) collective-permute-start(bf16[2,32,256]{2,1,0:T(8,128)(2,1)S(1)} %pad_maximum_fusion), channel_id=1, source_target_pairs={{0,1},{1,0},{2,3},{3,2},{4,5},{5,4},{6,7},{7,6},{8,9},{9,8},{10,11... | collective-permute-start | bytes 98312 | tf_op jit(solution)/shard_map/ppermute | solution.py:337
  46.8 3.9 %collective-permute-start.11 = (bf16[32,256]{1,0:T(8,128)(2,1)S(1)}, bf16[32,256]{1,0:T(8,128)(2,1)S(1)}, u32[]{:S(2)}, u32[]{:S(2)}) collective-permute-start(bf16[32,256]{1,0:T(8,128)(2,1)S(1)} %fusion.9), channel_id=1, source_target_pairs={{0,7},{1,6},{2,5},{3,4},{4,3},{5,2},{6,1},{7,0},{8,15},{9,14},{10,... | collective-permute-start | bytes 49160 | tf_op jit(solution)/shard_map/ppermute | solution.py:337
  50.6 5.7 %collective-permute-start.12 = (bf16[32,256]{1,0:T(8,128)(2,1)S(1)}, bf16[32,256]{1,0:T(8,128)(2,1)S(1)}, u32[]{:S(2)}, u32[]{:S(2)}) collective-permute-start(bf16[32,256]{1,0:T(8,128)(2,1)S(1)} %fusion.8), channel_id=1, source_target_pairs={{0,32},{1,33},{2,34},{3,35},{4,36},{5,37},{6,38},{7,39},{8,40},{9,... | collective-permute-start | bytes 49160 | tf_op jit(solution)/shard_map/ppermute | solution.py:337
  56.4 4.0 %collective-permute-start.15 = (bf16[2,32,256]{2,1,0:T(8,128)(2,1)S(1)}, bf16[2,32,256]{2,1,0:T(8,128)(2,1)S(1)}, u32[]{:S(2)}, u32[]{:S(2)}) collective-permute-start(bf16[2,32,256]{2,1,0:T(8,128)(2,1)S(1)} %pad_maximum_fusion.3.p0), channel_id=1, source_target_pairs={{0,192},{1,193},{2,194},{3,195},{4,196},{5,197},{6,198},{7,199},{8... | collective-permute-start | bytes 98312 | tf_op jit(solution)/shard_map/ppermute | solution.py:337
  58.2 4.3 %collective-permute-start.14 = (bf16[2,32,256]{2,1,0:T(8,128)(2,1)S(1)}, bf16[2,32,256]{2,1,0:T(8,128)(2,1)S(1)}, u32[]{:S(2)}, u32[]{:S(2)}) collective-permute-start(bf16[2,32,256]{2,1,0:T(8,128)(2,1)S(1)} %pad_maximum_fusion.3.p0), channel_id=1, source_target_pairs={{0,128},{1,129},{2,130},{3,131},{4,132},{5,133},{6,134},{7,135},{8... | collective-permute-start | bytes 98312 | tf_op jit(solution)/shard_map/ppermute | solution.py:337
  58.2 4.3 %collective-permute-start.13 = (bf16[2,32,256]{2,1,0:T(8,128)(2,1)S(1)}, bf16[2,32,256]{2,1,0:T(8,128)(2,1)S(1)}, u32[]{:S(2)}, u32[]{:S(2)}) collective-permute-start(bf16[2,32,256]{2,1,0:T(8,128)(2,1)S(1)} %pad_maximum_fusion.3.p0), channel_id=1, source_target_pairs={{0,64},{1,65},{2,66},{3,67},{4,68},{5,69},{6,70},{7,71},{8,72},{9,... | collective-permute-start | bytes 98312 | tf_op jit(solution)/shard_map/ppermute | solution.py:337
